TPU v7x, 256 devices: a whole 4x4x8 slice. The times are simulated.
256 devices in a mesh: rep: 4 (over y), task: 64 (over z, x, core).
Axes of the slice: x: 4, y: 4, z: 8, core: 2. Of those that a mesh axis runs over, the one named last changes fastest.
Arguments:
- amps: bfloat16 [512, 256, 256], P('task', None, 'rep'), may hold values from -6 to 6
- integrals: bfloat16 [64, 256, 256], P(None, 'rep'), may hold values from -0.125 to 0.125
- a_index: int32 [24576], P('task'), may hold values from 0 to 7
- b_index: int32 [24576], P('task'), may hold values from 0 to 63
- live: int32 [24576], P('task'), may hold values 0 or 1
- owner: int32 [3072, 1], P('task'), may hold values from 0 to 63; in each aligned block of 48 rows (0 to 47, 48 to 95, ...) at most 2 rows name the same one
- target: int32 [3072], P('task'), may hold values from 0 to 7
Outputs:
- result: float32 [512, 256, 256], P('task', 'rep')
Inputs may be any that keep to these rules, and one draw needn't show every extreme that they name: Among the 48 slots of one index of task (aligned blocks of 48 rows) no owner is named more than 2 times, a bound that some block reaches.
All inputs are finite; a program needn't handle non-finite values. No bound on the sum of `live` on one device may be relied on, other than what follows from the above.
Results may differ from a plain program's by a relative error of at most 0.013.
Values may be sent and summed in bfloat16 or wider, within the bound.
No kernel may reach another device: no remote copies, remote signals or barrier semaphores. Data moves between devices by JAX's collectives and lax.ppermute only.
A program may use at most 128 MiB of HBM per device.

v0:
```python
import jax
import jax.numpy as jnp
from jax import lax
from jax.sharding import PartitionSpec as P

OWN_DEV = 8


def slot_products(amps, integrals, a_index, b_index, live, slot_count, per_slot):
    block = 1
    for factor in (2, 4, 8):
        block = factor
    steps_total = slot_count // block
    first = a_index.reshape(steps_total, block * per_slot)
    second = b_index.reshape(steps_total, block * per_slot)
    masked = live.reshape(steps_total, block * per_slot)

    def one_block(items):
        left_ids, right_ids, alive = items
        left = amps[left_ids].reshape(block, per_slot, amps.shape[1], amps.shape[2])
        right = jnp.where(
            alive[:, None, None] > 0, integrals[right_ids], jnp.zeros((), integrals.dtype)
        )
        right = right.reshape(block, per_slot, integrals.shape[1], integrals.shape[2])
        summed = jnp.einsum("stik,stkj->sij", left, right, preferred_element_type=jnp.float32)
        return summed.astype(jnp.bfloat16)

    blocks = lax.map(one_block, (first, second, masked))
    return blocks.reshape(slot_count, amps.shape[1], integrals.shape[2])


def route_slots(values, owner, target, peer_count, capacity):
    slot_count = values.shape[0]
    destination = owner[:, 0]
    arrivals = (destination[:, None] == jnp.arange(peer_count, dtype=jnp.int32)[None, :]).astype(
        jnp.int32
    )
    running = jnp.cumsum(arrivals, axis=0) - 1
    standing = jnp.sum(running * arrivals, axis=1)
    position = destination * capacity + standing
    matches = position[None, :] == jnp.arange(peer_count * capacity, dtype=jnp.int32)[:, None]
    filled = jnp.any(matches, axis=1)
    source = jnp.sum(
        jnp.where(matches, jnp.arange(slot_count, dtype=jnp.int32)[None, :], 0), axis=1
    )
    outgoing = jnp.where(filled[:, None, None], values[source], jnp.zeros((), values.dtype))
    labels = jnp.where(filled, target[source] + 1, 0).astype(jnp.bfloat16)
    outgoing = outgoing.reshape(peer_count, capacity, values.shape[1], values.shape[2])
    return (outgoing, labels.reshape(peer_count, capacity))


def collect_tiles(received, labels, own_count):
    flat = received.reshape(-1, received.shape[2], received.shape[3])
    wanted = (jnp.arange(own_count, dtype=jnp.int32) + 1).astype(jnp.bfloat16)
    selector = (labels.reshape(-1)[None, :] == wanted[:, None]).astype(jnp.bfloat16)
    return jnp.einsum("oq,qij->oij", selector, flat, preferred_element_type=jnp.float32)


def body(amps, integrals, a_index, b_index, live, owner, target):
    slot_count = owner.shape[0]
    per_slot = a_index.shape[0] // slot_count
    peer_count = lax.axis_size("task")
    capacity = max(2, (2 * slot_count + peer_count - 1) // peer_count)
    partials = slot_products(amps, integrals, a_index, b_index, live, slot_count, per_slot)
    outgoing, labels = route_slots(partials, owner, target, peer_count, capacity)
    received, got_labels = (
        lax.all_to_all(outgoing, "task", split_axis=0, concat_axis=0, tiled=True),
        lax.all_to_all(labels, "task", split_axis=0, concat_axis=0, tiled=True),
    )
    summed = lax.psum_scatter(
        received.astype(jnp.float32).astype(jnp.bfloat16), "rep", scatter_dimension=2, tiled=True
    )
    return collect_tiles(summed, got_labels, OWN_DEV)


def solution(mesh):
    in_specs = (
        P("task", None, "rep"),
        P(None, "rep", None),
        P("task"),
        P("task"),
        P("task"),
        P("task", None),
        P("task"),
    )
    out_specs = P("task", "rep", None)
    return jax.shard_map(body, mesh=mesh, in_specs=in_specs, out_specs=out_specs, check_vma=False)
```

profile of v0, /device:TPU:1, one launch (start us, length us, event | category | flops | bytes accessed | tf_op | source)
XLA Modules:
  0.0 652.0 jit_solution(350049568072402258)
XLA Ops:
  6.5 0.0 copy-start
  6.5 0.0 reduce-scatter.2.cloned.1.call-start
  6.5 0.7 fusion.20
  7.3 0.1 reduce_window_sum.11
  7.4 0.8 select_reduce_fusion.1
  8.2 0.7 multiply_add_fusion
  8.9 0.1 fusion.19
  9.0 0.1 select_reduce_fusion
  9.0 0.8 reshape.154
  9.8 0.8 reshape.156
  10.6 0.8 reshape.155
  11.3 0.1 broadcast_in_dim.60
  11.5 48.4 %while.10 = (s32[]{:T(128)}, bf16[6,8,256,256]{3,2,1,0:T(8,128)(2,1)}, s32[6,64]{1,0:T(8,128)S(1)}, bf16[8,256,64]{1,2,0:T(8,128)(2,1)}, s32[6,64]{1,0:T(8,128)S...) while((s32[]{:T(128)}, bf16[6,8,256,256]{3,2,1,0:T(8,128)(2,1)}, ...), condition=%wide.region_5.6_spmd, body=%wide.region_4.5_spmd.sunk | while | flops 538446272 | bytes 14690949 | solution.py:28
  11.5 0.0 copy-start.1
  11.5 0.1 gt.15
  11.7 3.6 gather_fusion.1
  15.3 0.0 copy-done.1
  15.3 0.7 gather_fusion
  16.0 3.6 fusion.34
  19.6 0.0 copy-start.1
  19.6 0.1 gt.15
  19.7 3.6 gather_fusion.1
  23.3 0.0 copy-done.1
  23.3 0.7 gather_fusion
  24.0 3.6 fusion.34
  27.7 0.0 copy-start.1
  27.7 0.1 gt.15
  27.8 3.6 gather_fusion.1
  31.4 0.0 copy-done.1
  31.4 0.7 gather_fusion
  32.1 3.6 fusion.34
  35.7 0.0 copy-start.1
  35.7 0.1 gt.15
  35.9 3.6 gather_fusion.1
  39.5 0.0 copy-done.1
  39.5 0.7 gather_fusion
  40.2 3.6 fusion.34
  43.8 0.1 gt.15
  43.9 3.6 gather_fusion.1
  47.5 0.0 copy-done.1
  47.5 0.7 gather_fusion
  48.2 3.6 fusion.34
  51.8 0.1 gt.15
  51.9 3.6 gather_fusion.1
  55.6 0.0 copy-done.1
  55.6 0.7 gather_fusion
  56.3 3.6 fusion.34
  59.9 10.8 %gather_fusion.3 = bf16[128,256,256]{2,1,0:T(8,128)(2,1)} fusion(bf16[48,256,256]{2,1,0:T(8,128)(2,1)} %bitcast.59, s32[1024]{0:T(1024)S(1)} %pad_clamp_fusion.2), kind=kCustom, calls=%fused_computation.3 | custom fusion | bytes 33554944 | tf_op jit(solution)/shard_map/gather | solution.py:46
  70.6 8.3 %broadcast_select_fusion = bf16[64,2,256,256]{3,2,1,0:T(8,128)(2,1)S(1)} fusion(bf16[64,2,256,256]{3,2,1,0:T(8,128)(2,1)} %bitcast.57, pred[64,2]{1,0:T(8,128)(4,1)S(1)} %broadcast_in_dim.60), kind=kLoop, calls=%fused_computation.24 | loop fusion | flops 8388608 | bytes 33554560 | tf_op jit(solution)/shard_map/jit(_where)/select_n | solution.py:46
  78.9 14.6 %copy.22 = bf16[64,2,256,256]{3,1,2,0:T(2,128)(2,1)} copy(bf16[64,2,256,256]{3,2,1,0:T(8,128)(2,1)S(1)} %broadcast_select_fusion) | data formatting | bytes 33554432 | tf_op jit(solution)/shard_map/jit(_where)/select_n | solution.py:46
  93.5 377.4 %all_to_all.11 = bf16[64,2,256,256]{3,1,2,0:T(2,128)(2,1)S(1)} all-to-all(bf16[64,2,256,256]{3,1,2,0:T(2,128)(2,1)} %copy.22), channel_id=1, replica_groups=mesh['rep'=4,'task'=64] {'task'}, dimensions={0} | all-to-all | bytes 33554432 | tf_op jit(solution)/shard_map/all_to_all | solution.py:67
  470.9 18.0 %copy.23 = bf16[64,2,256,256]{3,0,1,2:T(8,128)(2,1)} copy(bf16[64,2,256,256]{3,1,2,0:T(2,128)(2,1)S(1)} %all_to_all.11) | data formatting | bytes 33554432 | tf_op jit(solution)/shard_map/all_to_all | solution.py:67
  488.9 0.0 reduce-scatter.2.cloned.1.call-update
  488.9 0.0 copy-done
  488.9 1.2 gather_fusion.2
  490.2 0.8 convert_element_type.34
  491.0 6.9 %all-to-all-start = ((bf16[64,1,2]{2,1,0:T(2,128)(2,1)}), bf16[64,1,2]{2,1,0:T(2,128)(2,1)S(1)}, u32[]{:S(2)}, u32[]{:S(2)}) async-start(bf16[64,1,2]{2,1,0:T(2,128)(2,1)} %convert_element_type.34), calls=%async_computation | async-start | bytes 65536 | tf_op jit(solution)/shard_map/all_to_all | solution.py:68
  497.9 9.3 %all-to-all-done = bf16[64,1,2]{2,1,0:T(2,128)(2,1)S(1)} async-done(((bf16[64,1,2]{2,1,0:T(2,128)(2,1)}), bf16[64,1,2]{2,1,0:T(2,128)(2,1)S(1)}, u32[]{:S(2)}, u32[]{:S(2)}) %all-to-all-start) | async-done | bytes 288 | tf_op jit(solution)/shard_map/all_to_all | solution.py:68
  507.2 0.1 reduce.1
  507.3 0.1 eq.47
  507.4 129.9 %reduce-scatter.2.cloned.1.call-done = bf16[64,2,64,256]{3,0,1,2:T(8,128)(2,1)} async-done(((bf16[64,2,256,256]{3,0,1,2:T(8,128)(2,1)}), bf16[64,2,64,256]{3,0,1,2:T(8,128)(2,1)}) %reduce-scatter.2.cloned.1.call-update) | async-done | bytes 4194320 | tf_op jit(solution)/shard_map/reduce_scatter | solution.py:70
  637.3 4.6 copy.24
  641.9 2.3 fusion.17
  644.2 1.0 copy.26
  (31 shorter events, 0.3 us)
Async XLA Ops:
  6.5 482.4 %copy-start = (s32[48]{0:T(128)S(1)}, s32[48]{0:T(128)}, u32[]{:S(2)}) copy-start(s32[48]{0:T(128)} %param.15) | copy-start | bytes 580
  6.5 630.8 %reduce-scatter.2.cloned.1.call-start = ((), (), s32[]{:S(2)}) async-start(), calls=%async_computation.3 | async-start | bytes 20971520 | tf_op jit(solution)/shard_map/reduce_scatter | solution.py:70
  11.5 3.8 copy-start.1
  19.6 3.8 copy-start.1
  27.7 3.8 copy-start.1
  35.7 3.8 copy-start.1
  43.8 3.8 copy-start.1
  51.8 3.8 copy-start.1
  491.0 16.2 %all-to-all-start = ((bf16[64,1,2]{2,1,0:T(2,128)(2,1)}), bf16[64,1,2]{2,1,0:T(2,128)(2,1)S(1)}, u32[]{:S(2)}, u32[]{:S(2)}) async-start(bf16[64,1,2]{2,1,0:T(2,128)(2,1)} %convert_element_type.34), calls=%async_computation | async-start | bytes 65536 | tf_op jit(solution)/shard_map/all_to_all | solution.py:68
Sparse Core Ops, SparseCore 0:
  489.0 148.2 reduce-scatter.1
where the time goes:
time: 653 us; the launch traced here: 652 us
  blocking collectives  377 us (58%)
  waiting for transfers between devices  139 us (21%)
  local copies, waits for them, and re-layouts  79.8 us (12%)
  matrix products  23.9 us (4%)
  between operations  13.5 us (2%)
  other arithmetic  11.2 us (2%)
  starting transfers between devices  6.89 us (1%)
    all_to_all x1, blocking collectives, body(): lax.all_to_all(outgoing, 'task', split_axis=0, concat_axis=0, tiled=True)  377 us
    reduce_scatter x1, waiting for transfers between devices, body(): lax.psum_scatter(received.astype(jnp.float32).astype(jnp.bfloat16), 'rep'...  130 us
    gather x6, local copies, waits for them, and re-layouts, one_block(): integrals[right_ids]  21.7 us
    dot_general x6, matrix products, one_block(): jnp.einsum('stik,stkj->sij', left, right, preferred_element_type=jnp.floa...  21.6 us
    all_to_all x1, local copies, waits for them, and re-layouts, body(): lax.all_to_all(outgoing, 'task', split_axis=0, concat_axis=0, tiled=True)  18 us
    select_n x1, local copies, waits for them, and re-layouts, route_slots(): jnp.where(filled[:, None, None], values[source], jnp.zeros((), values.dty...  14.6 us
  transfers between devices with their start and end apart: 2, of which 2 were waited for; matrix products, arithmetic and copies ran while one was open for 0% of the time, Pallas kernels for 0%

commit v1 on v0

v1 whole, which is shorter than its diff:
```python
import functools

import jax
import jax.numpy as jnp
from jax import lax
from jax.experimental import pallas as pl
from jax.experimental.pallas import tpu as pltpu
from jax.sharding import Mesh
from jax.sharding import PartitionSpec as P

N_REP, N_Z, N_X, N_CORE = 4, 8, 4, 2
N_SRC = N_Z * N_CORE
OWN_DEV = 8
CAP = 2
TPS = 8
NB = 64
FIELDS = 32
ENTRIES = N_X * CAP
BF16 = jnp.bfloat16
F32 = jnp.float32


def slot_table(a_index, b_index, live, owner, target):
    slots = owner.shape[0]
    own = owner[:, 0]
    order = jnp.arange(slots, dtype=jnp.int32)
    earlier = (own[:, None] == own[None, :]) & (order[None, :] < order[:, None])
    standing = jnp.sum(earlier.astype(jnp.int32), axis=1)
    z, x, core = own // (N_X * N_CORE), (own // N_CORE) % N_X, own % N_CORE
    position = (z * N_CORE + core) * ENTRIES + x * CAP + standing
    chosen = jnp.arange(N_SRC * ENTRIES, dtype=jnp.int32)[:, None] == position[None, :]
    right = jnp.where(live > 0, b_index + 1, 0).reshape(slots, TPS)
    fields = jnp.concatenate(
        [
            (target + 1)[:, None],
            a_index.reshape(slots, TPS),
            right,
            jnp.zeros((slots, FIELDS - 1 - 2 * TPS), jnp.int32),
        ],
        axis=1,
    )
    table = jnp.dot(chosen.astype(F32), fields.astype(F32), precision=lax.Precision.HIGHEST)
    return table.astype(jnp.int32).reshape(N_SRC, ENTRIES * FIELDS)


def spread_rows(left):
    packed = left.transpose(0, 2, 1).reshape(4, 128, 4, 64)
    return packed.transpose(2, 0, 3, 1)


def join_k_kernel(parts_ref, out_ref):
    for pair in range(4):
        pieces = [parts_ref[r, pair] for r in range(N_REP)]
        for side in range(2):
            out_ref[2 * pair + side] = jnp.concatenate(
                [p[:, 64 * side : 64 * side + 64] for p in pieces], axis=1
            )


def join_k(parts):
    return pl.pallas_call(
        join_k_kernel,
        out_shape=jax.ShapeDtypeStruct((8, 64, 256), BF16),
        in_specs=[pl.BlockSpec(memory_space=pltpu.VMEM)],
        out_specs=pl.BlockSpec(memory_space=pltpu.VMEM),
        name="join_k",
    )(parts)


def products_kernel(place_ref, table_ref, *refs):
    lefts = refs[:N_SRC]
    right_hbm = refs[N_SRC]
    outs = refs[N_SRC + 1 : N_SRC + 1 + N_X]
    left, right, total, left_sems, right_sem = refs[N_SRC + 1 + N_X :]
    copies = [
        pltpu.make_async_copy(lefts[i], left.at[i], left_sems.at[i]) for i in range(N_SRC)
    ]
    copies.append(pltpu.make_async_copy(right_hbm, right, right_sem))
    for copy in copies:
        copy.start()
    total[...] = jnp.zeros_like(total)
    for copy in copies:
        copy.wait()
    my_x = place_ref[N_SRC]

    def one_entry(entry, carry):
        base = entry * FIELDS
        label = table_ref[base]

        @pl.when(label > 0)
        def _():
            source = entry // ENTRIES
            ahead = lax.rem((entry // CAP) % N_X - my_x + N_X, N_X)
            block = place_ref[source]
            spot = ahead * OWN_DEV + label - 1
            acc = jnp.zeros((64, 256), F32)
            for t in range(TPS):
                a = table_ref[base + 1 + t]
                b = table_ref[base + 1 + TPS + t]
                lhs = left[block, a]
                lhs = jnp.where(b > 0, lhs, jnp.zeros_like(lhs))
                b = jnp.maximum(b - 1, 0)
                rhs = jnp.concatenate([right[r, b] for r in range(N_REP)], axis=0)
                acc += jnp.dot(lhs, rhs, preferred_element_type=F32)
            total[spot] += acc

        return carry

    lax.fori_loop(0, N_SRC * ENTRIES, one_entry, 0)
    for ahead in range(N_X):
        part = total[ahead * OWN_DEV : (ahead + 1) * OWN_DEV]
        outs[ahead][...] = part.astype(outs[ahead].dtype)


def products(place, table, lefts, right):
    anywhere = pl.BlockSpec(memory_space=pl.ANY)
    shape = (OWN_DEV, 64, 256)
    return pl.pallas_call(
        products_kernel,
        out_shape=[jax.ShapeDtypeStruct(shape, F32 if s == 0 else BF16) for s in range(N_X)],
        grid_spec=pltpu.PrefetchScalarGridSpec(
            num_scalar_prefetch=2,
            grid=(),
            in_specs=[anywhere] * (N_SRC + 1),
            out_specs=[pl.BlockSpec(memory_space=pltpu.VMEM)] * N_X,
            scratch_shapes=[
                pltpu.VMEM((N_SRC, 8, 64, 256), BF16),
                pltpu.VMEM((N_REP, NB, 64, 256), BF16),
                pltpu.VMEM((N_X * OWN_DEV, 64, 256), F32),
                pltpu.SemaphoreType.DMA((N_SRC,)),
                pltpu.SemaphoreType.DMA,
            ],
        ),
        compiler_params=pltpu.CompilerParams(vmem_limit_bytes=40 * 1024 * 1024),
        cost_estimate=pl.CostEstimate(
            flops=2 * 384 * 64 * 256 * 256, bytes_accessed=13 << 20, transcendentals=0
        ),
        name="products",
    )(place, table, *lefts, right)


def away(value):
    perm = []
    for z in range(N_Z):
        perm.append((z * 2, ((z + 1) % N_Z) * 2))
        perm.append((z * 2 + 1, ((z - 1) % N_Z) * 2 + 1))
    return lax.ppermute(value, ("z", "core"), perm)


def other_core(value):
    return lax.ppermute(value, "core", [(0, 1), (1, 0)])


def gather_blocks(mine):
    own, other = mine, other_core(mine)
    blocks = [own, other]
    for distance in range(1, 4):
        own, other = away(own), away(other)
        blocks += [own, other, other_core(own), other_core(other)]
    own = away(own)
    blocks += [own, other_core(own)]
    z, core = lax.axis_index("z"), lax.axis_index("core")
    source = jnp.arange(N_SRC, dtype=jnp.int32)
    ahead = (source // N_CORE - z + N_Z) % N_Z
    ahead = jnp.where(core == 0, (N_Z - ahead) % N_Z, ahead)
    same = source % N_CORE == core
    first = jnp.where(same, 0, 1)
    place = jnp.where(ahead < 4, 4 * ahead - 2 + first, 4 * (N_Z - ahead) + 1 - first)
    place = jnp.where(ahead == 0, first, place)
    place = jnp.where(ahead == 4, 14 + first, place)
    return blocks, place.astype(jnp.int32)


def body(amps, integrals, a_index, b_index, live, owner, target):
    core = lax.axis_index("core")
    half = lax.dynamic_slice_in_dim(integrals, core * (NB // 2), NB // 2, 0)
    right = lax.all_gather(half, ("rep", "core"), tiled=False).reshape(N_REP, NB, 64, 256)
    table = slot_table(a_index, b_index, live, owner, target)
    table = lax.all_to_all(table, ("z", "core"), split_axis=0, concat_axis=0, tiled=True)
    parts = lax.all_to_all(spread_rows(amps), "rep", split_axis=0, concat_axis=0, tiled=True)
    blocks, place = gather_blocks(join_k(parts))
    place = jnp.concatenate([place, lax.axis_index("x").astype(jnp.int32)[None]])
    sums = products(place, table.reshape(-1), blocks, right)
    total = sums[0]
    for ahead in range(1, N_X):
        perm = [(i, (i + ahead) % N_X) for i in range(N_X)]
        total = total + lax.ppermute(sums[ahead], "x", perm).astype(F32)
    return total


def solution(mesh):
    devices = mesh.devices.reshape(N_REP, N_Z, N_X, N_CORE)
    fine = Mesh(devices, ("rep", "z", "x", "core"))
    task = ("z", "x", "core")
    in_specs = (
        P(task, None, "rep"),
        P(None, "rep", None),
        P(task),
        P(task),
        P(task),
        P(task, None),
        P(task),
    )
    return jax.shard_map(
        body, mesh=fine, in_specs=in_specs, out_specs=P(task, "rep", None), check_vma=False
    )
```

time: 653 us -> 125 us (0.19)
  the two profiles are of different devices: /device:TPU:1 before, /device:TPU:6 now
where the time goes in v1:
time: 125 us; the launch traced here: 123 us
  waiting for transfers between devices  46.8 us (37%)
  Pallas kernels  27.9 us (22%)
  between operations  13.6 us (11%)
  starting transfers between devices  13.4 us (11%)
  blocking collectives  11 us (9%)
  local copies, waits for them, and re-layouts  8.82 us (7%)
    ppermute x7, waiting for transfers between devices, away(): return lax.ppermute(value, ('z', 'core'), perm)  30.5 us
    pallas_call x1, Pallas kernels, products(): pl.pallas_call(products_kernel, out_shape=[jax.ShapeDtypeStruct(shape, F3...  26.1 us
    all_to_all x1, blocking collectives, body(): lax.all_to_all(spread_rows(amps), 'rep', split_axis=0, concat_axis=0, til...  11 us
    ppermute x3, waiting for transfers between devices, body(): total = total + lax.ppermute(sums[ahead], 'x', perm).astype(F32)  8.75 us
    all_to_all x1, waiting for transfers between devices, body(): lax.all_to_all(table, ('z', 'core'), split_axis=0, concat_axis=0, tiled=T...  7.5 us
    all_to_all x1, starting transfers between devices, body(): lax.all_to_all(table, ('z', 'core'), split_axis=0, concat_axis=0, tiled=T...  6.03 us
    unnamed x18, local copies, waits for them, and re-layouts  5.94 us
    ppermute x8, starting transfers between devices, other_core(): return lax.ppermute(value, 'core', [(0, 1), (1, 0)])  3.38 us
  transfers between devices with their start and end apart: 20, of which 11 were waited for; matrix products, arithmetic and copies ran while one was open for 1% of the time, Pallas kernels for 1%

profile of v1, /device:TPU:6, one launch (start us, length us, event | category | flops | bytes accessed | tf_op | source)
XLA Modules:
  0.0 123.1 jit_solution(2978883179491948580)
XLA Ops:
  6.5 0.0 copy-start
  6.5 0.0 all-gather.3.cloned.1.call-start
  6.5 1.6 %copy-done = bf16[64,64,256]{2,1,0:T(8,128)(2,1)S(1)} copy-done((bf16[64,64,256]{2,1,0:T(8,128)(2,1)S(1)}, bf16[64,64,256]{2,1,0:T(8,128)(2,1)}, u32[]{:S(2)}) %copy-start) | copy-done | bytes 2097176
  8.1 1.2 constant_dynamic-slice_fusion
  9.3 0.0 copy-start.6
  9.3 0.0 all-gather.3.cloned.1.call-update
  9.3 0.2 reshape.105
  9.6 0.3 copy.22
  9.9 11.0 %all_to_all.15.parts_ref = bf16[4,4,64,128]{3,2,1,0:T(8,128)(2,1)} all-to-all(bf16[4,4,64,128]{3,2,1,0:T(8,128)(2,1)S(1)} %bitcast.11), channel_id=1, replica_groups=mesh['rep'=4,'z'=8,'x'=4,'core'=2] {'rep'}, dimensions={0} | all-to-all | bytes 524288 | tf_op jit(solution)/shard_map/all_to_all | solution.py:180
  21.0 1.8 %join_k.1.refs_0_ = bf16[8,64,256]{2,1,0:T(8,128)(2,1)} custom-call(bf16[4,4,64,128]{3,2,1,0:T(8,128)(2,1)} %all_to_all.15.parts_ref), custom_call_target="tpu_custom_call" | custom-call | tf_op jit(solution)/shard_map/join_k/pallas_call | solution.py:61
  22.8 1.9 %collective-permute-start.1 = (bf16[8,64,256]{2,1,0:T(8,128)(2,1)}, bf16[8,64,256]{2,1,0:T(8,128)(2,1)S(1)}, u32[]{:S(2)}, u32[]{:S(2)}) collective-permute-start(bf16[8,64,256]{2,1,0:T(8,128)(2,1)} %join_k.1.refs_0_), channel_id=1, source_target_pairs={{0,8},{1,57},{8,16},{9,1},{16,24},{17,9},{24,32},{25,17},{32,40},{... | collective-permute-start | bytes 786440 | tf_op jit(solution)/shard_map/ppermute | solution.py:147
  24.7 2.1 %collective-permute-start = (bf16[8,64,256]{2,1,0:T(8,128)(2,1)}, bf16[8,64,256]{2,1,0:T(8,128)(2,1)S(1)}, u32[]{:S(2)}, u32[]{:S(2)}) collective-permute-start(bf16[8,64,256]{2,1,0:T(8,128)(2,1)} %join_k.1.refs_0_), channel_id=1, source_target_pairs={{0,1},{1,0},{2,3},{3,2},{4,5},{5,4},{6,7},{7,6},{8,9},{9,8},{10,11... | collective-permute-start | bytes 786440 | tf_op jit(solution)/shard_map/ppermute | solution.py:151
  26.8 6.4 %collective-permute-done.1.refs_2_ = bf16[8,64,256]{2,1,0:T(8,128)(2,1)S(1)} collective-permute-done((bf16[8,64,256]{2,1,0:T(8,128)(2,1)}, bf16[8,64,256]{2,1,0:T(8,128)(2,1)S(1)}, u32[]{:S(2)}, u32[]{:S(2)}) %collective-permute-start.1) | collective-permute-done | bytes 262176 | tf_op jit(solution)/shard_map/ppermute | solution.py:147
  33.2 0.0 collective-permute-start.5
  33.2 0.0 collective-permute-done.refs_1_
  33.2 0.0 collective-permute-start.2
  33.2 7.6 %collective-permute-done.5.refs_6_ = bf16[8,64,256]{2,1,0:T(8,128)(2,1)S(1)} collective-permute-done((bf16[8,64,256]{2,1,0:T(8,128)(2,1)S(1)}, bf16[8,64,256]{2,1,0:T(8,128)(2,1)S(1)}, u32[]{:S(2)}, u32[]{:S(2)}) %collective-permute-start.5) | collective-permute-done | bytes 262176 | tf_op jit(solution)/shard_map/ppermute | solution.py:147
  40.8 0.0 collective-permute-start.9
  40.8 2.8 %collective-permute-done.2.refs_3_ = bf16[8,64,256]{2,1,0:T(8,128)(2,1)S(1)} collective-permute-done((bf16[8,64,256]{2,1,0:T(8,128)(2,1)S(1)}, bf16[8,64,256]{2,1,0:T(8,128)(2,1)S(1)}, u32[]{:S(2)}, u32[]{:S(2)}) %collective-permute-start.2) | collective-permute-done | bytes 262176 | tf_op jit(solution)/shard_map/ppermute | solution.py:147
  43.6 0.0 collective-permute-start.6
  43.6 0.0 copy-done.4
  43.6 0.0 copy-done.5
  43.6 0.1 collective-permute-start.3
  43.7 0.5 collective-permute-start.7
  44.2 4.1 %collective-permute-done.9.refs_10_ = bf16[8,64,256]{2,1,0:T(8,128)(2,1)S(1)} collective-permute-done((bf16[8,64,256]{2,1,0:T(8,128)(2,1)S(1)}, bf16[8,64,256]{2,1,0:T(8,128)(2,1)S(1)}, u32[]{:S(2)}, u32[]{:S(2)}) %collective-permute-start.9) | collective-permute-done | bytes 262176 | tf_op jit(solution)/shard_map/ppermute | solution.py:147
  48.4 0.0 collective-permute-start.13
  48.4 2.9 %collective-permute-done.6.refs_7_ = bf16[8,64,256]{2,1,0:T(8,128)(2,1)} collective-permute-done((bf16[8,64,256]{2,1,0:T(8,128)(2,1)S(1)}, bf16[8,64,256]{2,1,0:T(8,128)(2,1)}, u32[]{:S(2)}, u32[]{:S(2)}) %collective-permute-start.6) | collective-permute-done | bytes 262176 | tf_op jit(solution)/shard_map/ppermute | solution.py:147
  51.3 0.0 collective-permute-start.10
  51.3 0.2 convert_reduce_fusion
  51.5 0.1 pad.3.clone
  51.6 0.1 reshape.99
  51.6 0.1 copy.18
  51.7 0.1 reshape.98
  51.9 0.1 collective-permute-start.4
  52.0 0.0 collective-permute-done.3.refs_4_
  52.0 0.5 collective-permute-start.11
  52.5 0.0 collective-permute-done.7.refs_8_
  52.5 0.1 collective-permute-start.8
  52.6 3.5 %collective-permute-done.13.refs_14_ = bf16[8,64,256]{2,1,0:T(8,128)(2,1)} collective-permute-done((bf16[8,64,256]{2,1,0:T(8,128)(2,1)S(1)}, bf16[8,64,256]{2,1,0:T(8,128)(2,1)}, u32[]{:S(2)}, u32[]{:S(2)}) %collective-permute-start.13) | collective-permute-done | bytes 262176 | tf_op jit(solution)/shard_map/ppermute | solution.py:147
  56.1 0.0 collective-permute-start.14
  56.1 3.1 %collective-permute-done.10.refs_11_ = bf16[8,64,256]{2,1,0:T(8,128)(2,1)} collective-permute-done((bf16[8,64,256]{2,1,0:T(8,128)(2,1)}, bf16[8,64,256]{2,1,0:T(8,128)(2,1)}, u32[]{:S(2)}, u32[]{:S(2)}) %collective-permute-start.10) | collective-permute-done | bytes 262176 | tf_op jit(solution)/shard_map/ppermute | solution.py:147
  59.2 0.0 collective-permute-start.12
  59.2 0.3 convolution_convert_fusion
  59.5 0.1 copy.19
  59.6 0.7 all_to_all.12
  60.3 6.0 %all-to-all-start = ((s32[16,1,256]{2,1,0:T(1,128)}), s32[16,1,256]{2,1,0:T(1,128)S(1)}, u32[]{:S(2)}, u32[]{:S(2)}) async-start(s32[16,1,256]{2,1,0:T(1,128)} %all_to_all.12), calls=%async_computation | async-start | bytes 32768 | tf_op jit(solution)/shard_map/all_to_all | solution.py:179
  66.4 0.1 pad_add_fusion.place_ref
  66.5 7.5 %all-to-all-done = s32[16,1,256]{2,1,0:T(1,128)S(1)} async-done(((s32[16,1,256]{2,1,0:T(1,128)}), s32[16,1,256]{2,1,0:T(1,128)S(1)}, u32[]{:S(2)}, u32[]{:S(2)}) %all-to-all-start) | async-done | bytes 16416 | tf_op jit(solution)/shard_map/all_to_all | solution.py:179
  74.0 0.0 collective-permute-done.4.refs_5_
  74.0 0.0 collective-permute-done.11.refs_12_
  74.0 0.0 collective-permute-done.8.refs_9_
  74.0 0.0 collective-permute-done.14.refs_15_
  74.0 0.0 collective-permute-done.12.refs_13_
  74.0 0.0 all-gather.3.cloned.1.call-done
  74.0 3.4 %copy-done.1 = bf16[256,64,256]{2,1,0:T(8,128)(2,1)S(1)} copy-done((bf16[256,64,256]{2,1,0:T(8,128)(2,1)S(1)}, bf16[256,64,256]{2,1,0:T(8,128)(2,1)}, u32[]{:S(2)}) %copy-start.1) | copy-done | bytes 8388632
  77.4 0.9 copy-done.2
  78.4 26.1 %products.1 = (f32[8,64,256]{2,1,0:T(8,128)S(1)}, bf16[8,64,256]{2,1,0:T(8,128)(2,1)S(1)}, bf16[8,64,256]{2,1,0:T(8,128)(2,1)S(1)}, bf16[8,64,256]{2,1,0:T(8,128)(2,1)S(1)}) custom-call(s32[17]{0:T(128)S(1)} %pad_add_fusion.place_ref, s32[4096]{0:T(1024)S(1)} %bitcast.10, bf16[8,64,256]{2,1,0:T(8,128)(2,1)S(1)} %copy-done.2, ...), custom_call_target="tpu_custom_call" | custom-call | flops 3221225472 | bytes 13631488 | tf_op jit(solution)/shard_map/products/pallas_call | solution.py:118
  104.5 0.1 collective-permute-start.15
  104.5 0.6 collective-permute-start.16
  105.1 1.4 %collective-permute-start.17 = (bf16[8,64,256]{2,1,0:T(8,128)(2,1)S(1)}, bf16[8,64,256]{2,1,0:T(8,128)(2,1)S(1)}, u32[]{:S(2)}, u32[]{:S(2)}) collective-permute-start(bf16[8,64,256]{2,1,0:T(8,128)(2,1)S(1)} %get-tuple-element.12), channel_id=1, source_target_pairs={{0,6},{2,0},{4,2},{6,4},{1,7},{3,1},{5,3},{7,5},{8,14},{10,8},{12,... | collective-permute-start | bytes 786440 | tf_op jit(solution)/shard_map/ppermute | solution.py:187
  106.6 4.3 %collective-permute-done.15 = bf16[8,64,256]{2,1,0:T(8,128)(2,1)S(1)} collective-permute-done((bf16[8,64,256]{2,1,0:T(8,128)(2,1)S(1)}, bf16[8,64,256]{2,1,0:T(8,128)(2,1)S(1)}, u32[]{:S(2)}, u32[]{:S(2)}) %collective-permute-start.15) | collective-permute-done | bytes 262176 | tf_op jit(solution)/shard_map/ppermute | solution.py:187
  110.9 1.7 %collective-permute-done.16 = bf16[8,64,256]{2,1,0:T(8,128)(2,1)S(1)} collective-permute-done((bf16[8,64,256]{2,1,0:T(8,128)(2,1)S(1)}, bf16[8,64,256]{2,1,0:T(8,128)(2,1)S(1)}, u32[]{:S(2)}, u32[]{:S(2)}) %collective-permute-start.16) | collective-permute-done | bytes 262176 | tf_op jit(solution)/shard_map/ppermute | solution.py:187
  112.6 2.7 %collective-permute-done.17 = bf16[8,64,256]{2,1,0:T(8,128)(2,1)S(1)} collective-permute-done((bf16[8,64,256]{2,1,0:T(8,128)(2,1)S(1)}, bf16[8,64,256]{2,1,0:T(8,128)(2,1)S(1)}, u32[]{:S(2)}, u32[]{:S(2)}) %collective-permute-start.17) | collective-permute-done | bytes 262176 | tf_op jit(solution)/shard_map/ppermute | solution.py:187
  115.3 0.9 convert_add_fusion
  (16 shorter events, 0.1 us)
Async XLA Ops:
  6.5 1.6 %copy-start = (bf16[64,64,256]{2,1,0:T(8,128)(2,1)S(1)}, bf16[64,64,256]{2,1,0:T(8,128)(2,1)}, u32[]{:S(2)}) copy-start(bf16[64,64,256]{2,1,0:T(8,128)(2,1)} %param.8) | copy-start | bytes 6291460
  6.5 2.8 %copy-start.3 = (bf16[8,256,64]{1,2,0:T(8,128)(2,1)S(1)}, bf16[8,256,64]{1,2,0:T(8,128)(2,1)}, u32[]{:S(2)}) copy-start(bf16[8,256,64]{1,2,0:T(8,128)(2,1)} %param.7) | copy-start | bytes 786436
  6.5 67.5 %all-gather.3.cloned.1.call-start = ((), (), s32[]{:S(2)}) async-start(), calls=%async_computation.2 | async-start | bytes 9437184 | tf_op jit(solution)/shard_map/all_gather | solution.py:177
  9.3 34.3 %copy-start.7 = (s32[48]{0:T(128)S(1)}, s32[48]{0:T(128)}, u32[]{:S(2)}) copy-start(s32[48]{0:T(128)} %param.13) | copy-start | bytes 580
  9.3 34.3 %copy-start.4 = (s32[384]{0:T(512)S(1)}, s32[384]{0:T(512)}, u32[]{:S(2)}) copy-start(s32[384]{0:T(512)} %param.10) | copy-start | bytes 4612
  9.3 34.3 %copy-start.5 = (s32[384]{0:T(512)S(1)}, s32[384]{0:T(512)}, u32[]{:S(2)}) copy-start(s32[384]{0:T(512)} %param.11) | copy-start | bytes 4612
  9.3 42.0 %copy-start.8 = (s32[48,1]{0,1:T(1,128)S(1)}, s32[48,1]{0,1:T(1,128)}, u32[]{:S(2)}) copy-start(s32[48,1]{0,1:T(1,128)} %param.12) | copy-start | bytes 580
  9.3 42.4 %copy-start.6 = (s32[384]{0:T(512)S(1)}, s32[384]{0:T(512)}, u32[]{:S(2)}) copy-start(s32[384]{0:T(512)} %param.9) | copy-start | bytes 4612
  22.8 10.4 %collective-permute-start.1 = (bf16[8,64,256]{2,1,0:T(8,128)(2,1)}, bf16[8,64,256]{2,1,0:T(8,128)(2,1)S(1)}, u32[]{:S(2)}, u32[]{:S(2)}) collective-permute-start(bf16[8,64,256]{2,1,0:T(8,128)(2,1)} %join_k.1.refs_0_), channel_id=1, source_target_pairs={{0,8},{1,57},{8,16},{9,1},{16,24},{17,9},{24,32},{25,17},{32,40},{... | collective-permute-start | bytes 786440 | tf_op jit(solution)/shard_map/ppermute | solution.py:147
  24.7 8.5 %collective-permute-start = (bf16[8,64,256]{2,1,0:T(8,128)(2,1)}, bf16[8,64,256]{2,1,0:T(8,128)(2,1)S(1)}, u32[]{:S(2)}, u32[]{:S(2)}) collective-permute-start(bf16[8,64,256]{2,1,0:T(8,128)(2,1)} %join_k.1.refs_0_), channel_id=1, source_target_pairs={{0,1},{1,0},{2,3},{3,2},{4,5},{5,4},{6,7},{7,6},{8,9},{9,8},{10,11... | collective-permute-start | bytes 786440 | tf_op jit(solution)/shard_map/ppermute | solution.py:151
  33.2 7.6 %collective-permute-start.5 = (bf16[8,64,256]{2,1,0:T(8,128)(2,1)S(1)}, bf16[8,64,256]{2,1,0:T(8,128)(2,1)S(1)}, u32[]{:S(2)}, u32[]{:S(2)}) collective-permute-start(bf16[8,64,256]{2,1,0:T(8,128)(2,1)S(1)} %collective-permute-done.1.refs_2_), channel_id=1, source_target_pairs={{0,8},{1,57},{8,16},{9,1},{16,24},{17,9},{24,32},{25,17},{32,40},{... | collective-permute-start | bytes 786440 | tf_op jit(solution)/shard_map/ppermute | solution.py:147
  33.2 10.4 %collective-permute-start.2 = (bf16[8,64,256]{2,1,0:T(8,128)(2,1)S(1)}, bf16[8,64,256]{2,1,0:T(8,128)(2,1)S(1)}, u32[]{:S(2)}, u32[]{:S(2)}) collective-permute-start(bf16[8,64,256]{2,1,0:T(8,128)(2,1)S(1)} %collective-permute-done.refs_1_), channel_id=1, source_target_pairs={{0,8},{1,57},{8,16},{9,1},{16,24},{17,9},{24,32},{25,17},{32,40},{... | collective-permute-start | bytes 786440 | tf_op jit(solution)/shard_map/ppermute | solution.py:147
  40.8 7.6 %collective-permute-start.9 = (bf16[8,64,256]{2,1,0:T(8,128)(2,1)S(1)}, bf16[8,64,256]{2,1,0:T(8,128)(2,1)S(1)}, u32[]{:S(2)}, u32[]{:S(2)}) collective-permute-start(bf16[8,64,256]{2,1,0:T(8,128)(2,1)S(1)} %collective-permute-done.5.refs_6_), channel_id=1, source_target_pairs={{0,8},{1,57},{8,16},{9,1},{16,24},{17,9},{24,32},{25,17},{32,40},{... | collective-permute-start | bytes 786440 | tf_op jit(solution)/shard_map/ppermute | solution.py:147
  43.6 7.7 %collective-permute-start.6 = (bf16[8,64,256]{2,1,0:T(8,128)(2,1)S(1)}, bf16[8,64,256]{2,1,0:T(8,128)(2,1)}, u32[]{:S(2)}, u32[]{:S(2)}) collective-permute-start(bf16[8,64,256]{2,1,0:T(8,128)(2,1)S(1)} %collective-permute-done.2.refs_3_), channel_id=1, source_target_pairs={{0,8},{1,57},{8,16},{9,1},{16,24},{17,9},{24,32},{25,17},{32,40},{... | collective-permute-start | bytes 786440 | tf_op jit(solution)/shard_map/ppermute | solution.py:147
  43.6 8.3 %collective-permute-start.3 = (bf16[8,64,256]{2,1,0:T(8,128)(2,1)S(1)}, bf16[8,64,256]{2,1,0:T(8,128)(2,1)}, u32[]{:S(2)}, u32[]{:S(2)}) collective-permute-start(bf16[8,64,256]{2,1,0:T(8,128)(2,1)S(1)} %collective-permute-done.1.refs_2_), channel_id=1, source_target_pairs={{0,1},{1,0},{2,3},{3,2},{4,5},{5,4},{6,7},{7,6},{8,9},{9,8},{10,11... | collective-permute-start | bytes 786440 | tf_op jit(solution)/shard_map/ppermute | solution.py:151
  43.7 8.7 %collective-permute-start.7 = (bf16[8,64,256]{2,1,0:T(8,128)(2,1)S(1)}, bf16[8,64,256]{2,1,0:T(8,128)(2,1)}, u32[]{:S(2)}, u32[]{:S(2)}) collective-permute-start(bf16[8,64,256]{2,1,0:T(8,128)(2,1)S(1)} %collective-permute-done.5.refs_6_), channel_id=1, source_target_pairs={{0,1},{1,0},{2,3},{3,2},{4,5},{5,4},{6,7},{7,6},{8,9},{9,8},{10,11... | collective-permute-start | bytes 786440 | tf_op jit(solution)/shard_map/ppermute | solution.py:151
  48.4 7.7 %collective-permute-start.13 = (bf16[8,64,256]{2,1,0:T(8,128)(2,1)S(1)}, bf16[8,64,256]{2,1,0:T(8,128)(2,1)}, u32[]{:S(2)}, u32[]{:S(2)}) collective-permute-start(bf16[8,64,256]{2,1,0:T(8,128)(2,1)S(1)} %collective-permute-done.9.refs_10_), channel_id=1, source_target_pairs={{0,8},{1,57},{8,16},{9,1},{16,24},{17,9},{24,32},{25,17},{32,40},{... | collective-permute-start | bytes 786440 | tf_op jit(solution)/shard_map/ppermute | solution.py:147
  51.3 7.9 %collective-permute-start.10 = (bf16[8,64,256]{2,1,0:T(8,128)(2,1)}, bf16[8,64,256]{2,1,0:T(8,128)(2,1)}, u32[]{:S(2)}, u32[]{:S(2)}) collective-permute-start(bf16[8,64,256]{2,1,0:T(8,128)(2,1)} %collective-permute-done.6.refs_7_), channel_id=1, source_target_pairs={{0,8},{1,57},{8,16},{9,1},{16,24},{17,9},{24,32},{25,17},{32,40},{... | collective-permute-start | bytes 786440 | tf_op jit(solution)/shard_map/ppermute | solution.py:147
  51.9 22.1 %collective-permute-start.4 = (bf16[8,64,256]{2,1,0:T(8,128)(2,1)S(1)}, bf16[8,64,256]{2,1,0:T(8,128)(2,1)}, u32[]{:S(2)}, u32[]{:S(2)}) collective-permute-start(bf16[8,64,256]{2,1,0:T(8,128)(2,1)S(1)} %collective-permute-done.2.refs_3_), channel_id=1, source_target_pairs={{0,1},{1,0},{2,3},{3,2},{4,5},{5,4},{6,7},{7,6},{8,9},{9,8},{10,11... | collective-permute-start | bytes 786440 | tf_op jit(solution)/shard_map/ppermute | solution.py:151
  52.0 22.0 %collective-permute-start.11 = (bf16[8,64,256]{2,1,0:T(8,128)(2,1)S(1)}, bf16[8,64,256]{2,1,0:T(8,128)(2,1)}, u32[]{:S(2)}, u32[]{:S(2)}) collective-permute-start(bf16[8,64,256]{2,1,0:T(8,128)(2,1)S(1)} %collective-permute-done.9.refs_10_), channel_id=1, source_target_pairs={{0,1},{1,0},{2,3},{3,2},{4,5},{5,4},{6,7},{7,6},{8,9},{9,8},{10,11... | collective-permute-start | bytes 786440 | tf_op jit(solution)/shard_map/ppermute | solution.py:151
  52.5 21.5 %collective-permute-start.8 = (bf16[8,64,256]{2,1,0:T(8,128)(2,1)}, bf16[8,64,256]{2,1,0:T(8,128)(2,1)}, u32[]{:S(2)}, u32[]{:S(2)}) collective-permute-start(bf16[8,64,256]{2,1,0:T(8,128)(2,1)} %collective-permute-done.6.refs_7_), channel_id=1, source_target_pairs={{0,1},{1,0},{2,3},{3,2},{4,5},{5,4},{6,7},{7,6},{8,9},{9,8},{10,11... | collective-permute-start | bytes 786440 | tf_op jit(solution)/shard_map/ppermute | solution.py:151
  56.1 17.9 %collective-permute-start.14 = (bf16[8,64,256]{2,1,0:T(8,128)(2,1)}, bf16[8,64,256]{2,1,0:T(8,128)(2,1)}, u32[]{:S(2)}, u32[]{:S(2)}) collective-permute-start(bf16[8,64,256]{2,1,0:T(8,128)(2,1)} %collective-permute-done.13.refs_14_), channel_id=1, source_target_pairs={{0,1},{1,0},{2,3},{3,2},{4,5},{5,4},{6,7},{7,6},{8,9},{9,8},{10,11... | collective-permute-start | bytes 786440 | tf_op jit(solution)/shard_map/ppermute | solution.py:151
  59.2 14.8 %collective-permute-start.12 = (bf16[8,64,256]{2,1,0:T(8,128)(2,1)}, bf16[8,64,256]{2,1,0:T(8,128)(2,1)}, u32[]{:S(2)}, u32[]{:S(2)}) collective-permute-start(bf16[8,64,256]{2,1,0:T(8,128)(2,1)} %collective-permute-done.10.refs_11_), channel_id=1, source_target_pairs={{0,1},{1,0},{2,3},{3,2},{4,5},{5,4},{6,7},{7,6},{8,9},{9,8},{10,11... | collective-permute-start | bytes 786440 | tf_op jit(solution)/shard_map/ppermute | solution.py:151
  60.3 13.7 %all-to-all-start = ((s32[16,1,256]{2,1,0:T(1,128)}), s32[16,1,256]{2,1,0:T(1,128)S(1)}, u32[]{:S(2)}, u32[]{:S(2)}) async-start(s32[16,1,256]{2,1,0:T(1,128)} %all_to_all.12), calls=%async_computation | async-start | bytes 32768 | tf_op jit(solution)/shard_map/all_to_all | solution.py:179
  74.0 3.4 %copy-start.1 = (bf16[256,64,256]{2,1,0:T(8,128)(2,1)S(1)}, bf16[256,64,256]{2,1,0:T(8,128)(2,1)}, u32[]{:S(2)}) copy-start(bf16[256,64,256]{2,1,0:T(8,128)(2,1)} %all-gather.3.cloned.1.call-done) | copy-start | bytes 25165828
  77.4 0.9 copy-start.2
  104.5 6.4 %collective-permute-start.15 = (bf16[8,64,256]{2,1,0:T(8,128)(2,1)S(1)}, bf16[8,64,256]{2,1,0:T(8,128)(2,1)S(1)}, u32[]{:S(2)}, u32[]{:S(2)}) collective-permute-start(bf16[8,64,256]{2,1,0:T(8,128)(2,1)S(1)} %get-tuple-element.10), channel_id=1, source_target_pairs={{0,2},{2,4},{4,6},{6,0},{1,3},{3,5},{5,7},{7,1},{8,10},{10,12},{12... | collective-permute-start | bytes 786440 | tf_op jit(solution)/shard_map/ppermute | solution.py:187
  104.5 8.1 %collective-permute-start.16 = (bf16[8,64,256]{2,1,0:T(8,128)(2,1)S(1)}, bf16[8,64,256]{2,1,0:T(8,128)(2,1)S(1)}, u32[]{:S(2)}, u32[]{:S(2)}) collective-permute-start(bf16[8,64,256]{2,1,0:T(8,128)(2,1)S(1)} %get-tuple-element.11), channel_id=1, source_target_pairs={{0,4},{2,6},{4,0},{6,2},{1,5},{3,7},{5,1},{7,3},{8,12},{10,14},{12... | collective-permute-start | bytes 786440 | tf_op jit(solution)/shard_map/ppermute | solution.py:187
  105.1 10.2 %collective-permute-start.17 = (bf16[8,64,256]{2,1,0:T(8,128)(2,1)S(1)}, bf16[8,64,256]{2,1,0:T(8,128)(2,1)S(1)}, u32[]{:S(2)}, u32[]{:S(2)}) collective-permute-start(bf16[8,64,256]{2,1,0:T(8,128)(2,1)S(1)} %get-tuple-element.12), channel_id=1, source_target_pairs={{0,6},{2,0},{4,2},{6,4},{1,7},{3,1},{5,3},{7,5},{8,14},{10,8},{12,... | collective-permute-start | bytes 786440 | tf_op jit(solution)/shard_map/ppermute | solution.py:187
Sparse Core Ops, SparseCore 0:
  9.5 55.1 all-gather.2

commit v2 on v0

v2 whole, which is shorter than its diff:
```python
import jax
import jax.numpy as jnp
from jax import lax
from jax.experimental import pallas as pl
from jax.experimental.pallas import tpu as pltpu
from jax.sharding import Mesh
from jax.sharding import PartitionSpec as P

N_REP, N_Z, N_X, N_CORE = 4, 8, 4, 2
N_SRC = N_Z * N_CORE
A_DEV = 8
OWN_DEV = 8
TPS = 8
NB = 64
HALF = NB // 2
PART = HALF // 2
QUARTER = 64
TILE = 256
MOST = 128
LABELS = 2 * N_SRC
SPOTS = N_X * OWN_DEV
GROUP = 4
WIDE = 8
LIST = 2304
NOWHERE = 2 * SPOTS * 512
TRASH = LIST - 1
ROWS = A_DEV * QUARTER
BLOCK = ROWS + LABELS
VMEM_LIMIT = 56 * 1024 * 1024
BF16 = jnp.bfloat16
F32 = jnp.float32
I32 = jnp.int32
VMEM = pl.BlockSpec(memory_space=pltpu.VMEM)
SMEM = pl.BlockSpec(memory_space=pltpu.SMEM)
ANY = pl.BlockSpec(memory_space=pl.ANY)


def product_table(x, a_index, b_index, live, owner, target):
    products = a_index.shape[0]
    own = jnp.repeat(owner[:, 0], TPS)
    z, own_x, own_core = own // (N_X * N_CORE), (own // N_CORE) % N_X, own % N_CORE
    half = b_index // HALF
    place = jnp.where(live > 0, z * N_CORE + half, -1)
    away = (own_core != half).astype(I32) * SPOTS
    spot = away + ((own_x - x + N_X) % N_X) * OWN_DEV + jnp.repeat(target, TPS) + 1
    order = jnp.arange(products, dtype=I32)
    earlier = (place[:, None] == place[None, :]) & (order[None, :] < order[:, None])
    standing = jnp.sum(earlier.astype(I32), axis=1)
    alike = earlier & (b_index[:, None] == b_index[None, :])
    rank = jnp.sum(alike.astype(I32), axis=1)
    at = jnp.where(live > 0, place * MOST + standing, -1)
    chosen = jnp.arange(N_SRC * MOST, dtype=I32)[:, None] == at[None, :]
    fields = jnp.stack([spot, a_index, b_index % HALF, rank]).astype(BF16)
    table = jnp.dot(fields, chosen.astype(BF16).T, preferred_element_type=F32).astype(BF16)
    return table.reshape(2, 2, N_SRC, MOST).transpose(2, 0, 1, 3).reshape(LABELS, 2 * MOST)


def spread_kernel(rep_ref, left_ref, *refs):
    outs, turned = refs[:N_REP], refs[N_REP]
    for pair in range(4):
        tile = left_ref[2 * pair : 2 * pair + 2].reshape(2 * QUARTER, TILE)
        turned[pair] = tile.T
    for shift in range(N_REP):
        to = lax.rem(rep_ref[0] + shift, N_REP)
        first = pl.multiple_of(to * QUARTER, QUARTER)
        for pair in range(4):
            outs[shift][pair] = turned[pair, pl.ds(first, QUARTER), :]


def spread_rows(rep, left):
    return pl.pallas_call(
        spread_kernel,
        out_shape=[jax.ShapeDtypeStruct((4, QUARTER, 2 * QUARTER), BF16)] * N_REP,
        in_specs=[SMEM, VMEM],
        out_specs=[VMEM] * N_REP,
        scratch_shapes=[pltpu.VMEM((4, TILE, 2 * QUARTER), BF16)],
        name="spread_rows",
    )(rep, left.transpose(0, 2, 1))


def join_kernel(table_ref, *refs):
    parts, out_ref = refs[:N_REP], refs[N_REP]
    for pair in range(4):
        pieces = [part[pair] for part in parts]
        for side in range(2):
            first = (2 * pair + side) * QUARTER
            out_ref[first : first + QUARTER] = jnp.concatenate(
                [p[:, QUARTER * side : QUARTER * (side + 1)] for p in pieces], axis=1
            )
    out_ref[ROWS:BLOCK] = table_ref[...]


def join_k(table, parts):
    return pl.pallas_call(
        join_kernel,
        out_shape=jax.ShapeDtypeStruct((BLOCK, TILE), BF16),
        in_specs=[VMEM] * (N_REP + 1),
        out_specs=VMEM,
        name="join_k",
    )(table, *parts)


def sort_products(me, left, labels, lines, scalars, listed, sem):
    for block in range(N_SRC):
        labels[block] = left[block, ROWS:BLOCK].astype(F32)
    for block in range(N_SRC):
        first, second = labels[block, pl.ds(2 * me, 1), :], labels[block, pl.ds(2 * me + 1, 1), :]
        spot, a, b, rank = first[:, :MOST], first[:, MOST:], second[:, :MOST], second[:, MOST:]
        code = (spot - 1.0) * 512.0 + b * 8.0 + a + rank * 65536.0
        lines[block : block + 1, :] = jnp.where(spot > 0.0, code.astype(I32), HALF * 8)
    codes = lines[:N_SRC]
    tile = (codes >> 3) & 63
    lane = lax.broadcasted_iota(I32, (N_SRC, MOST), 1)
    sizes = jnp.zeros((N_SRC, MOST), F32)
    for b in range(HALF):
        size = jnp.sum((tile == b).astype(F32), axis=1, keepdims=True)
        sizes = jnp.where(lane == b, size, sizes)
    counts = jnp.sum(sizes, axis=1, keepdims=True)
    row = lax.broadcasted_iota(I32, (N_SRC, N_SRC), 0)
    column = lax.broadcasted_iota(I32, (N_SRC, N_SRC), 1)
    before = jnp.dot((column < row).astype(F32), sizes, precision=lax.Precision.HIGHEST)
    all_sizes = jnp.broadcast_to(jnp.sum(sizes, axis=0, keepdims=True), (8, MOST))
    groups = ((all_sizes.astype(I32) + GROUP - 1) // GROUP).astype(F32)
    row = lax.broadcasted_iota(I32, (MOST, MOST), 0)
    column = lax.broadcasted_iota(I32, (MOST, MOST), 1)
    starts = GROUP * jnp.dot(groups, (row < column).astype(F32), precision=lax.Precision.HIGHEST)
    base = jnp.where(lane < HALF, before + starts[:1], TRASH)
    lines[N_SRC : 2 * N_SRC] = base.astype(I32)
    lines[2 * N_SRC : 3 * N_SRC] = jnp.broadcast_to(counts, (N_SRC, MOST)).astype(I32)
    lines[3 * N_SRC : 3 * N_SRC + 8] = (starts + all_sizes).astype(I32)
    lines[3 * N_SRC + 8 : 3 * N_SRC + 16] = starts.astype(I32)
    copy = pltpu.make_async_copy(lines, scalars, sem)
    copy.start()
    copy.wait()
    total = scalars[3 * N_SRC + 8, HALF]
    for b in range(HALF):
        end = scalars[3 * N_SRC, b]
        for u in range(GROUP - 1):
            listed[end + u] = NOWHERE + b * 8
    for u in range(GROUP * WIDE):
        listed[total + u] = jnp.int32(NOWHERE)

    def one_source(block, carry):
        def some_products(i, carry):
            for u in range(8):
                code = scalars[block, i * 8 + u]
                to = scalars[N_SRC + block, (code >> 3) & 63] + (code >> 16)
                listed[to] = (code & 65535) + (block << 16)
            return carry

        return lax.fori_loop(0, (scalars[2 * N_SRC + block, 0] + 7) // 8, some_products, carry)

    lax.fori_loop(0, N_SRC, one_source, 0)
    return total


RIGHT_PLACES = [(quarter, first) for quarter in (0, 1, 3, 2) for first in (0, PART)]
N_RIGHT = len(RIGHT_PLACES)


def products_kernel(me_ref, *refs):
    lefts, rights, refs = refs[:N_SRC], refs[N_SRC : N_SRC + N_RIGHT], refs[N_SRC + N_RIGHT :]
    away_ref, home_ref, left, right, total, labels, lines, scalars, listed = refs[:9]
    left_sems, right_sems, lines_sem = refs[9:]
    copies = [
        pltpu.make_async_copy(lefts[i], left.at[i], left_sems.at[i]) for i in range(N_SRC)
    ]
    fetches = [
        pltpu.make_async_copy(rights[i], right.at[q, pl.ds(b, PART)], right_sems.at[i])
        for i, (q, b) in enumerate(RIGHT_PLACES)
    ]
    for copy in copies + fetches:
        copy.start()
    total[...] = jnp.zeros_like(total)
    for copy in copies:
        copy.wait()
    length = sort_products(me_ref[0], left, labels, lines, scalars, listed, lines_sem)
    for fetch in fetches:
        fetch.wait()

    def step(i, carry):
        sums = []
        for w in range(WIDE):
            spots, rows = [], []
            for u in range(GROUP):
                code = listed[(i * WIDE + w) * GROUP + u]
                first = pl.multiple_of((code & 7) * QUARTER, QUARTER)
                rows.append(left[code >> 16, pl.ds(first, QUARTER), :])
                spots.append((code >> 9) & 127)
                b = (code >> 3) & (HALF - 1)
            tile = jnp.concatenate([right[q, b] for q in range(N_REP)], axis=0)
            lhs = jnp.concatenate(rows, axis=0)
            sums.append((spots, jnp.dot(lhs, tile, preferred_element_type=F32)))
        for spots, value in sums:
            for u in range(GROUP):
                total[spots[u]] += value[u * QUARTER : (u + 1) * QUARTER]
        return carry

    lax.fori_loop(0, (length + GROUP * WIDE - 1) // (GROUP * WIDE), step, 0)
    home_ref[...] = total[:SPOTS].astype(BF16)
    away_ref[...] = total[SPOTS : 2 * SPOTS].astype(BF16)


def products(me, lefts, rights):
    shape = (SPOTS, QUARTER, TILE)
    return pl.pallas_call(
        products_kernel,
        out_shape=[jax.ShapeDtypeStruct(shape, BF16)] * 2,
        in_specs=[SMEM] + [ANY] * (N_SRC + N_RIGHT),
        out_specs=[VMEM] * 2,
        scratch_shapes=[
            pltpu.VMEM((N_SRC, BLOCK, TILE), BF16),
            pltpu.VMEM((N_REP, HALF, QUARTER, TILE), BF16),
            pltpu.VMEM((2 * SPOTS + 1, QUARTER, TILE), F32),
            pltpu.VMEM((N_SRC, LABELS, TILE), F32),
            pltpu.VMEM((4 * N_SRC, MOST), I32),
            pltpu.SMEM((4 * N_SRC, MOST), I32),
            pltpu.SMEM((LIST,), I32),
            pltpu.SemaphoreType.DMA((N_SRC,)),
            pltpu.SemaphoreType.DMA((N_RIGHT,)),
            pltpu.SemaphoreType.DMA,
        ],
        compiler_params=pltpu.CompilerParams(vmem_limit_bytes=VMEM_LIMIT),
        cost_estimate=pl.CostEstimate(
            flops=2 * 384 * 64 * 256 * 256, bytes_accessed=10 << 20, transcendentals=0
        ),
        name="products",
    )(me, *lefts, *rights)


def shift_by(value, axis, size, step):
    return lax.ppermute(value, axis, [(i, (i + step) % size) for i in range(size)])


def apart(value):
    perm = []
    for i in range(N_Z):
        perm.append((i * 2, ((i + 1) % N_Z) * 2))
        perm.append((i * 2 + 1, ((i - 1) % N_Z) * 2 + 1))
    return lax.ppermute(value, ("z", "core"), perm)


def other_core(value):
    return lax.ppermute(value, "core", [(0, 1), (1, 0)])


def gather(mine, first, second):
    back_first, ahead_second = shift_by(first, "rep", N_REP, 1), shift_by(second, "rep", N_REP, -1)
    back_second, ahead_first = shift_by(second, "rep", N_REP, 1), shift_by(first, "rep", N_REP, -1)
    own, other = mine, other_core(mine)
    blocks = [own, other]
    for distance in range(1, 4):
        if distance == 3:
            own, other, back_first, ahead_second = lax.optimization_barrier(
                (own, other, back_first, ahead_second)
            )
        own, other = apart(own), apart(other)
        blocks += [own, other, other_core(own), other_core(other)]
    own = apart(own)
    far_first = shift_by(back_first, "rep", N_REP, 1)
    far_second = shift_by(ahead_second, "rep", N_REP, -1)
    rights = [
        first, second, back_first, back_second, ahead_first, ahead_second, far_first, far_second
    ]
    return blocks + [own, other_core(own)], rights


def body(amps, integrals, a_index, b_index, live, owner, target):
    rep, z, x, core = [lax.axis_index(n).astype(I32) for n in ("rep", "z", "x", "core")]
    pieces = spread_rows(rep[None], amps)
    first = lax.dynamic_slice_in_dim(integrals, core * HALF, PART, 0)
    second = lax.dynamic_slice_in_dim(integrals, core * HALF + PART, PART, 0)
    table = product_table(x, a_index, b_index, live, owner, target)
    parts = [pieces[0]] + [shift_by(pieces[s], "rep", N_REP, s) for s in range(1, N_REP)]
    first, second, *parts = lax.optimization_barrier((first, second, *parts))
    lefts, rights = gather(join_k(table, parts), first, second)
    away, home = products((z * N_CORE + core)[None], lefts, rights)
    sums = home.astype(F32) + other_core(away).astype(F32)
    sums = sums.reshape(N_X, OWN_DEV, QUARTER, TILE)
    total = sums[0]
    for step in range(1, N_X):
        total = total + shift_by(sums[step].astype(BF16), "x", N_X, step).astype(F32)
    return total


def solution(mesh):
    devices = mesh.devices.reshape(N_REP, N_Z, N_X, N_CORE)
    fine = Mesh(devices, ("rep", "z", "x", "core"))
    task = ("z", "x", "core")
    in_specs = (
        P(task, None, "rep"),
        P(None, "rep", None),
        P(task),
        P(task),
        P(task),
        P(task, None),
        P(task),
    )
    return jax.shard_map(
        body, mesh=fine, in_specs=in_specs, out_specs=P(task, "rep", None), check_vma=False
    )
```

time: 653 us -> 106 us (0.16)
  the two profiles are of different devices: /device:TPU:1 before, /device:TPU:56 now
where the time goes in v2:
time: 106 us; the launch traced here: 104 us
  waiting for transfers between devices  41.2 us (39%)
  starting transfers between devices  35.3 us (33%)
  Pallas kernels  17.2 us (16%)
  other arithmetic  5.11 us (5%)
  local copies, waits for them, and re-layouts  4.38 us (4%)
    ppermute x12, waiting for transfers between devices, shift_by(): lax.ppermute(value, axis, [(i, (i + step) % size) for i in range(size)])  30.4 us
    ppermute x12, starting transfers between devices, shift_by(): lax.ppermute(value, axis, [(i, (i + step) % size) for i in range(size)])  19.5 us
    pallas_call x1, Pallas kernels, products(): pl.pallas_call(products_kernel, out_shape=[jax.ShapeDtypeStruct(shape, BF...  13.6 us
    ppermute x7, starting transfers between devices, apart(): return lax.ppermute(value, ('z', 'core'), perm)  10.1 us
    ppermute x7, waiting for transfers between devices, apart(): return lax.ppermute(value, ('z', 'core'), perm)  8.28 us
    ppermute x9, starting transfers between devices, other_core(): return lax.ppermute(value, 'core', [(0, 1), (1, 0)])  5.71 us
    ppermute x9, waiting for transfers between devices, other_core(): return lax.ppermute(value, 'core', [(0, 1), (1, 0)])  2.52 us
    another operation x3, other arithmetic  2.37 us
  transfers between devices with their start and end apart: 28, of which 13 were waited for; matrix products, arithmetic and copies ran while one was open for 6% of the time, Pallas kernels for 0%

profile of v2, /device:TPU:56, one launch (start us, length us, event | category | flops | bytes accessed | tf_op | source)
XLA Modules:
  0.0 104.1 jit_solution(15356152939787136369)
XLA Ops:
  0.0 1.8 %spread_rows.1 = (bf16[4,64,128]{2,1,0:T(8,128)(2,1)}, bf16[4,64,128]{2,1,0:T(8,128)(2,1)}, bf16[4,64,128]{2,1,0:T(8,128)(2,1)}, bf16[4,64,128]{2,1,0:T(8,128)(2,1)}) custom-call(s32[1]{0:T(128)} %bitcast.4.rep_ref, bf16[8,64,256]{2,1,0:T(8,128)(2,1)} %bitcast.12), custom_call_target="tpu_custom_call" | custom-call | tf_op jit(solution)/shard_map/spread_rows/pallas_call | solution.py:71
  1.8 0.2 collective-permute-start
  2.1 2.6 %collective-permute-start.1 = (bf16[4,64,128]{2,1,0:T(8,128)(2,1)}, bf16[4,64,128]{2,1,0:T(8,128)(2,1)S(1)}, u32[]{:S(2)}, u32[]{:S(2)}) collective-permute-start(bf16[4,64,128]{2,1,0:T(8,128)(2,1)} %get-tuple-element.23), channel_id=1, source_target_pairs={{0,128},{64,192},{128,0},{192,64},{1,129},{65,193},{129,1},{193,65... | collective-permute-start | bytes 196616 | tf_op jit(solution)/shard_map/ppermute | solution.py:232
  4.6 0.0 collective-permute-start.2
  4.6 0.7 convert.22
  5.3 0.7 broadcast_in_dim.12
  6.1 0.1 reshape.26
  6.2 0.7 broadcast_in_dim.13
  6.9 0.1 reshape.27
  7.0 0.7 fusion.27
  7.7 1.1 %convert_reduce_fusion.1 = (s32[384]{0:T(512)S(1)}, s32[384]{0:T(512)S(1)}) fusion(s32[384]{0:T(512)} %param.10, s32[384]{0:T(512)S(1)} %get-tuple-element.39), kind=kLoop, calls=%fused_computation.6 | loop fusion | flops 1326336 | bytes 6144 | tf_op jit(solution)/shard_map/reduce_sum | solution.py:50
  8.8 0.6 fusion.1
  9.5 1.3 %constant_dynamic-slice_fusion = (bf16[16,64,256]{2,1,0:T(8,128)(2,1)S(1)}, bf16[16,64,256]{2,1,0:T(8,128)(2,1)S(1)}) fusion(bf16[64,64,256]{2,1,0:T(8,128)(2,1)} %param.8, s32[]{:T(128)S(6)} %select_n.53, s32[]{:T(128)S(6)} %select_n.52), kind=kLoop, calls=%fused_computation.61 | loop fusion | bytes 2097160 | tf_op jit(solution)/shard_map/dynamic_slice | solution.py:272
  10.8 0.0 copy-start.1
  10.8 0.7 copy.13
  11.5 0.0 collective-permute-done.2.refs_3_
  11.5 0.6 copy-done.2
  12.1 0.0 copy-done.3
  12.1 0.0 copy-done.4
  12.1 1.8 %join_k.1.refs_0_ = bf16[544,256]{1,0:T(8,128)(2,1)} custom-call(bf16[32,256]{1,0:T(8,128)(2,1)} %bitcast.13, bf16[4,64,128]{2,1,0:T(8,128)(2,1)} %get-tuple-element.25.refs_0_, bf16[4,64,128]{2,1,0:T(8,128)(2,1)} %copy-done.2, bf16[4,64,128]{2,1,0:T(8,128)(2,1)} %copy-done.3, bf16[4,64,128]{2,1,0:T(8,128)(2,1)} %copy-done.4), custom_call_target="tpu_custom_call" | custom-call | tf_op jit(solution)/shard_map/join_k/pallas_call | solution.py:94
  13.9 0.0 collective-permute-start.3
  13.9 3.2 %collective-permute-start.12 = (bf16[16,64,256]{2,1,0:T(8,128)(2,1)S(1)}, bf16[16,64,256]{2,1,0:T(8,128)(2,1)S(1)}, u32[]{:S(2)}, u32[]{:S(2)}) collective-permute-start(bf16[16,64,256]{2,1,0:T(8,128)(2,1)S(1)} %get-tuple-element.29.refs_16_), channel_id=1, source_target_pairs={{0,64},{64,128},{128,192},{192,0},{1,65},{65,129},{129,193},{193,1... | collective-permute-start | bytes 1572872 | tf_op jit(solution)/shard_map/ppermute | solution.py:232
  17.2 1.9 %collective-permute-start.4 = (bf16[544,256]{1,0:T(8,128)(2,1)}, bf16[544,256]{1,0:T(8,128)(2,1)S(1)}, u32[]{:S(2)}, u32[]{:S(2)}) collective-permute-start(bf16[544,256]{1,0:T(8,128)(2,1)} %join_k.1.refs_0_), channel_id=1, source_target_pairs={{0,8},{1,57},{8,16},{9,1},{16,24},{17,9},{24,32},{25,17},{32,40},{... | collective-permute-start | bytes 835592 | tf_op jit(solution)/shard_map/ppermute | solution.py:240
  19.1 0.0 collective-permute-done.3.refs_1_
  19.1 1.9 %collective-permute-start.5 = (bf16[544,256]{1,0:T(8,128)(2,1)S(1)}, bf16[544,256]{1,0:T(8,128)(2,1)S(1)}, u32[]{:S(2)}, u32[]{:S(2)}) collective-permute-start(bf16[544,256]{1,0:T(8,128)(2,1)S(1)} %collective-permute-done.3.refs_1_), channel_id=1, source_target_pairs={{0,8},{1,57},{8,16},{9,1},{16,24},{17,9},{24,32},{25,17},{32,40},{... | collective-permute-start | bytes 835592 | tf_op jit(solution)/shard_map/ppermute | solution.py:240
  21.0 0.0 collective-permute-start.13
  21.0 0.1 collective-permute-start.21
  21.1 2.8 %collective-permute-done.4.refs_2_ = bf16[544,256]{1,0:T(8,128)(2,1)S(1)} collective-permute-done((bf16[544,256]{1,0:T(8,128)(2,1)}, bf16[544,256]{1,0:T(8,128)(2,1)S(1)}, u32[]{:S(2)}, u32[]{:S(2)}) %collective-permute-start.4) | collective-permute-done | bytes 278560 | tf_op jit(solution)/shard_map/ppermute | solution.py:240
  23.9 1.9 %collective-permute-start.8 = (bf16[544,256]{1,0:T(8,128)(2,1)S(1)}, bf16[544,256]{1,0:T(8,128)(2,1)S(1)}, u32[]{:S(2)}, u32[]{:S(2)}) collective-permute-start(bf16[544,256]{1,0:T(8,128)(2,1)S(1)} %collective-permute-done.4.refs_2_), channel_id=1, source_target_pairs={{0,8},{1,57},{8,16},{9,1},{16,24},{17,9},{24,32},{25,17},{32,40},{... | collective-permute-start | bytes 835592 | tf_op jit(solution)/shard_map/ppermute | solution.py:240
  25.8 1.1 %collective-permute-done.5.refs_3_ = bf16[544,256]{1,0:T(8,128)(2,1)S(1)} collective-permute-done((bf16[544,256]{1,0:T(8,128)(2,1)S(1)}, bf16[544,256]{1,0:T(8,128)(2,1)S(1)}, u32[]{:S(2)}, u32[]{:S(2)}) %collective-permute-start.5) | collective-permute-done | bytes 278560 | tf_op jit(solution)/shard_map/ppermute | solution.py:240
  26.9 1.9 %collective-permute-start.9 = (bf16[544,256]{1,0:T(8,128)(2,1)S(1)}, bf16[544,256]{1,0:T(8,128)(2,1)S(1)}, u32[]{:S(2)}, u32[]{:S(2)}) collective-permute-start(bf16[544,256]{1,0:T(8,128)(2,1)S(1)} %collective-permute-done.5.refs_3_), channel_id=1, source_target_pairs={{0,8},{1,57},{8,16},{9,1},{16,24},{17,9},{24,32},{25,17},{32,40},{... | collective-permute-start | bytes 835592 | tf_op jit(solution)/shard_map/ppermute | solution.py:240
  28.8 0.2 collective-permute-done.12.refs_18_
  29.0 3.7 %collective-permute-start.20 = (bf16[16,64,256]{2,1,0:T(8,128)(2,1)S(1)}, bf16[16,64,256]{2,1,0:T(8,128)(2,1)S(1)}, u32[]{:S(2)}, u32[]{:S(2)}) collective-permute-start(bf16[16,64,256]{2,1,0:T(8,128)(2,1)S(1)} %get-tuple-element.30.refs_17_), channel_id=1, source_target_pairs={{0,64},{64,128},{128,192},{192,0},{1,65},{65,129},{129,193},{193,1... | collective-permute-start | bytes 1572872 | tf_op jit(solution)/shard_map/ppermute | solution.py:232
  32.7 3.5 %collective-permute-done.13.refs_21_ = bf16[16,64,256]{2,1,0:T(8,128)(2,1)S(1)} collective-permute-done((bf16[16,64,256]{2,1,0:T(8,128)(2,1)S(1)}, bf16[16,64,256]{2,1,0:T(8,128)(2,1)S(1)}, u32[]{:S(2)}, u32[]{:S(2)}) %collective-permute-start.13) | collective-permute-done | bytes 524320 | tf_op jit(solution)/shard_map/ppermute | solution.py:232
  36.2 1.7 %collective-permute-start.6 = (bf16[544,256]{1,0:T(8,128)(2,1)S(1)}, bf16[544,256]{1,0:T(8,128)(2,1)S(1)}, u32[]{:S(2)}, u32[]{:S(2)}) collective-permute-start(bf16[544,256]{1,0:T(8,128)(2,1)S(1)} %collective-permute-done.4.refs_2_), channel_id=1, source_target_pairs={{0,1},{1,0},{2,3},{3,2},{4,5},{5,4},{6,7},{7,6},{8,9},{9,8},{10,11... | collective-permute-start | bytes 835592 | tf_op jit(solution)/shard_map/ppermute | solution.py:244
  37.9 0.0 collective-permute-done.8.refs_6_
  37.9 0.0 collective-permute-done.9.refs_7_
  37.9 2.3 %collective-permute-start.14 = (bf16[544,256]{1,0:T(8,128)(2,1)S(1)}, bf16[544,256]{1,0:T(8,128)(2,1)}, u32[]{:S(2)}, u32[]{:S(2)}) collective-permute-start(bf16[544,256]{1,0:T(8,128)(2,1)S(1)} %collective-permute-done.8.refs_6_), channel_id=1, source_target_pairs={{0,8},{1,57},{8,16},{9,1},{16,24},{17,9},{24,32},{25,17},{32,40},{... | collective-permute-start | bytes 835592 | tf_op jit(solution)/shard_map/ppermute | solution.py:240
  40.3 0.0 collective-permute-start.10
  40.3 7.2 %collective-permute-done.21.refs_20_ = bf16[16,64,256]{2,1,0:T(8,128)(2,1)S(1)} collective-permute-done((bf16[16,64,256]{2,1,0:T(8,128)(2,1)S(1)}, bf16[16,64,256]{2,1,0:T(8,128)(2,1)S(1)}, u32[]{:S(2)}, u32[]{:S(2)}) %collective-permute-start.21) | collective-permute-done | bytes 524320 | tf_op jit(solution)/shard_map/ppermute | solution.py:232
  47.4 0.6 collective-permute-start.7
  48.1 0.1 collective-permute-start.11
  48.2 0.0 collective-permute-start.15
  48.2 0.1 collective-permute-start.18
  48.3 3.1 %collective-permute-start.22 = (bf16[16,64,256]{2,1,0:T(8,128)(2,1)S(1)}, bf16[16,64,256]{2,1,0:T(8,128)(2,1)}, u32[]{:S(2)}, u32[]{:S(2)}) collective-permute-start(bf16[16,64,256]{2,1,0:T(8,128)(2,1)S(1)} %collective-permute-done.12.refs_18_), channel_id=1, source_target_pairs={{0,64},{64,128},{128,192},{192,0},{1,65},{65,129},{129,193},{193,1... | collective-permute-start | bytes 1572872 | tf_op jit(solution)/shard_map/ppermute | solution.py:232
  51.4 0.0 collective-permute-done.7.refs_5_
  51.4 0.1 collective-permute-start.23
  51.6 1.8 %collective-permute-start.16 = (bf16[544,256]{1,0:T(8,128)(2,1)}, bf16[544,256]{1,0:T(8,128)(2,1)}, u32[]{:S(2)}, u32[]{:S(2)}) collective-permute-start(bf16[544,256]{1,0:T(8,128)(2,1)} %collective-permute-done.14.refs_10_), channel_id=1, source_target_pairs={{0,1},{1,0},{2,3},{3,2},{4,5},{5,4},{6,7},{7,6},{8,9},{9,8},{10,11... | collective-permute-start | bytes 835592 | tf_op jit(solution)/shard_map/ppermute | solution.py:244
  53.4 1.5 %collective-permute-done.15.refs_11_ = bf16[544,256]{1,0:T(8,128)(2,1)} collective-permute-done((bf16[544,256]{1,0:T(8,128)(2,1)S(1)}, bf16[544,256]{1,0:T(8,128)(2,1)}, u32[]{:S(2)}, u32[]{:S(2)}) %collective-permute-start.15) | collective-permute-done | bytes 278560 | tf_op jit(solution)/shard_map/ppermute | solution.py:240
  54.8 3.0 %collective-permute-done.18.refs_14_ = bf16[544,256]{1,0:T(8,128)(2,1)} collective-permute-done((bf16[544,256]{1,0:T(8,128)(2,1)}, bf16[544,256]{1,0:T(8,128)(2,1)}, u32[]{:S(2)}, u32[]{:S(2)}) %collective-permute-start.18) | collective-permute-done | bytes 278560 | tf_op jit(solution)/shard_map/ppermute | solution.py:240
  57.8 4.9 %collective-permute-done.22.refs_22_ = bf16[16,64,256]{2,1,0:T(8,128)(2,1)} collective-permute-done((bf16[16,64,256]{2,1,0:T(8,128)(2,1)S(1)}, bf16[16,64,256]{2,1,0:T(8,128)(2,1)}, u32[]{:S(2)}, u32[]{:S(2)}) %collective-permute-start.22) | collective-permute-done | bytes 524320 | tf_op jit(solution)/shard_map/ppermute | solution.py:232
  62.7 4.2 %collective-permute-done.23.refs_23_ = bf16[16,64,256]{2,1,0:T(8,128)(2,1)} collective-permute-done((bf16[16,64,256]{2,1,0:T(8,128)(2,1)S(1)}, bf16[16,64,256]{2,1,0:T(8,128)(2,1)}, u32[]{:S(2)}, u32[]{:S(2)}) %collective-permute-start.23) | collective-permute-done | bytes 524320 | tf_op jit(solution)/shard_map/ppermute | solution.py:232
  67.0 13.6 %products.1 = (bf16[32,64,256]{2,1,0:T(8,128)(2,1)}, bf16[32,64,256]{2,1,0:T(8,128)(2,1)}) custom-call(s32[1]{0:T(128)} %bitcast.me_ref, bf16[544,256]{1,0:T(8,128)(2,1)} %join_k.1.refs_0_, bf16[544,256]{1,0:T(8,128)(2,1)} %copy-done.9, bf16[544,256]{1,0:T(8,128)(2,1)} %copy-done.10, bf16[544,256]{1,0:T(8,128)(2,1)} %copy-done.11, ...), custom_call_target="tpu_custom_call" | custom-call | flops 3221225472 | bytes 10485760 | tf_op jit(solution)/shard_map/products/pallas_call | solution.py:206
  80.6 1.5 %collective-permute-start.24 = (bf16[32,64,256]{2,1,0:T(8,128)(2,1)}, bf16[32,64,256]{2,1,0:T(8,128)(2,1)S(1)}, u32[]{:S(2)}, u32[]{:S(2)}) collective-permute-start(bf16[32,64,256]{2,1,0:T(8,128)(2,1)} %get-tuple-element.36), channel_id=1, source_target_pairs={{0,1},{1,0},{2,3},{3,2},{4,5},{5,4},{6,7},{7,6},{8,9},{9,8},{10,11... | collective-permute-start | bytes 3145736 | tf_op jit(solution)/shard_map/ppermute | solution.py:244
  82.1 2.5 %collective-permute-done.24 = bf16[32,64,256]{2,1,0:T(8,128)(2,1)S(1)} collective-permute-done((bf16[32,64,256]{2,1,0:T(8,128)(2,1)}, bf16[32,64,256]{2,1,0:T(8,128)(2,1)S(1)}, u32[]{:S(2)}, u32[]{:S(2)}) %collective-permute-start.24) | collective-permute-done | bytes 1048608 | tf_op jit(solution)/shard_map/ppermute | solution.py:244
  84.6 1.7 %fusion.31 = (bf16[32,64,256]{2,1,0:T(8,128)(2,1)S(1)}, f32[32,64,256]{2,1,0:T(8,128)S(1)}) fusion(bf16[32,64,256]{2,1,0:T(8,128)(2,1)S(1)} %collective-permute-done.24, bf16[32,64,256]{2,1,0:T(8,128)(2,1)} %get-tuple-element.35), kind=kLoop, calls=%fused_computation.64 | loop fusion | flops 2097152 | bytes 5242880 | tf_op jit(solution)/shard_map/convert.2
  86.2 0.1 fusion.32
  86.3 0.7 collective-permute-start.25
  87.1 2.6 %collective-permute-start.27 = (bf16[8,64,256]{2,1,0:T(8,128)(2,1)S(1)}, bf16[8,64,256]{2,1,0:T(8,128)(2,1)S(1)}, u32[]{:S(2)}, u32[]{:S(2)}) collective-permute-start(bf16[8,64,256]{2,1,0:T(8,128)(2,1)S(1)} %get-tuple-element.46), channel_id=1, source_target_pairs={{0,6},{2,0},{4,2},{6,4},{1,7},{3,1},{5,3},{7,5},{8,14},{10,8},{12,... | collective-permute-start | bytes 786440 | tf_op jit(solution)/shard_map/ppermute | solution.py:232
  89.7 3.1 %collective-permute-start.26 = (bf16[8,64,256]{2,1,0:T(8,128)(2,1)S(1)}, bf16[8,64,256]{2,1,0:T(8,128)(2,1)S(1)}, u32[]{:S(2)}, u32[]{:S(2)}) collective-permute-start(bf16[8,64,256]{2,1,0:T(8,128)(2,1)S(1)} %get-tuple-element.47), channel_id=1, source_target_pairs={{0,4},{2,6},{4,0},{6,2},{1,5},{3,7},{5,1},{7,3},{8,12},{10,14},{12... | collective-permute-start | bytes 786440 | tf_op jit(solution)/shard_map/ppermute | solution.py:232
  92.8 3.4 %collective-permute-done.25 = bf16[8,64,256]{2,1,0:T(8,128)(2,1)S(1)} collective-permute-done((bf16[8,64,256]{2,1,0:T(8,128)(2,1)S(1)}, bf16[8,64,256]{2,1,0:T(8,128)(2,1)S(1)}, u32[]{:S(2)}, u32[]{:S(2)}) %collective-permute-start.25) | collective-permute-done | bytes 262176 | tf_op jit(solution)/shard_map/ppermute | solution.py:232
  96.2 1.6 %collective-permute-done.27 = bf16[8,64,256]{2,1,0:T(8,128)(2,1)S(1)} collective-permute-done((bf16[8,64,256]{2,1,0:T(8,128)(2,1)S(1)}, bf16[8,64,256]{2,1,0:T(8,128)(2,1)S(1)}, u32[]{:S(2)}, u32[]{:S(2)}) %collective-permute-start.27) | collective-permute-done | bytes 262176 | tf_op jit(solution)/shard_map/ppermute | solution.py:232
  97.8 5.4 %collective-permute-done.26 = bf16[8,64,256]{2,1,0:T(8,128)(2,1)S(1)} collective-permute-done((bf16[8,64,256]{2,1,0:T(8,128)(2,1)S(1)}, bf16[8,64,256]{2,1,0:T(8,128)(2,1)S(1)}, u32[]{:S(2)}, u32[]{:S(2)}) %collective-permute-start.26) | collective-permute-done | bytes 262176 | tf_op jit(solution)/shard_map/ppermute | solution.py:232
  103.2 0.9 fusion.5
  (50 shorter events, 0.1 us)
Async XLA Ops:
  1.8 9.6 %collective-permute-start = (bf16[4,64,128]{2,1,0:T(8,128)(2,1)}, bf16[4,64,128]{2,1,0:T(8,128)(2,1)S(1)}, u32[]{:S(2)}, u32[]{:S(2)}) collective-permute-start(bf16[4,64,128]{2,1,0:T(8,128)(2,1)} %get-tuple-element.22), channel_id=1, source_target_pairs={{0,64},{64,128},{128,192},{192,0},{1,65},{65,129},{129,193},{193,1... | collective-permute-start | bytes 196616 | tf_op jit(solution)/shard_map/ppermute | solution.py:232
  2.1 9.4 %collective-permute-start.1 = (bf16[4,64,128]{2,1,0:T(8,128)(2,1)}, bf16[4,64,128]{2,1,0:T(8,128)(2,1)S(1)}, u32[]{:S(2)}, u32[]{:S(2)}) collective-permute-start(bf16[4,64,128]{2,1,0:T(8,128)(2,1)} %get-tuple-element.23), channel_id=1, source_target_pairs={{0,128},{64,192},{128,0},{192,64},{1,129},{65,193},{129,1},{193,65... | collective-permute-start | bytes 196616 | tf_op jit(solution)/shard_map/ppermute | solution.py:232
  4.6 6.8 %collective-permute-start.2 = (bf16[4,64,128]{2,1,0:T(8,128)(2,1)}, bf16[4,64,128]{2,1,0:T(8,128)(2,1)S(1)}, u32[]{:S(2)}, u32[]{:S(2)}) collective-permute-start(bf16[4,64,128]{2,1,0:T(8,128)(2,1)} %get-tuple-element.24), channel_id=1, source_target_pairs={{0,192},{64,0},{128,64},{192,128},{1,193},{65,1},{129,65},{193,129... | collective-permute-start | bytes 196616 | tf_op jit(solution)/shard_map/ppermute | solution.py:232
  10.7 56.2 %copy-start = (bf16[16,64,256]{2,1,0:T(8,128)(2,1)}, bf16[16,64,256]{2,1,0:T(8,128)(2,1)S(1)}, u32[]{:S(2)}) copy-start(bf16[16,64,256]{2,1,0:T(8,128)(2,1)S(1)} %get-tuple-element.30.refs_17_) | copy-start | bytes 1572868
  10.8 56.2 %copy-start.1 = (bf16[16,64,256]{2,1,0:T(8,128)(2,1)}, bf16[16,64,256]{2,1,0:T(8,128)(2,1)S(1)}, u32[]{:S(2)}) copy-start(bf16[16,64,256]{2,1,0:T(8,128)(2,1)S(1)} %get-tuple-element.29.refs_16_) | copy-start | bytes 1572868
  11.4 0.6 copy-start.2
  11.5 0.7 copy-start.3
  11.5 0.7 copy-start.4
  13.9 5.2 %collective-permute-start.3 = (bf16[544,256]{1,0:T(8,128)(2,1)}, bf16[544,256]{1,0:T(8,128)(2,1)S(1)}, u32[]{:S(2)}, u32[]{:S(2)}) collective-permute-start(bf16[544,256]{1,0:T(8,128)(2,1)} %join_k.1.refs_0_), channel_id=1, source_target_pairs={{0,1},{1,0},{2,3},{3,2},{4,5},{5,4},{6,7},{7,6},{8,9},{9,8},{10,11... | collective-permute-start | bytes 835592 | tf_op jit(solution)/shard_map/ppermute | solution.py:244
  13.9 15.1 %collective-permute-start.12 = (bf16[16,64,256]{2,1,0:T(8,128)(2,1)S(1)}, bf16[16,64,256]{2,1,0:T(8,128)(2,1)S(1)}, u32[]{:S(2)}, u32[]{:S(2)}) collective-permute-start(bf16[16,64,256]{2,1,0:T(8,128)(2,1)S(1)} %get-tuple-element.29.refs_16_), channel_id=1, source_target_pairs={{0,64},{64,128},{128,192},{192,0},{1,65},{65,129},{129,193},{193,1... | collective-permute-start | bytes 1572872 | tf_op jit(solution)/shard_map/ppermute | solution.py:232
  17.2 6.8 %collective-permute-start.4 = (bf16[544,256]{1,0:T(8,128)(2,1)}, bf16[544,256]{1,0:T(8,128)(2,1)S(1)}, u32[]{:S(2)}, u32[]{:S(2)}) collective-permute-start(bf16[544,256]{1,0:T(8,128)(2,1)} %join_k.1.refs_0_), channel_id=1, source_target_pairs={{0,8},{1,57},{8,16},{9,1},{16,24},{17,9},{24,32},{25,17},{32,40},{... | collective-permute-start | bytes 835592 | tf_op jit(solution)/shard_map/ppermute | solution.py:240
  19.1 47.9 %copy-start.9 = (bf16[544,256]{1,0:T(8,128)(2,1)}, bf16[544,256]{1,0:T(8,128)(2,1)S(1)}, u32[]{:S(2)}) copy-start(bf16[544,256]{1,0:T(8,128)(2,1)S(1)} %collective-permute-done.3.refs_1_) | copy-start | bytes 835588
  19.1 7.8 %collective-permute-start.5 = (bf16[544,256]{1,0:T(8,128)(2,1)S(1)}, bf16[544,256]{1,0:T(8,128)(2,1)S(1)}, u32[]{:S(2)}, u32[]{:S(2)}) collective-permute-start(bf16[544,256]{1,0:T(8,128)(2,1)S(1)} %collective-permute-done.3.refs_1_), channel_id=1, source_target_pairs={{0,8},{1,57},{8,16},{9,1},{16,24},{17,9},{24,32},{25,17},{32,40},{... | collective-permute-start | bytes 835592 | tf_op jit(solution)/shard_map/ppermute | solution.py:240
  21.0 15.2 %collective-permute-start.13 = (bf16[16,64,256]{2,1,0:T(8,128)(2,1)S(1)}, bf16[16,64,256]{2,1,0:T(8,128)(2,1)S(1)}, u32[]{:S(2)}, u32[]{:S(2)}) collective-permute-start(bf16[16,64,256]{2,1,0:T(8,128)(2,1)S(1)} %get-tuple-element.30.refs_17_), channel_id=1, source_target_pairs={{0,192},{64,0},{128,64},{192,128},{1,193},{65,1},{129,65},{193,129... | collective-permute-start | bytes 1572872 | tf_op jit(solution)/shard_map/ppermute | solution.py:232
  21.0 26.4 %collective-permute-start.21 = (bf16[16,64,256]{2,1,0:T(8,128)(2,1)S(1)}, bf16[16,64,256]{2,1,0:T(8,128)(2,1)S(1)}, u32[]{:S(2)}, u32[]{:S(2)}) collective-permute-start(bf16[16,64,256]{2,1,0:T(8,128)(2,1)S(1)} %get-tuple-element.29.refs_16_), channel_id=1, source_target_pairs={{0,192},{64,0},{128,64},{192,128},{1,193},{65,1},{129,65},{193,129... | collective-permute-start | bytes 1572872 | tf_op jit(solution)/shard_map/ppermute | solution.py:232
  23.9 27.5 %copy-start.10 = (bf16[544,256]{1,0:T(8,128)(2,1)}, bf16[544,256]{1,0:T(8,128)(2,1)S(1)}, u32[]{:S(2)}) copy-start(bf16[544,256]{1,0:T(8,128)(2,1)S(1)} %collective-permute-done.4.refs_2_) | copy-start | bytes 835588
  23.9 14.0 %collective-permute-start.8 = (bf16[544,256]{1,0:T(8,128)(2,1)S(1)}, bf16[544,256]{1,0:T(8,128)(2,1)S(1)}, u32[]{:S(2)}, u32[]{:S(2)}) collective-permute-start(bf16[544,256]{1,0:T(8,128)(2,1)S(1)} %collective-permute-done.4.refs_2_), channel_id=1, source_target_pairs={{0,8},{1,57},{8,16},{9,1},{16,24},{17,9},{24,32},{25,17},{32,40},{... | collective-permute-start | bytes 835592 | tf_op jit(solution)/shard_map/ppermute | solution.py:240
  26.9 24.5 %copy-start.11 = (bf16[544,256]{1,0:T(8,128)(2,1)}, bf16[544,256]{1,0:T(8,128)(2,1)S(1)}, u32[]{:S(2)}) copy-start(bf16[544,256]{1,0:T(8,128)(2,1)S(1)} %collective-permute-done.5.refs_3_) | copy-start | bytes 835588
  26.9 11.0 %collective-permute-start.9 = (bf16[544,256]{1,0:T(8,128)(2,1)S(1)}, bf16[544,256]{1,0:T(8,128)(2,1)S(1)}, u32[]{:S(2)}, u32[]{:S(2)}) collective-permute-start(bf16[544,256]{1,0:T(8,128)(2,1)S(1)} %collective-permute-done.5.refs_3_), channel_id=1, source_target_pairs={{0,8},{1,57},{8,16},{9,1},{16,24},{17,9},{24,32},{25,17},{32,40},{... | collective-permute-start | bytes 835592 | tf_op jit(solution)/shard_map/ppermute | solution.py:240
  29.0 38.0 %copy-start.5 = (bf16[16,64,256]{2,1,0:T(8,128)(2,1)}, bf16[16,64,256]{2,1,0:T(8,128)(2,1)S(1)}, u32[]{:S(2)}) copy-start(bf16[16,64,256]{2,1,0:T(8,128)(2,1)S(1)} %collective-permute-done.12.refs_18_) | copy-start | bytes 1572868
  29.0 19.1 %collective-permute-start.20 = (bf16[16,64,256]{2,1,0:T(8,128)(2,1)S(1)}, bf16[16,64,256]{2,1,0:T(8,128)(2,1)S(1)}, u32[]{:S(2)}, u32[]{:S(2)}) collective-permute-start(bf16[16,64,256]{2,1,0:T(8,128)(2,1)S(1)} %get-tuple-element.30.refs_17_), channel_id=1, source_target_pairs={{0,64},{64,128},{128,192},{192,0},{1,65},{65,129},{129,193},{193,1... | collective-permute-start | bytes 1572872 | tf_op jit(solution)/shard_map/ppermute | solution.py:232
  36.2 30.8 %copy-start.6 = (bf16[16,64,256]{2,1,0:T(8,128)(2,1)}, bf16[16,64,256]{2,1,0:T(8,128)(2,1)S(1)}, u32[]{:S(2)}) copy-start(bf16[16,64,256]{2,1,0:T(8,128)(2,1)S(1)} %collective-permute-done.13.refs_21_) | copy-start | bytes 1572868
  36.2 12.0 %collective-permute-start.6 = (bf16[544,256]{1,0:T(8,128)(2,1)S(1)}, bf16[544,256]{1,0:T(8,128)(2,1)S(1)}, u32[]{:S(2)}, u32[]{:S(2)}) collective-permute-start(bf16[544,256]{1,0:T(8,128)(2,1)S(1)} %collective-permute-done.4.refs_2_), channel_id=1, source_target_pairs={{0,1},{1,0},{2,3},{3,2},{4,5},{5,4},{6,7},{7,6},{8,9},{9,8},{10,11... | collective-permute-start | bytes 835592 | tf_op jit(solution)/shard_map/ppermute | solution.py:244
  37.9 13.6 %copy-start.12 = (bf16[544,256]{1,0:T(8,128)(2,1)}, bf16[544,256]{1,0:T(8,128)(2,1)S(1)}, u32[]{:S(2)}) copy-start(bf16[544,256]{1,0:T(8,128)(2,1)S(1)} %collective-permute-done.8.refs_6_) | copy-start | bytes 835588
  37.9 13.6 %copy-start.13 = (bf16[544,256]{1,0:T(8,128)(2,1)}, bf16[544,256]{1,0:T(8,128)(2,1)S(1)}, u32[]{:S(2)}) copy-start(bf16[544,256]{1,0:T(8,128)(2,1)S(1)} %collective-permute-done.9.refs_7_) | copy-start | bytes 835588
  37.9 10.3 %collective-permute-start.14 = (bf16[544,256]{1,0:T(8,128)(2,1)S(1)}, bf16[544,256]{1,0:T(8,128)(2,1)}, u32[]{:S(2)}, u32[]{:S(2)}) collective-permute-start(bf16[544,256]{1,0:T(8,128)(2,1)S(1)} %collective-permute-done.8.refs_6_), channel_id=1, source_target_pairs={{0,8},{1,57},{8,16},{9,1},{16,24},{17,9},{24,32},{25,17},{32,40},{... | collective-permute-start | bytes 835592 | tf_op jit(solution)/shard_map/ppermute | solution.py:240
  40.3 8.0 %collective-permute-start.10 = (bf16[544,256]{1,0:T(8,128)(2,1)S(1)}, bf16[544,256]{1,0:T(8,128)(2,1)S(1)}, u32[]{:S(2)}, u32[]{:S(2)}) collective-permute-start(bf16[544,256]{1,0:T(8,128)(2,1)S(1)} %collective-permute-done.8.refs_6_), channel_id=1, source_target_pairs={{0,1},{1,0},{2,3},{3,2},{4,5},{5,4},{6,7},{7,6},{8,9},{9,8},{10,11... | collective-permute-start | bytes 835592 | tf_op jit(solution)/shard_map/ppermute | solution.py:244
  47.4 19.5 %copy-start.7 = (bf16[16,64,256]{2,1,0:T(8,128)(2,1)}, bf16[16,64,256]{2,1,0:T(8,128)(2,1)S(1)}, u32[]{:S(2)}) copy-start(bf16[16,64,256]{2,1,0:T(8,128)(2,1)S(1)} %collective-permute-done.21.refs_20_) | copy-start | bytes 1572868
  47.4 4.0 %collective-permute-start.7 = (bf16[544,256]{1,0:T(8,128)(2,1)S(1)}, bf16[544,256]{1,0:T(8,128)(2,1)S(1)}, u32[]{:S(2)}, u32[]{:S(2)}) collective-permute-start(bf16[544,256]{1,0:T(8,128)(2,1)S(1)} %collective-permute-done.5.refs_3_), channel_id=1, source_target_pairs={{0,1},{1,0},{2,3},{3,2},{4,5},{5,4},{6,7},{7,6},{8,9},{9,8},{10,11... | collective-permute-start | bytes 835592 | tf_op jit(solution)/shard_map/ppermute | solution.py:244
  48.1 18.9 %copy-start.8 = (bf16[16,64,256]{2,1,0:T(8,128)(2,1)}, bf16[16,64,256]{2,1,0:T(8,128)(2,1)S(1)}, u32[]{:S(2)}) copy-start(bf16[16,64,256]{2,1,0:T(8,128)(2,1)S(1)} %collective-permute-done.20.refs_19_) | copy-start | bytes 1572868
  48.1 3.5 %collective-permute-start.11 = (bf16[544,256]{1,0:T(8,128)(2,1)S(1)}, bf16[544,256]{1,0:T(8,128)(2,1)S(1)}, u32[]{:S(2)}, u32[]{:S(2)}) collective-permute-start(bf16[544,256]{1,0:T(8,128)(2,1)S(1)} %collective-permute-done.9.refs_7_), channel_id=1, source_target_pairs={{0,1},{1,0},{2,3},{3,2},{4,5},{5,4},{6,7},{7,6},{8,9},{9,8},{10,11... | collective-permute-start | bytes 835592 | tf_op jit(solution)/shard_map/ppermute | solution.py:244
  48.2 6.7 %copy-start.14 = (bf16[544,256]{1,0:T(8,128)(2,1)}, bf16[544,256]{1,0:T(8,128)(2,1)S(1)}, u32[]{:S(2)}) copy-start(bf16[544,256]{1,0:T(8,128)(2,1)S(1)} %collective-permute-done.6.refs_4_) | copy-start | bytes 835588
  48.2 6.7 %collective-permute-start.15 = (bf16[544,256]{1,0:T(8,128)(2,1)S(1)}, bf16[544,256]{1,0:T(8,128)(2,1)}, u32[]{:S(2)}, u32[]{:S(2)}) collective-permute-start(bf16[544,256]{1,0:T(8,128)(2,1)S(1)} %collective-permute-done.9.refs_7_), channel_id=1, source_target_pairs={{0,8},{1,57},{8,16},{9,1},{16,24},{17,9},{24,32},{25,17},{32,40},{... | collective-permute-start | bytes 835592 | tf_op jit(solution)/shard_map/ppermute | solution.py:240
  48.2 9.6 %collective-permute-start.18 = (bf16[544,256]{1,0:T(8,128)(2,1)}, bf16[544,256]{1,0:T(8,128)(2,1)}, u32[]{:S(2)}, u32[]{:S(2)}) collective-permute-start(bf16[544,256]{1,0:T(8,128)(2,1)} %collective-permute-done.14.refs_10_), channel_id=1, source_target_pairs={{0,8},{1,57},{8,16},{9,1},{16,24},{17,9},{24,32},{25,17},{32,40},{... | collective-permute-start | bytes 835592 | tf_op jit(solution)/shard_map/ppermute | solution.py:240
  48.3 6.5 %copy-start.15 = (bf16[544,256]{1,0:T(8,128)(2,1)}, bf16[544,256]{1,0:T(8,128)(2,1)S(1)}, u32[]{:S(2)}) copy-start(bf16[544,256]{1,0:T(8,128)(2,1)S(1)} %collective-permute-done.10.refs_8_) | copy-start | bytes 835588
  48.3 14.4 %collective-permute-start.22 = (bf16[16,64,256]{2,1,0:T(8,128)(2,1)S(1)}, bf16[16,64,256]{2,1,0:T(8,128)(2,1)}, u32[]{:S(2)}, u32[]{:S(2)}) collective-permute-start(bf16[16,64,256]{2,1,0:T(8,128)(2,1)S(1)} %collective-permute-done.12.refs_18_), channel_id=1, source_target_pairs={{0,64},{64,128},{128,192},{192,0},{1,65},{65,129},{129,193},{193,1... | collective-permute-start | bytes 1572872 | tf_op jit(solution)/shard_map/ppermute | solution.py:232
  51.4 6.4 %copy-start.16 = (bf16[544,256]{1,0:T(8,128)(2,1)}, bf16[544,256]{1,0:T(8,128)(2,1)S(1)}, u32[]{:S(2)}) copy-start(bf16[544,256]{1,0:T(8,128)(2,1)S(1)} %collective-permute-done.7.refs_5_) | copy-start | bytes 835588
  51.4 15.5 %collective-permute-start.23 = (bf16[16,64,256]{2,1,0:T(8,128)(2,1)S(1)}, bf16[16,64,256]{2,1,0:T(8,128)(2,1)}, u32[]{:S(2)}, u32[]{:S(2)}) collective-permute-start(bf16[16,64,256]{2,1,0:T(8,128)(2,1)S(1)} %collective-permute-done.13.refs_21_), channel_id=1, source_target_pairs={{0,192},{64,0},{128,64},{192,128},{1,193},{65,1},{129,65},{193,129... | collective-permute-start | bytes 1572872 | tf_op jit(solution)/shard_map/ppermute | solution.py:232
  51.6 6.3 %copy-start.17 = (bf16[544,256]{1,0:T(8,128)(2,1)}, bf16[544,256]{1,0:T(8,128)(2,1)S(1)}, u32[]{:S(2)}) copy-start(bf16[544,256]{1,0:T(8,128)(2,1)S(1)} %collective-permute-done.11.refs_9_) | copy-start | bytes 835588
  51.6 15.4 %collective-permute-start.16 = (bf16[544,256]{1,0:T(8,128)(2,1)}, bf16[544,256]{1,0:T(8,128)(2,1)}, u32[]{:S(2)}, u32[]{:S(2)}) collective-permute-start(bf16[544,256]{1,0:T(8,128)(2,1)} %collective-permute-done.14.refs_10_), channel_id=1, source_target_pairs={{0,1},{1,0},{2,3},{3,2},{4,5},{5,4},{6,7},{7,6},{8,9},{9,8},{10,11... | collective-permute-start | bytes 835592 | tf_op jit(solution)/shard_map/ppermute | solution.py:244
  54.8 12.1 %collective-permute-start.17 = (bf16[544,256]{1,0:T(8,128)(2,1)}, bf16[544,256]{1,0:T(8,128)(2,1)}, u32[]{:S(2)}, u32[]{:S(2)}) collective-permute-start(bf16[544,256]{1,0:T(8,128)(2,1)} %collective-permute-done.15.refs_11_), channel_id=1, source_target_pairs={{0,1},{1,0},{2,3},{3,2},{4,5},{5,4},{6,7},{7,6},{8,9},{9,8},{10,11... | collective-permute-start | bytes 835592 | tf_op jit(solution)/shard_map/ppermute | solution.py:244
  57.8 9.1 %collective-permute-start.19 = (bf16[544,256]{1,0:T(8,128)(2,1)}, bf16[544,256]{1,0:T(8,128)(2,1)}, u32[]{:S(2)}, u32[]{:S(2)}) collective-permute-start(bf16[544,256]{1,0:T(8,128)(2,1)} %collective-permute-done.18.refs_14_), channel_id=1, source_target_pairs={{0,1},{1,0},{2,3},{3,2},{4,5},{5,4},{6,7},{7,6},{8,9},{9,8},{10,11... | collective-permute-start | bytes 835592 | tf_op jit(solution)/shard_map/ppermute | solution.py:244
  80.6 4.0 %collective-permute-start.24 = (bf16[32,64,256]{2,1,0:T(8,128)(2,1)}, bf16[32,64,256]{2,1,0:T(8,128)(2,1)S(1)}, u32[]{:S(2)}, u32[]{:S(2)}) collective-permute-start(bf16[32,64,256]{2,1,0:T(8,128)(2,1)} %get-tuple-element.36), channel_id=1, source_target_pairs={{0,1},{1,0},{2,3},{3,2},{4,5},{5,4},{6,7},{7,6},{8,9},{9,8},{10,11... | collective-permute-start | bytes 3145736 | tf_op jit(solution)/shard_map/ppermute | solution.py:244
  86.3 9.9 %collective-permute-start.25 = (bf16[8,64,256]{2,1,0:T(8,128)(2,1)S(1)}, bf16[8,64,256]{2,1,0:T(8,128)(2,1)S(1)}, u32[]{:S(2)}, u32[]{:S(2)}) collective-permute-start(bf16[8,64,256]{2,1,0:T(8,128)(2,1)S(1)} %get-tuple-element.45), channel_id=1, source_target_pairs={{0,2},{2,4},{4,6},{6,0},{1,3},{3,5},{5,7},{7,1},{8,10},{10,12},{12... | collective-permute-start | bytes 786440 | tf_op jit(solution)/shard_map/ppermute | solution.py:232
  87.1 10.7 %collective-permute-start.27 = (bf16[8,64,256]{2,1,0:T(8,128)(2,1)S(1)}, bf16[8,64,256]{2,1,0:T(8,128)(2,1)S(1)}, u32[]{:S(2)}, u32[]{:S(2)}) collective-permute-start(bf16[8,64,256]{2,1,0:T(8,128)(2,1)S(1)} %get-tuple-element.46), channel_id=1, source_target_pairs={{0,6},{2,0},{4,2},{6,4},{1,7},{3,1},{5,3},{7,5},{8,14},{10,8},{12,... | collective-permute-start | bytes 786440 | tf_op jit(solution)/shard_map/ppermute | solution.py:232
  89.7 13.5 %collective-permute-start.26 = (bf16[8,64,256]{2,1,0:T(8,128)(2,1)S(1)}, bf16[8,64,256]{2,1,0:T(8,128)(2,1)S(1)}, u32[]{:S(2)}, u32[]{:S(2)}) collective-permute-start(bf16[8,64,256]{2,1,0:T(8,128)(2,1)S(1)} %get-tuple-element.47), channel_id=1, source_target_pairs={{0,4},{2,6},{4,0},{6,2},{1,5},{3,7},{5,1},{7,3},{8,12},{10,14},{12... | collective-permute-start | bytes 786440 | tf_op jit(solution)/shard_map/ppermute | solution.py:232

commit v3 on v2

v3 whole, which is shorter than its diff:
```python
import jax
import jax.numpy as jnp
from jax import lax
from jax.experimental import pallas as pl
from jax.experimental.pallas import tpu as pltpu
from jax.sharding import Mesh
from jax.sharding import PartitionSpec as P

N_REP, N_Z, N_X, N_CORE = 4, 8, 4, 2
N_SRC = N_Z
A_DEV = 8
OWN_DEV = 8
TPS = 8
NB = 64
HALF = NB // 2
QUARTER = 64
TILE = 256
MOST = 128
LABELS = 2 * N_Z
SPOTS = N_X * OWN_DEV
GROUP = 4
WIDE = 8
LIST = 1280
NOWHERE = 2.0 * SPOTS * 4096
SORT_COST = 10**10
ROWS = A_DEV * QUARTER
BLOCK = ROWS + LABELS
TABLE_COST = 4 * 10**9
VMEM_LIMIT = 56 * 1024 * 1024
BF16 = jnp.bfloat16
F32 = jnp.float32
I32 = jnp.int32
VMEM = pl.BlockSpec(memory_space=pltpu.VMEM)
SMEM = pl.BlockSpec(memory_space=pltpu.SMEM)
ANY = pl.BlockSpec(memory_space=pl.ANY)


def table_kernel(x_ref, a_ref, b_ref, live_ref, owner_ref, target_ref, out_ref, lines):
    products, slots = a_ref.shape[0], owner_ref.shape[0]
    x = x_ref[0]
    row = lax.broadcasted_iota(I32, (8, slots), 0)
    named = jnp.where(row == 0, owner_ref[...][None], jnp.where(row == 1, target_ref[...][None], 0))
    slot = lax.broadcasted_iota(I32, (slots, products), 0)
    spread = lax.broadcasted_iota(I32, (slots, products), 1) // TPS == slot
    named = jnp.dot(named.astype(F32), spread.astype(F32), precision=lax.Precision.HIGHEST)
    own, target = named[0:1].astype(I32), named[1:2].astype(I32)
    a, b = a_ref[...][None], b_ref[...][None]
    place = jnp.where(live_ref[...][None] > 0, own // (N_X * N_CORE), -1)
    spot = own % N_CORE * SPOTS + ((own // N_CORE - x) & (N_X - 1)) * OWN_DEV + target + 1
    row = lax.broadcasted_iota(I32, (8, products), 0)
    turned = jnp.where(row == 0, place, b).astype(F32).T
    same = turned[:, 0:1] == place.astype(F32)
    order = lax.broadcasted_iota(I32, (products, products), 0)
    same = same & (order < lax.broadcasted_iota(I32, (products, products), 1))
    alike = same & (turned[:, 1:2] == b.astype(F32))
    standing = jnp.sum(same.astype(F32), axis=0, keepdims=True).astype(I32)
    rank = jnp.sum(alike.astype(F32), axis=0, keepdims=True).astype(I32)
    at = jnp.where(place >= 0, place * MOST + standing, -1)
    fields = jnp.where(row == 0, spot, jnp.where(row == 1, a, jnp.where(row == 2, b, rank)))
    fields = fields.astype(F32).astype(BF16)
    position = lax.broadcasted_iota(I32, (MOST, products), 0)
    for place in range(N_Z):
        chosen = (at == position + place * MOST).astype(F32).astype(BF16)
        found = lax.dot_general(
            fields, chosen, (((1,), (1,)), ((), ())), preferred_element_type=F32
        )
        lines[2 * place : 2 * place + 1, :MOST] = found[0:1]
        lines[2 * place : 2 * place + 1, MOST:] = found[1:2]
        lines[2 * place + 1 : 2 * place + 2, :MOST] = found[2:3]
        lines[2 * place + 1 : 2 * place + 2, MOST:] = found[3:4]
    out_ref[...] = lines[...].astype(BF16)


def product_table(x, a_index, b_index, live, owner, target):
    lists = [a_index, b_index, live, owner[:, 0], target]
    return pl.pallas_call(
        table_kernel,
        out_shape=jax.ShapeDtypeStruct((LABELS, 2 * MOST), BF16),
        in_specs=[SMEM] + [VMEM] * 5,
        out_specs=VMEM,
        scratch_shapes=[pltpu.VMEM((LABELS, 2 * MOST), F32)],
        cost_estimate=pl.CostEstimate(flops=TABLE_COST, bytes_accessed=1 << 16, transcendentals=0),
        name="product_table",
    )(x, *lists)


def spread_kernel(rep_ref, left_ref, *refs):
    outs, turned = refs[:N_REP], refs[N_REP]
    for pair in range(4):
        tile = left_ref[2 * pair : 2 * pair + 2].reshape(2 * QUARTER, TILE)
        turned[pair] = tile.T
    for shift in range(N_REP):
        to = lax.rem(rep_ref[0] + shift, N_REP)
        first = pl.multiple_of(to * QUARTER, QUARTER)
        for pair in range(4):
            outs[shift][pair] = turned[pair, pl.ds(first, QUARTER), :]


def spread_rows(rep, left):
    return pl.pallas_call(
        spread_kernel,
        out_shape=[jax.ShapeDtypeStruct((4, QUARTER, 2 * QUARTER), BF16)] * N_REP,
        in_specs=[SMEM, VMEM],
        out_specs=[VMEM] * N_REP,
        scratch_shapes=[pltpu.VMEM((4, TILE, 2 * QUARTER), BF16)],
        name="spread_rows",
    )(rep, left.transpose(0, 2, 1))


def join_kernel(table_ref, *refs):
    parts, out_ref = refs[:N_REP], refs[N_REP]
    for pair in range(4):
        pieces = [part[pair] for part in parts]
        for side in range(2):
            first = (2 * pair + side) * QUARTER
            out_ref[first : first + QUARTER] = jnp.concatenate(
                [p[:, QUARTER * side : QUARTER * (side + 1)] for p in pieces], axis=1
            )
    out_ref[ROWS:BLOCK] = table_ref[...]


def join_k(table, parts):
    return pl.pallas_call(
        join_kernel,
        out_shape=jax.ShapeDtypeStruct((BLOCK, TILE), BF16),
        in_specs=[VMEM] * (N_REP + 1),
        out_specs=VMEM,
        name="join_k",
    )(table, *parts)


def exact_dot(left, right):
    return jnp.dot(left.astype(F32).astype(BF16), right, preferred_element_type=F32)


def sort_kernel(me_ref, *refs):
    lefts, listed, fetched, labels, sems = refs[:N_SRC], *refs[N_SRC:]
    me = me_ref[0]
    tables = [
        pltpu.make_async_copy(lefts[i].at[pl.ds(ROWS, LABELS)], fetched.at[i], sems.at[i])
        for i in range(N_SRC)
    ]
    for copy in tables:
        copy.start()
    for copy in tables:
        copy.wait()
    labels[...] = fetched[...].astype(F32)
    rows = [labels[i, pl.ds(2 * me + half, 1), :] for half in range(2) for i in range(N_SRC)]
    first = jnp.concatenate(rows[:N_SRC], axis=0)
    second = jnp.concatenate(rows[N_SRC:], axis=0)
    spot, a, b, rank = first[:, :MOST], first[:, MOST:], second[:, :MOST], second[:, MOST:]
    lane = lax.broadcasted_iota(I32, (MOST, MOST), 1)
    row = lax.broadcasted_iota(I32, (MOST, MOST), 0)
    lane_f = lane.astype(F32)
    tile = jnp.where(spot > 0.0, b, float(NB)).T
    rank = rank.T
    of_tile = [(tile[:, i : i + 1] == lane_f).astype(F32).astype(BF16) for i in range(N_SRC)]
    ones = jnp.ones((N_SRC, MOST), F32)
    source = lax.broadcasted_iota(I32, (N_SRC, MOST), 0)
    sizes = jnp.zeros((N_SRC, MOST), F32)
    for i in range(N_SRC):
        sizes = jnp.where(source == i, exact_dot(ones, of_tile[i]), sizes)
    before, below = jnp.zeros((N_SRC, MOST), F32), jnp.zeros((1, MOST), F32)
    for i in range(N_SRC):
        before = jnp.where(source == i, below, before)
        below = below + sizes[i : i + 1]
    groups = jnp.floor((below + (GROUP - 1)) * (1.0 / GROUP))
    groups = jnp.where(lane[:1] < NB, groups, 0.0)
    high = jnp.floor(groups * (1.0 / 128.0))
    earlier = (row < lane).astype(F32).astype(BF16)
    starts = exact_dot(jnp.broadcast_to(groups - 128.0 * high, (N_SRC, MOST)), earlier)
    starts += 128.0 * exact_dot(jnp.broadcast_to(high, (N_SRC, MOST)), earlier)
    starts = GROUP * starts
    base = jnp.where(lane[:N_SRC] < NB, before + starts, 2.0 * LIST)
    high = jnp.floor(base * (1.0 / 128.0))
    low, high = (base - 128.0 * high).T, high.T
    places, fields = [], []
    for i in range(N_SRC):
        place = 128.0 * jnp.dot(of_tile[i], high.astype(BF16), preferred_element_type=F32)
        place += jnp.dot(of_tile[i], low.astype(BF16), preferred_element_type=F32)
        places.append(place[:, i : i + 1] + rank[:, i : i + 1])
        field = jnp.where(source == 0, spot[i : i + 1] - 1.0, a[i : i + 1] + 8.0 * i)
        field = jnp.where(source == 2, b[i : i + 1], field)
        fields.append(jnp.where(source == 3, 1.0, field).astype(BF16))
    for line in range(LIST // MOST):
        found = jnp.zeros((N_SRC, MOST), F32)
        for i in range(N_SRC):
            here = (places[i] == lane_f + float(line * MOST)).astype(F32).astype(BF16)
            found += jnp.dot(fields[i], here, preferred_element_type=F32)
        code = found[0:1] * 4096.0 + found[1:2] * 64.0 + found[2:3]
        code = jnp.where(found[3:4] > 0.0, code, NOWHERE)
        listed[line : line + 1, :] = code.astype(I32)
    listed[LIST // MOST : LIST // MOST + 1, :] = starts[:1].astype(I32)


def sort_products(me, lefts):
    return pl.pallas_call(
        sort_kernel,
        out_shape=jax.ShapeDtypeStruct((LIST // MOST + 1, MOST), I32),
        in_specs=[SMEM] + [ANY] * N_SRC,
        out_specs=VMEM,
        scratch_shapes=[
            pltpu.VMEM((N_SRC, LABELS, TILE), BF16),
            pltpu.VMEM((N_SRC, LABELS, TILE), F32),
            pltpu.SemaphoreType.DMA((N_SRC,)),
        ],
        cost_estimate=pl.CostEstimate(flops=SORT_COST, bytes_accessed=1 << 16, transcendentals=0),
        name="sort_products",
    )(me, *lefts)


N_RIGHT = 9


def products_kernel(me_ref, listed, *refs):
    lefts, rights, refs = refs[:N_SRC], refs[N_SRC : N_SRC + N_RIGHT], refs[N_SRC + N_RIGHT :]
    away_ref, home_ref, left, right, total, left_sems, right_sems = refs
    core = me_ref[1]
    copies = [
        pltpu.make_async_copy(lefts[i].at[pl.ds(0, ROWS)], left.at[i], left_sems.at[i])
        for i in range(N_SRC)
    ]
    copies.append(pltpu.make_async_copy(rights[0], right.at[0], right_sems.at[0]))
    i = 1
    for first in (core * HALF, (1 - core) * HALF):
        for quarter, skip, size in ((1, 0, HALF), (3, 0, HALF), (2, 0, HALF // 2), (2, HALF // 2, HALF // 2)):
            spot = right.at[quarter, pl.ds(pl.multiple_of(first + skip, HALF // 2), size)]
            copies.append(pltpu.make_async_copy(rights[i], spot, right_sems.at[i]))
            i += 1
    for copy in copies:
        copy.start()
    total[...] = jnp.zeros_like(total)
    for copy in copies:
        copy.wait()

    def step(i, carry):
        sums = []
        for w in range(WIDE):
            spots, rows = [], []
            for u in range(GROUP):
                at = (i % 4) * GROUP * WIDE + w * GROUP + u
                code = listed[i // 4, at]
                first = pl.multiple_of(((code >> 6) & 7) * QUARTER, QUARTER)
                rows.append(left[(code >> 9) & 7, pl.ds(first, QUARTER), :])
                spots.append(code >> 12)
                b = code & (NB - 1) if u == 0 else b
            tile = jnp.concatenate([right[q, b] for q in range(N_REP)], axis=0)
            lhs = jnp.concatenate(rows, axis=0)
            sums.append((spots, jnp.dot(lhs, tile, preferred_element_type=F32)))
        for spots, value in sums:
            for u in range(GROUP):
                total[spots[u]] += value[u * QUARTER : (u + 1) * QUARTER]
        return carry

    lax.fori_loop(0, (listed[LIST // MOST, NB] + GROUP * WIDE - 1) // (GROUP * WIDE), step, 0)
    home_ref[...] = total[pl.ds(pl.multiple_of(core * SPOTS, SPOTS), SPOTS)].astype(BF16)
    away_ref[...] = total[pl.ds(pl.multiple_of((1 - core) * SPOTS, SPOTS), SPOTS)].astype(BF16)


def products(me, listed, lefts, rights):
    shape = (SPOTS, QUARTER, TILE)
    return pl.pallas_call(
        products_kernel,
        out_shape=[jax.ShapeDtypeStruct(shape, BF16)] * 2,
        in_specs=[SMEM] * 2 + [ANY] * (N_SRC + N_RIGHT),
        out_specs=[VMEM] * 2,
        scratch_shapes=[
            pltpu.VMEM((N_SRC, ROWS, TILE), BF16),
            pltpu.VMEM((N_REP, NB, QUARTER, TILE), BF16),
            pltpu.VMEM((2 * SPOTS + 1, QUARTER, TILE), F32),
            pltpu.SemaphoreType.DMA((N_SRC,)),
            pltpu.SemaphoreType.DMA((N_RIGHT,)),
        ],
        compiler_params=pltpu.CompilerParams(vmem_limit_bytes=VMEM_LIMIT),
        cost_estimate=pl.CostEstimate(
            flops=2 * 384 * 64 * 256 * 256, bytes_accessed=10 << 20, transcendentals=0
        ),
        name="products",
    )(me, listed, *lefts, *rights)


def shift_by(value, axis, size, step):
    return lax.ppermute(value, axis, [(i, (i + step) % size) for i in range(size)])


def apart(value, axis, size):
    perm = []
    for i in range(size):
        perm.append((i * 2, ((i + 1) % size) * 2))
        perm.append((i * 2 + 1, ((i - 1) % size) * 2 + 1))
    return lax.ppermute(value, (axis, "core"), perm)


def other_core(value):
    return lax.ppermute(value, "core", [(0, 1), (1, 0)])


def gather(mine, half):
    back = shift_by(half, "rep", N_REP, 1)
    ahead = shift_by(half, "rep", N_REP, -1)
    own, other = mine, other_core(mine)
    blocks = [own]
    for distance in range(3):
        own, other = apart(own, "z", N_Z), apart(other, "z", N_Z)
        blocks += [own, other]
    far_back = shift_by(back[: HALF // 2], "rep", N_REP, 1)
    far_ahead = shift_by(ahead[HALF // 2 :], "rep", N_REP, -1)
    parts = [back, ahead, far_back, far_ahead]
    return blocks + [apart(own, "z", N_Z)], parts + [other_core(part) for part in parts]


def body(amps, integrals, a_index, b_index, live, owner, target):
    rep, z, x, core = [lax.axis_index(n).astype(I32) for n in ("rep", "z", "x", "core")]
    x, *pieces = lax.optimization_barrier((x, *spread_rows(rep[None], amps)))
    half = lax.dynamic_slice_in_dim(integrals, core * HALF, HALF, 0)
    table = product_table(x[None], a_index, b_index, live, owner, target)
    parts = [pieces[0]] + [shift_by(pieces[s], "rep", N_REP, s) for s in range(1, N_REP)]
    half, table, *parts = lax.optimization_barrier((half, table, *parts))
    lefts, rights = gather(join_k(table, parts), half)
    me = jnp.stack([z, core])
    away, home = products(me, sort_products(me, lefts), lefts, [integrals] + rights)
    sums = home.astype(F32) + other_core(away).astype(F32)
    sums = sums.reshape(N_X, OWN_DEV, QUARTER, TILE)
    total = sums[0]
    for step in range(1, N_X):
        total = total + shift_by(sums[step].astype(BF16), "x", N_X, step).astype(F32)
    return total


def solution(mesh):
    devices = mesh.devices.reshape(N_REP, N_Z, N_X, N_CORE)
    fine = Mesh(devices, ("rep", "z", "x", "core"))
    task = ("z", "x", "core")
    in_specs = (
        P(task, None, "rep"),
        P(None, "rep", None),
        P(task),
        P(task),
        P(task),
        P(task, None),
        P(task),
    )
    return jax.shard_map(
        body, mesh=fine, in_specs=in_specs, out_specs=P(task, "rep", None), check_vma=False
    )
```

time: 106 us -> 94.7 us (0.89)
  the two profiles are of different devices: /device:TPU:56 before, /device:TPU:1 now
where the time goes in v3:
time: 94.7 us; the launch traced here: 93.6 us
  starting transfers between devices  43.7 us (46%)
  Pallas kernels  22.3 us (24%)
  waiting for transfers between devices  21.9 us (23%)
  other arithmetic  3.24 us (3%)
  local copies, waits for them, and re-layouts  2.28 us (2%)
    ppermute x7, starting transfers between devices, apart(): return lax.ppermute(value, (axis, 'core'), perm)  19.8 us
    ppermute x10, waiting for transfers between devices, shift_by(): lax.ppermute(value, axis, [(i, (i + step) % size) for i in range(size)])  14.2 us
    ppermute x10, starting transfers between devices, shift_by(): lax.ppermute(value, axis, [(i, (i + step) % size) for i in range(size)])  14.1 us
    pallas_call x1, Pallas kernels, products(): pl.pallas_call(products_kernel, out_shape=[jax.ShapeDtypeStruct(shape, BF...  12.4 us
    ppermute x6, starting transfers between devices, other_core(): return lax.ppermute(value, 'core', [(0, 1), (1, 0)])  9.74 us
    ppermute x7, waiting for transfers between devices, apart(): return lax.ppermute(value, (axis, 'core'), perm)  4.83 us
    pallas_call x1, Pallas kernels, sort_products(): pl.pallas_call(sort_kernel, out_shape=jax.ShapeDtypeStruct((LIST // MOST...  3.92 us
    ppermute x6, waiting for transfers between devices, other_core(): return lax.ppermute(value, 'core', [(0, 1), (1, 0)])  2.86 us
  transfers between devices with their start and end apart: 23, of which 7 were waited for; matrix products, arithmetic and copies ran while one was open for 2% of the time, Pallas kernels for 9%

profile of v3, /device:TPU:1, one launch (start us, length us, event | category | flops | bytes accessed | tf_op | source)
XLA Modules:
  0.0 93.6 jit_solution(4205025742415148218)
XLA Ops:
  0.0 1.8 %spread_rows.1 = (bf16[4,64,128]{2,1,0:T(8,128)(2,1)}, bf16[4,64,128]{2,1,0:T(8,128)(2,1)}, bf16[4,64,128]{2,1,0:T(8,128)(2,1)}, bf16[4,64,128]{2,1,0:T(8,128)(2,1)}) custom-call(s32[1]{0:T(128)} %bitcast.2.rep_ref, bf16[8,64,256]{2,1,0:T(8,128)(2,1)} %bitcast.6), custom_call_target="tpu_custom_call" | custom-call | tf_op jit(solution)/shard_map/spread_rows/pallas_call | solution.py:100
  1.8 2.1 %collective-permute-start = (bf16[4,64,128]{2,1,0:T(8,128)(2,1)}, bf16[4,64,128]{2,1,0:T(8,128)(2,1)S(1)}, u32[]{:S(2)}, u32[]{:S(2)}) collective-permute-start(bf16[4,64,128]{2,1,0:T(8,128)(2,1)} %get-tuple-element.28), channel_id=1, source_target_pairs={{0,64},{64,128},{128,192},{192,0},{1,65},{65,129},{129,193},{193,1... | collective-permute-start | bytes 196616 | tf_op jit(solution)/shard_map/ppermute | solution.py:283
  3.9 2.6 %collective-permute-start.1 = (bf16[4,64,128]{2,1,0:T(8,128)(2,1)}, bf16[4,64,128]{2,1,0:T(8,128)(2,1)S(1)}, u32[]{:S(2)}, u32[]{:S(2)}) collective-permute-start(bf16[4,64,128]{2,1,0:T(8,128)(2,1)} %get-tuple-element.29), channel_id=1, source_target_pairs={{0,128},{64,192},{128,0},{192,64},{1,129},{65,193},{129,1},{193,65... | collective-permute-start | bytes 196616 | tf_op jit(solution)/shard_map/ppermute | solution.py:283
  6.6 1.1 %collective-permute-start.2 = (bf16[4,64,128]{2,1,0:T(8,128)(2,1)}, bf16[4,64,128]{2,1,0:T(8,128)(2,1)S(1)}, u32[]{:S(2)}, u32[]{:S(2)}) collective-permute-start(bf16[4,64,128]{2,1,0:T(8,128)(2,1)} %get-tuple-element.30), channel_id=1, source_target_pairs={{0,192},{64,0},{128,64},{192,128},{1,193},{65,1},{129,65},{193,129... | collective-permute-start | bytes 196616 | tf_op jit(solution)/shard_map/ppermute | solution.py:283
  7.6 2.4 %product_table.1.table_ref = bf16[16,256]{1,0:T(8,128)(2,1)} custom-call(s32[1]{0:T(128)} %bitcast.4.x_ref, s32[384]{0:T(512)} %a_ref.1, s32[384]{0:T(512)} %b_ref.1, s32[384]{0:T(512)} %live_ref.1, s32[48]{0:T(128)} %bitcast.7, s32[48]{0:T(128)} %target_ref.1), custom_call_target="tpu_custom_call" | custom-call | flops 4000000000 | bytes 65536 | tf_op jit(solution)/shard_map/product_table/pallas_call | solution.py:76
  10.0 0.1 constant_dynamic-slice_fusion
  10.1 0.0 collective-permute-done.refs_1_
  10.1 0.0 collective-permute-done.1.refs_2_
  10.2 0.0 collective-permute-done.2.refs_3_
  10.2 2.0 %collective-permute-start.12 = (bf16[32,64,256]{2,1,0:T(8,128)(2,1)S(1)}, bf16[32,64,256]{2,1,0:T(8,128)(2,1)S(1)}, u32[]{:S(2)}, u32[]{:S(2)}) collective-permute-start(bf16[32,64,256]{2,1,0:T(8,128)(2,1)S(1)} %constant_dynamic-slice_fusion), channel_id=1, source_target_pairs={{0,192},{64,0},{128,64},{192,128},{1,193},{65,1},{129,65},{193,129... | collective-permute-start | bytes 3145736 | tf_op jit(solution)/shard_map/ppermute | solution.py:283
  12.2 0.0 collective-permute-start.11
  12.2 0.0 copy-done.4
  12.2 1.8 %join_k.1.refs_0_ = bf16[528,256]{1,0:T(8,128)(2,1)} custom-call(bf16[16,256]{1,0:T(8,128)(2,1)} %product_table.1.table_ref, bf16[4,64,128]{2,1,0:T(8,128)(2,1)} %get-tuple-element.32.refs_0_, bf16[4,64,128]{2,1,0:T(8,128)(2,1)} %copy-done.2, bf16[4,64,128]{2,1,0:T(8,128)(2,1)} %copy-done.3, bf16[4,64,128]{2,1,0:T(8,128)(2,1)} %copy-done.4), custom_call_target="tpu_custom_call" | custom-call | tf_op jit(solution)/shard_map/join_k/pallas_call | solution.py:123
  14.0 2.8 %collective-permute-start.4 = (bf16[528,256]{1,0:T(8,128)(2,1)}, bf16[528,256]{1,0:T(8,128)(2,1)S(1)}, u32[]{:S(2)}, u32[]{:S(2)}) collective-permute-start(bf16[528,256]{1,0:T(8,128)(2,1)} %join_k.1.refs_0_), channel_id=1, source_target_pairs={{0,1},{1,0},{2,3},{3,2},{4,5},{5,4},{6,7},{7,6},{8,9},{9,8},{10,11... | collective-permute-start | bytes 811016 | tf_op jit(solution)/shard_map/ppermute | solution.py:295
  16.8 5.4 %collective-permute-start.3 = (bf16[528,256]{1,0:T(8,128)(2,1)}, bf16[528,256]{1,0:T(8,128)(2,1)S(1)}, u32[]{:S(2)}, u32[]{:S(2)}) collective-permute-start(bf16[528,256]{1,0:T(8,128)(2,1)} %join_k.1.refs_0_), channel_id=1, source_target_pairs={{0,8},{1,57},{8,16},{9,1},{16,24},{17,9},{24,32},{25,17},{32,40},{... | collective-permute-start | bytes 811016 | tf_op jit(solution)/shard_map/ppermute | solution.py:291
  22.3 0.0 collective-permute-done.4
  22.3 1.4 %collective-permute-start.5 = (bf16[528,256]{1,0:T(8,128)(2,1)S(1)}, bf16[528,256]{1,0:T(8,128)(2,1)S(1)}, u32[]{:S(2)}, u32[]{:S(2)}) collective-permute-start(bf16[528,256]{1,0:T(8,128)(2,1)S(1)} %collective-permute-done.4), channel_id=1, source_target_pairs={{0,8},{1,57},{8,16},{9,1},{16,24},{17,9},{24,32},{25,17},{32,40},{... | collective-permute-start | bytes 811016 | tf_op jit(solution)/shard_map/ppermute | solution.py:291
  23.6 2.3 %collective-permute-done.3.refs_1_ = bf16[528,256]{1,0:T(8,128)(2,1)S(1)} collective-permute-done((bf16[528,256]{1,0:T(8,128)(2,1)}, bf16[528,256]{1,0:T(8,128)(2,1)S(1)}, u32[]{:S(2)}, u32[]{:S(2)}) %collective-permute-start.3) | collective-permute-done | bytes 270368 | tf_op jit(solution)/shard_map/ppermute | solution.py:291
  26.0 3.4 %collective-permute-start.6 = (bf16[528,256]{1,0:T(8,128)(2,1)S(1)}, bf16[528,256]{1,0:T(8,128)(2,1)S(1)}, u32[]{:S(2)}, u32[]{:S(2)}) collective-permute-start(bf16[528,256]{1,0:T(8,128)(2,1)S(1)} %collective-permute-done.3.refs_1_), channel_id=1, source_target_pairs={{0,8},{1,57},{8,16},{9,1},{16,24},{17,9},{24,32},{25,17},{32,40},{... | collective-permute-start | bytes 811016 | tf_op jit(solution)/shard_map/ppermute | solution.py:291
  29.4 0.0 collective-permute-done.5.refs_2_
  29.4 2.9 %collective-permute-start.7 = (bf16[528,256]{1,0:T(8,128)(2,1)S(1)}, bf16[528,256]{1,0:T(8,128)(2,1)}, u32[]{:S(2)}, u32[]{:S(2)}) collective-permute-start(bf16[528,256]{1,0:T(8,128)(2,1)S(1)} %collective-permute-done.5.refs_2_), channel_id=1, source_target_pairs={{0,8},{1,57},{8,16},{9,1},{16,24},{17,9},{24,32},{25,17},{32,40},{... | collective-permute-start | bytes 811016 | tf_op jit(solution)/shard_map/ppermute | solution.py:291
  32.3 0.5 collective-permute-done.6.refs_3_
  32.8 3.5 %collective-permute-start.8 = (bf16[528,256]{1,0:T(8,128)(2,1)S(1)}, bf16[528,256]{1,0:T(8,128)(2,1)}, u32[]{:S(2)}, u32[]{:S(2)}) collective-permute-start(bf16[528,256]{1,0:T(8,128)(2,1)S(1)} %collective-permute-done.6.refs_3_), channel_id=1, source_target_pairs={{0,8},{1,57},{8,16},{9,1},{16,24},{17,9},{24,32},{25,17},{32,40},{... | collective-permute-start | bytes 811016 | tf_op jit(solution)/shard_map/ppermute | solution.py:291
  36.3 0.0 collective-permute-done.12.refs_10_
  36.4 2.8 %collective-permute-start.14 = (bf16[16,64,256]{2,1,0:T(8,128)(2,1)S(1)}, bf16[16,64,256]{2,1,0:T(8,128)(2,1)S(1)}, u32[]{:S(2)}, u32[]{:S(2)}) collective-permute-start(bf16[16,64,256]{2,1,0:T(8,128)(2,1)S(1)} %slice.32), channel_id=1, source_target_pairs={{0,192},{64,0},{128,64},{192,128},{1,193},{65,1},{129,65},{193,129... | collective-permute-start | bytes 1572872 | tf_op jit(solution)/shard_map/ppermute | solution.py:283
  39.2 0.0 collective-permute-done.11.refs_9_
  39.2 1.1 %slice.31 = bf16[16,64,256]{2,1,0:T(8,128)(2,1)S(1)} slice(bf16[32,64,256]{2,1,0:T(8,128)(2,1)} %collective-permute-done.11.refs_9_), slice={[0:16], [0:64], [0:256]} | slice | bytes 1048576 | tf_op jit(solution)/shard_map/slice | solution.py:306
  40.3 0.1 collective-permute-start.13
  40.4 0.0 collective-permute-done.7.refs_4_
  40.4 2.5 %collective-permute-start.9 = (bf16[528,256]{1,0:T(8,128)(2,1)}, bf16[528,256]{1,0:T(8,128)(2,1)}, u32[]{:S(2)}, u32[]{:S(2)}) collective-permute-start(bf16[528,256]{1,0:T(8,128)(2,1)} %collective-permute-done.7.refs_4_), channel_id=1, source_target_pairs={{0,8},{1,57},{8,16},{9,1},{16,24},{17,9},{24,32},{25,17},{32,40},{... | collective-permute-start | bytes 811016 | tf_op jit(solution)/shard_map/ppermute | solution.py:291
  42.8 0.0 collective-permute-done.8.refs_5_
  42.8 0.7 collective-permute-start.10
  43.6 1.0 %collective-permute-start.16 = (bf16[32,64,256]{2,1,0:T(8,128)(2,1)S(1)}, bf16[32,64,256]{2,1,0:T(8,128)(2,1)}, u32[]{:S(2)}, u32[]{:S(2)}) collective-permute-start(bf16[32,64,256]{2,1,0:T(8,128)(2,1)S(1)} %collective-permute-done.12.refs_10_), channel_id=1, source_target_pairs={{0,1},{1,0},{2,3},{3,2},{4,5},{5,4},{6,7},{7,6},{8,9},{9,8},{10,11... | collective-permute-start | bytes 3145736 | tf_op jit(solution)/shard_map/ppermute | solution.py:295
  44.6 2.0 %collective-permute-done.9.refs_6_ = bf16[528,256]{1,0:T(8,128)(2,1)} collective-permute-done((bf16[528,256]{1,0:T(8,128)(2,1)}, bf16[528,256]{1,0:T(8,128)(2,1)}, u32[]{:S(2)}, u32[]{:S(2)}) %collective-permute-start.9) | collective-permute-done | bytes 270368 | tf_op jit(solution)/shard_map/ppermute | solution.py:291
  46.6 4.8 %collective-permute-start.15 = (bf16[32,64,256]{2,1,0:T(8,128)(2,1)}, bf16[32,64,256]{2,1,0:T(8,128)(2,1)}, u32[]{:S(2)}, u32[]{:S(2)}) collective-permute-start(bf16[32,64,256]{2,1,0:T(8,128)(2,1)} %collective-permute-done.11.refs_9_), channel_id=1, source_target_pairs={{0,1},{1,0},{2,3},{3,2},{4,5},{5,4},{6,7},{7,6},{8,9},{9,8},{10,11... | collective-permute-start | bytes 3145736 | tf_op jit(solution)/shard_map/ppermute | solution.py:295
  51.4 0.6 pad_add_fusion.me_ref
  52.0 0.0 collective-permute-done.14.refs_12_
  52.0 0.0 collective-permute-start.18
  52.0 2.9 %collective-permute-done.13.refs_11_ = bf16[16,64,256]{2,1,0:T(8,128)(2,1)S(1)} collective-permute-done((bf16[16,64,256]{2,1,0:T(8,128)(2,1)S(1)}, bf16[16,64,256]{2,1,0:T(8,128)(2,1)S(1)}, u32[]{:S(2)}, u32[]{:S(2)}) %collective-permute-start.13) | collective-permute-done | bytes 524320 | tf_op jit(solution)/shard_map/ppermute | solution.py:283
  54.9 1.0 %collective-permute-start.17 = (bf16[16,64,256]{2,1,0:T(8,128)(2,1)S(1)}, bf16[16,64,256]{2,1,0:T(8,128)(2,1)S(1)}, u32[]{:S(2)}, u32[]{:S(2)}) collective-permute-start(bf16[16,64,256]{2,1,0:T(8,128)(2,1)S(1)} %collective-permute-done.13.refs_11_), channel_id=1, source_target_pairs={{0,1},{1,0},{2,3},{3,2},{4,5},{5,4},{6,7},{7,6},{8,9},{9,8},{10,11... | collective-permute-start | bytes 1572872 | tf_op jit(solution)/shard_map/ppermute | solution.py:295
  55.9 0.0 collective-permute-done.10.refs_7_
  55.9 3.9 %sort_products.1.listed = s32[11,128]{1,0:T(8,128)} custom-call(s32[2]{0:T(128)} %pad_add_fusion.me_ref, bf16[528,256]{1,0:T(8,128)(2,1)} %join_k.1.refs_0_, bf16[528,256]{1,0:T(8,128)(2,1)} %copy-done.9, bf16[528,256]{1,0:T(8,128)(2,1)} %copy-done.10, bf16[528,256]{1,0:T(8,128)(2,1)} %copy-done.11, bf16[528,256]{1,0:T(8,128)(2,1)} %collective-permute-done.7.refs_4_, ...), custom_call_target="tpu_custom_call" | custom-call | flops 10000000000 | bytes 65536 | tf_op jit(solution)/shard_map/sort_products/pallas_call | solution.py:197
  59.8 0.0 copy-done.1
  59.8 0.0 copy-done.5
  59.8 0.0 copy-done.6
  59.8 0.0 collective-permute-done.18.refs_16_
  59.9 0.0 collective-permute-done.16.refs_14_
  59.9 0.0 collective-permute-done.17.refs_15_
  59.9 0.0 copy-start.8
  59.9 0.0 collective-permute-done.15.refs_13_
  59.9 0.8 copy-done.7
  60.7 0.2 copy-done.8
  60.9 12.4 %products.1 = (bf16[32,64,256]{2,1,0:T(8,128)(2,1)}, bf16[32,64,256]{2,1,0:T(8,128)(2,1)}) custom-call(s32[2]{0:T(128)} %pad_add_fusion.me_ref, s32[11,128]{1,0:T(8,128)} %sort_products.1.listed, bf16[528,256]{1,0:T(8,128)(2,1)} %join_k.1.refs_0_, bf16[528,256]{1,0:T(8,128)(2,1)} %copy-done.9, bf16[528,256]{1,0:T(8,128)(2,1)} %copy-done.10, ...), custom_call_target="tpu_custom_call" | custom-call | flops 3221225472 | bytes 10485760 | tf_op jit(solution)/shard_map/products/pallas_call | solution.py:262
  73.2 0.1 collective-permute-start.19
  73.4 2.8 %collective-permute-done.19 = bf16[32,64,256]{2,1,0:T(8,128)(2,1)S(1)} collective-permute-done((bf16[32,64,256]{2,1,0:T(8,128)(2,1)}, bf16[32,64,256]{2,1,0:T(8,128)(2,1)S(1)}, u32[]{:S(2)}, u32[]{:S(2)}) %collective-permute-start.19) | collective-permute-done | bytes 1048608 | tf_op jit(solution)/shard_map/ppermute | solution.py:295
  76.2 1.7 %fusion.2 = (bf16[32,64,256]{2,1,0:T(8,128)(2,1)S(1)}, f32[32,64,256]{2,1,0:T(8,128)S(1)}) fusion(bf16[32,64,256]{2,1,0:T(8,128)(2,1)S(1)} %collective-permute-done.19, bf16[32,64,256]{2,1,0:T(8,128)(2,1)} %get-tuple-element.37), kind=kLoop, calls=%fused_computation.6 | loop fusion | flops 2097152 | bytes 5242880 | tf_op jit(solution)/shard_map/convert.2
  77.9 0.1 fusion.3
  78.0 0.4 collective-permute-start.20
  78.4 2.3 %collective-permute-start.22 = (bf16[8,64,256]{2,1,0:T(8,128)(2,1)S(1)}, bf16[8,64,256]{2,1,0:T(8,128)(2,1)S(1)}, u32[]{:S(2)}, u32[]{:S(2)}) collective-permute-start(bf16[8,64,256]{2,1,0:T(8,128)(2,1)S(1)} %get-tuple-element.42), channel_id=1, source_target_pairs={{0,6},{2,0},{4,2},{6,4},{1,7},{3,1},{5,3},{7,5},{8,14},{10,8},{12,... | collective-permute-start | bytes 786440 | tf_op jit(solution)/shard_map/ppermute | solution.py:283
  80.7 0.7 collective-permute-start.21
  81.4 5.6 %collective-permute-done.20 = bf16[8,64,256]{2,1,0:T(8,128)(2,1)S(1)} collective-permute-done((bf16[8,64,256]{2,1,0:T(8,128)(2,1)S(1)}, bf16[8,64,256]{2,1,0:T(8,128)(2,1)S(1)}, u32[]{:S(2)}, u32[]{:S(2)}) %collective-permute-start.20) | collective-permute-done | bytes 262176 | tf_op jit(solution)/shard_map/ppermute | solution.py:283
  87.0 0.0 collective-permute-done.22
  87.0 5.6 %collective-permute-done.21 = bf16[8,64,256]{2,1,0:T(8,128)(2,1)S(1)} collective-permute-done((bf16[8,64,256]{2,1,0:T(8,128)(2,1)S(1)}, bf16[8,64,256]{2,1,0:T(8,128)(2,1)S(1)}, u32[]{:S(2)}, u32[]{:S(2)}) %collective-permute-start.21) | collective-permute-done | bytes 262176 | tf_op jit(solution)/shard_map/ppermute | solution.py:283
  92.7 0.9 %fusion.1 = f32[8,64,256]{2,1,0:T(8,128)} fusion(f32[32,64,256]{2,1,0:T(8,128)S(1)} %get-tuple-element.40, bf16[8,64,256]{2,1,0:T(8,128)(2,1)S(1)} %collective-permute-done.22, bf16[8,64,256]{2,1,0:T(8,128)(2,1)S(1)} %collective-permute-done.21, bf16[8,64,256]{2,1,0:T(8,128)(2,1)S(1)} %collective-permute-done.20), kind=kLoop, calls=%fused_computation.3 | loop fusion | flops 786432 | bytes 1835008 | tf_op jit(solution)/shard_map/add | solution.py:326
  (18 shorter events, 0.1 us)
Async XLA Ops:
  1.8 8.3 %collective-permute-start = (bf16[4,64,128]{2,1,0:T(8,128)(2,1)}, bf16[4,64,128]{2,1,0:T(8,128)(2,1)S(1)}, u32[]{:S(2)}, u32[]{:S(2)}) collective-permute-start(bf16[4,64,128]{2,1,0:T(8,128)(2,1)} %get-tuple-element.28), channel_id=1, source_target_pairs={{0,64},{64,128},{128,192},{192,0},{1,65},{65,129},{129,193},{193,1... | collective-permute-start | bytes 196616 | tf_op jit(solution)/shard_map/ppermute | solution.py:283
  3.9 6.2 %collective-permute-start.1 = (bf16[4,64,128]{2,1,0:T(8,128)(2,1)}, bf16[4,64,128]{2,1,0:T(8,128)(2,1)S(1)}, u32[]{:S(2)}, u32[]{:S(2)}) collective-permute-start(bf16[4,64,128]{2,1,0:T(8,128)(2,1)} %get-tuple-element.29), channel_id=1, source_target_pairs={{0,128},{64,192},{128,0},{192,64},{1,129},{65,193},{129,1},{193,65... | collective-permute-start | bytes 196616 | tf_op jit(solution)/shard_map/ppermute | solution.py:283
  6.6 3.6 %collective-permute-start.2 = (bf16[4,64,128]{2,1,0:T(8,128)(2,1)}, bf16[4,64,128]{2,1,0:T(8,128)(2,1)S(1)}, u32[]{:S(2)}, u32[]{:S(2)}) collective-permute-start(bf16[4,64,128]{2,1,0:T(8,128)(2,1)} %get-tuple-element.30), channel_id=1, source_target_pairs={{0,192},{64,0},{128,64},{192,128},{1,193},{65,1},{129,65},{193,129... | collective-permute-start | bytes 196616 | tf_op jit(solution)/shard_map/ppermute | solution.py:283
  7.6 2.4 %copy-start = (bf16[64,64,256]{2,1,0:T(8,128)(2,1)S(1)}, bf16[64,64,256]{2,1,0:T(8,128)(2,1)}, u32[]{:S(2)}) copy-start(bf16[64,64,256]{2,1,0:T(8,128)(2,1)} %refs_8_.1) | copy-start | bytes 6291460
  10.1 2.0 %copy-start.2 = (bf16[4,64,128]{2,1,0:T(8,128)(2,1)}, bf16[4,64,128]{2,1,0:T(8,128)(2,1)S(1)}, u32[]{:S(2)}) copy-start(bf16[4,64,128]{2,1,0:T(8,128)(2,1)S(1)} %collective-permute-done.refs_1_) | copy-start | bytes 196612
  10.2 2.0 %copy-start.3 = (bf16[4,64,128]{2,1,0:T(8,128)(2,1)}, bf16[4,64,128]{2,1,0:T(8,128)(2,1)S(1)}, u32[]{:S(2)}) copy-start(bf16[4,64,128]{2,1,0:T(8,128)(2,1)S(1)} %collective-permute-done.1.refs_2_) | copy-start | bytes 196612
  10.2 2.0 %copy-start.4 = (bf16[4,64,128]{2,1,0:T(8,128)(2,1)}, bf16[4,64,128]{2,1,0:T(8,128)(2,1)S(1)}, u32[]{:S(2)}) copy-start(bf16[4,64,128]{2,1,0:T(8,128)(2,1)S(1)} %collective-permute-done.2.refs_3_) | copy-start | bytes 196612
  10.2 26.1 %collective-permute-start.12 = (bf16[32,64,256]{2,1,0:T(8,128)(2,1)S(1)}, bf16[32,64,256]{2,1,0:T(8,128)(2,1)S(1)}, u32[]{:S(2)}, u32[]{:S(2)}) collective-permute-start(bf16[32,64,256]{2,1,0:T(8,128)(2,1)S(1)} %constant_dynamic-slice_fusion), channel_id=1, source_target_pairs={{0,192},{64,0},{128,64},{192,128},{1,193},{65,1},{129,65},{193,129... | collective-permute-start | bytes 3145736 | tf_op jit(solution)/shard_map/ppermute | solution.py:283
  12.2 27.0 %collective-permute-start.11 = (bf16[32,64,256]{2,1,0:T(8,128)(2,1)S(1)}, bf16[32,64,256]{2,1,0:T(8,128)(2,1)}, u32[]{:S(2)}, u32[]{:S(2)}) collective-permute-start(bf16[32,64,256]{2,1,0:T(8,128)(2,1)S(1)} %constant_dynamic-slice_fusion), channel_id=1, source_target_pairs={{0,64},{64,128},{128,192},{192,0},{1,65},{65,129},{129,193},{193,1... | collective-permute-start | bytes 3145736 | tf_op jit(solution)/shard_map/ppermute | solution.py:283
  14.0 8.2 %collective-permute-start.4 = (bf16[528,256]{1,0:T(8,128)(2,1)}, bf16[528,256]{1,0:T(8,128)(2,1)S(1)}, u32[]{:S(2)}, u32[]{:S(2)}) collective-permute-start(bf16[528,256]{1,0:T(8,128)(2,1)} %join_k.1.refs_0_), channel_id=1, source_target_pairs={{0,1},{1,0},{2,3},{3,2},{4,5},{5,4},{6,7},{7,6},{8,9},{9,8},{10,11... | collective-permute-start | bytes 811016 | tf_op jit(solution)/shard_map/ppermute | solution.py:295
  16.8 9.2 %collective-permute-start.3 = (bf16[528,256]{1,0:T(8,128)(2,1)}, bf16[528,256]{1,0:T(8,128)(2,1)S(1)}, u32[]{:S(2)}, u32[]{:S(2)}) collective-permute-start(bf16[528,256]{1,0:T(8,128)(2,1)} %join_k.1.refs_0_), channel_id=1, source_target_pairs={{0,8},{1,57},{8,16},{9,1},{16,24},{17,9},{24,32},{25,17},{32,40},{... | collective-permute-start | bytes 811016 | tf_op jit(solution)/shard_map/ppermute | solution.py:291
  22.3 7.1 %collective-permute-start.5 = (bf16[528,256]{1,0:T(8,128)(2,1)S(1)}, bf16[528,256]{1,0:T(8,128)(2,1)S(1)}, u32[]{:S(2)}, u32[]{:S(2)}) collective-permute-start(bf16[528,256]{1,0:T(8,128)(2,1)S(1)} %collective-permute-done.4), channel_id=1, source_target_pairs={{0,8},{1,57},{8,16},{9,1},{16,24},{17,9},{24,32},{25,17},{32,40},{... | collective-permute-start | bytes 811016 | tf_op jit(solution)/shard_map/ppermute | solution.py:291
  26.0 29.9 %copy-start.9 = (bf16[528,256]{1,0:T(8,128)(2,1)}, bf16[528,256]{1,0:T(8,128)(2,1)S(1)}, u32[]{:S(2)}) copy-start(bf16[528,256]{1,0:T(8,128)(2,1)S(1)} %collective-permute-done.3.refs_1_) | copy-start | bytes 811012
  26.0 6.8 %collective-permute-start.6 = (bf16[528,256]{1,0:T(8,128)(2,1)S(1)}, bf16[528,256]{1,0:T(8,128)(2,1)S(1)}, u32[]{:S(2)}, u32[]{:S(2)}) collective-permute-start(bf16[528,256]{1,0:T(8,128)(2,1)S(1)} %collective-permute-done.3.refs_1_), channel_id=1, source_target_pairs={{0,8},{1,57},{8,16},{9,1},{16,24},{17,9},{24,32},{25,17},{32,40},{... | collective-permute-start | bytes 811016 | tf_op jit(solution)/shard_map/ppermute | solution.py:291
  29.4 11.0 %copy-start.10 = (bf16[528,256]{1,0:T(8,128)(2,1)}, bf16[528,256]{1,0:T(8,128)(2,1)S(1)}, u32[]{:S(2)}) copy-start(bf16[528,256]{1,0:T(8,128)(2,1)S(1)} %collective-permute-done.5.refs_2_) | copy-start | bytes 811012
  29.4 11.0 %collective-permute-start.7 = (bf16[528,256]{1,0:T(8,128)(2,1)S(1)}, bf16[528,256]{1,0:T(8,128)(2,1)}, u32[]{:S(2)}, u32[]{:S(2)}) collective-permute-start(bf16[528,256]{1,0:T(8,128)(2,1)S(1)} %collective-permute-done.5.refs_2_), channel_id=1, source_target_pairs={{0,8},{1,57},{8,16},{9,1},{16,24},{17,9},{24,32},{25,17},{32,40},{... | collective-permute-start | bytes 811016 | tf_op jit(solution)/shard_map/ppermute | solution.py:291
  32.8 7.6 %copy-start.11 = (bf16[528,256]{1,0:T(8,128)(2,1)}, bf16[528,256]{1,0:T(8,128)(2,1)S(1)}, u32[]{:S(2)}) copy-start(bf16[528,256]{1,0:T(8,128)(2,1)S(1)} %collective-permute-done.6.refs_3_) | copy-start | bytes 811012
  32.8 10.1 %collective-permute-start.8 = (bf16[528,256]{1,0:T(8,128)(2,1)S(1)}, bf16[528,256]{1,0:T(8,128)(2,1)}, u32[]{:S(2)}, u32[]{:S(2)}) collective-permute-start(bf16[528,256]{1,0:T(8,128)(2,1)S(1)} %collective-permute-done.6.refs_3_), channel_id=1, source_target_pairs={{0,8},{1,57},{8,16},{9,1},{16,24},{17,9},{24,32},{25,17},{32,40},{... | collective-permute-start | bytes 811016 | tf_op jit(solution)/shard_map/ppermute | solution.py:291
  36.3 23.5 %copy-start.1 = (bf16[32,64,256]{2,1,0:T(8,128)(2,1)}, bf16[32,64,256]{2,1,0:T(8,128)(2,1)S(1)}, u32[]{:S(2)}) copy-start(bf16[32,64,256]{2,1,0:T(8,128)(2,1)S(1)} %collective-permute-done.12.refs_10_) | copy-start | bytes 3145732
  36.4 15.6 %collective-permute-start.14 = (bf16[16,64,256]{2,1,0:T(8,128)(2,1)S(1)}, bf16[16,64,256]{2,1,0:T(8,128)(2,1)S(1)}, u32[]{:S(2)}, u32[]{:S(2)}) collective-permute-start(bf16[16,64,256]{2,1,0:T(8,128)(2,1)S(1)} %slice.32), channel_id=1, source_target_pairs={{0,192},{64,0},{128,64},{192,128},{1,193},{65,1},{129,65},{193,129... | collective-permute-start | bytes 1572872 | tf_op jit(solution)/shard_map/ppermute | solution.py:283
  40.3 14.6 %collective-permute-start.13 = (bf16[16,64,256]{2,1,0:T(8,128)(2,1)S(1)}, bf16[16,64,256]{2,1,0:T(8,128)(2,1)S(1)}, u32[]{:S(2)}, u32[]{:S(2)}) collective-permute-start(bf16[16,64,256]{2,1,0:T(8,128)(2,1)S(1)} %slice.31), channel_id=1, source_target_pairs={{0,64},{64,128},{128,192},{192,0},{1,65},{65,129},{129,193},{193,1... | collective-permute-start | bytes 1572872 | tf_op jit(solution)/shard_map/ppermute | solution.py:283
  40.4 6.2 %collective-permute-start.9 = (bf16[528,256]{1,0:T(8,128)(2,1)}, bf16[528,256]{1,0:T(8,128)(2,1)}, u32[]{:S(2)}, u32[]{:S(2)}) collective-permute-start(bf16[528,256]{1,0:T(8,128)(2,1)} %collective-permute-done.7.refs_4_), channel_id=1, source_target_pairs={{0,8},{1,57},{8,16},{9,1},{16,24},{17,9},{24,32},{25,17},{32,40},{... | collective-permute-start | bytes 811016 | tf_op jit(solution)/shard_map/ppermute | solution.py:291
  42.8 13.0 %collective-permute-start.10 = (bf16[528,256]{1,0:T(8,128)(2,1)}, bf16[528,256]{1,0:T(8,128)(2,1)}, u32[]{:S(2)}, u32[]{:S(2)}) collective-permute-start(bf16[528,256]{1,0:T(8,128)(2,1)} %collective-permute-done.8.refs_5_), channel_id=1, source_target_pairs={{0,8},{1,57},{8,16},{9,1},{16,24},{17,9},{24,32},{25,17},{32,40},{... | collective-permute-start | bytes 811016 | tf_op jit(solution)/shard_map/ppermute | solution.py:291
  43.6 16.3 %collective-permute-start.16 = (bf16[32,64,256]{2,1,0:T(8,128)(2,1)S(1)}, bf16[32,64,256]{2,1,0:T(8,128)(2,1)}, u32[]{:S(2)}, u32[]{:S(2)}) collective-permute-start(bf16[32,64,256]{2,1,0:T(8,128)(2,1)S(1)} %collective-permute-done.12.refs_10_), channel_id=1, source_target_pairs={{0,1},{1,0},{2,3},{3,2},{4,5},{5,4},{6,7},{7,6},{8,9},{9,8},{10,11... | collective-permute-start | bytes 3145736 | tf_op jit(solution)/shard_map/ppermute | solution.py:295
  46.6 13.3 %collective-permute-start.15 = (bf16[32,64,256]{2,1,0:T(8,128)(2,1)}, bf16[32,64,256]{2,1,0:T(8,128)(2,1)}, u32[]{:S(2)}, u32[]{:S(2)}) collective-permute-start(bf16[32,64,256]{2,1,0:T(8,128)(2,1)} %collective-permute-done.11.refs_9_), channel_id=1, source_target_pairs={{0,1},{1,0},{2,3},{3,2},{4,5},{5,4},{6,7},{7,6},{8,9},{9,8},{10,11... | collective-permute-start | bytes 3145736 | tf_op jit(solution)/shard_map/ppermute | solution.py:295
  52.0 7.8 %copy-start.5 = (bf16[16,64,256]{2,1,0:T(8,128)(2,1)}, bf16[16,64,256]{2,1,0:T(8,128)(2,1)S(1)}, u32[]{:S(2)}) copy-start(bf16[16,64,256]{2,1,0:T(8,128)(2,1)S(1)} %collective-permute-done.14.refs_12_) | copy-start | bytes 1572868
  52.0 7.9 %collective-permute-start.18 = (bf16[16,64,256]{2,1,0:T(8,128)(2,1)S(1)}, bf16[16,64,256]{2,1,0:T(8,128)(2,1)S(1)}, u32[]{:S(2)}, u32[]{:S(2)}) collective-permute-start(bf16[16,64,256]{2,1,0:T(8,128)(2,1)S(1)} %collective-permute-done.14.refs_12_), channel_id=1, source_target_pairs={{0,1},{1,0},{2,3},{3,2},{4,5},{5,4},{6,7},{7,6},{8,9},{9,8},{10,11... | collective-permute-start | bytes 1572872 | tf_op jit(solution)/shard_map/ppermute | solution.py:295
  54.9 5.0 %copy-start.6 = (bf16[16,64,256]{2,1,0:T(8,128)(2,1)}, bf16[16,64,256]{2,1,0:T(8,128)(2,1)S(1)}, u32[]{:S(2)}) copy-start(bf16[16,64,256]{2,1,0:T(8,128)(2,1)S(1)} %collective-permute-done.13.refs_11_) | copy-start | bytes 1572868
  54.9 5.0 %collective-permute-start.17 = (bf16[16,64,256]{2,1,0:T(8,128)(2,1)S(1)}, bf16[16,64,256]{2,1,0:T(8,128)(2,1)S(1)}, u32[]{:S(2)}, u32[]{:S(2)}) collective-permute-start(bf16[16,64,256]{2,1,0:T(8,128)(2,1)S(1)} %collective-permute-done.13.refs_11_), channel_id=1, source_target_pairs={{0,1},{1,0},{2,3},{3,2},{4,5},{5,4},{6,7},{7,6},{8,9},{9,8},{10,11... | collective-permute-start | bytes 1572872 | tf_op jit(solution)/shard_map/ppermute | solution.py:295
  59.9 0.8 copy-start.7
  59.9 1.0 %copy-start.8 = (bf16[16,64,256]{2,1,0:T(8,128)(2,1)}, bf16[16,64,256]{2,1,0:T(8,128)(2,1)S(1)}, u32[]{:S(2)}) copy-start(bf16[16,64,256]{2,1,0:T(8,128)(2,1)S(1)} %collective-permute-done.17.refs_15_) | copy-start | bytes 1572868
  73.2 3.0 %collective-permute-start.19 = (bf16[32,64,256]{2,1,0:T(8,128)(2,1)}, bf16[32,64,256]{2,1,0:T(8,128)(2,1)S(1)}, u32[]{:S(2)}, u32[]{:S(2)}) collective-permute-start(bf16[32,64,256]{2,1,0:T(8,128)(2,1)} %get-tuple-element.38), channel_id=1, source_target_pairs={{0,1},{1,0},{2,3},{3,2},{4,5},{5,4},{6,7},{7,6},{8,9},{9,8},{10,11... | collective-permute-start | bytes 3145736 | tf_op jit(solution)/shard_map/ppermute | solution.py:295
  78.0 9.1 %collective-permute-start.20 = (bf16[8,64,256]{2,1,0:T(8,128)(2,1)S(1)}, bf16[8,64,256]{2,1,0:T(8,128)(2,1)S(1)}, u32[]{:S(2)}, u32[]{:S(2)}) collective-permute-start(bf16[8,64,256]{2,1,0:T(8,128)(2,1)S(1)} %get-tuple-element.41), channel_id=1, source_target_pairs={{0,2},{2,4},{4,6},{6,0},{1,3},{3,5},{5,7},{7,1},{8,10},{10,12},{12... | collective-permute-start | bytes 786440 | tf_op jit(solution)/shard_map/ppermute | solution.py:283
  78.4 8.6 %collective-permute-start.22 = (bf16[8,64,256]{2,1,0:T(8,128)(2,1)S(1)}, bf16[8,64,256]{2,1,0:T(8,128)(2,1)S(1)}, u32[]{:S(2)}, u32[]{:S(2)}) collective-permute-start(bf16[8,64,256]{2,1,0:T(8,128)(2,1)S(1)} %get-tuple-element.42), channel_id=1, source_target_pairs={{0,6},{2,0},{4,2},{6,4},{1,7},{3,1},{5,3},{7,5},{8,14},{10,8},{12,... | collective-permute-start | bytes 786440 | tf_op jit(solution)/shard_map/ppermute | solution.py:283
  80.7 11.9 %collective-permute-start.21 = (bf16[8,64,256]{2,1,0:T(8,128)(2,1)S(1)}, bf16[8,64,256]{2,1,0:T(8,128)(2,1)S(1)}, u32[]{:S(2)}, u32[]{:S(2)}) collective-permute-start(bf16[8,64,256]{2,1,0:T(8,128)(2,1)S(1)} %get-tuple-element.43), channel_id=1, source_target_pairs={{0,4},{2,6},{4,0},{6,2},{1,5},{3,7},{5,1},{7,3},{8,12},{10,14},{12... | collective-permute-start | bytes 786440 | tf_op jit(solution)/shard_map/ppermute | solution.py:283

commit v4 on v3

--- a/solution.py
+++ b/solution.py
@@ -13,6 +13,7 @@
 TPS = 8
 NB = 64
 HALF = NB // 2
+PART = HALF // 2
 QUARTER = 64
 TILE = 256
 MOST = 128
@@ -22,7 +23,7 @@
 WIDE = 8
 LIST = 1280
 NOWHERE = 2.0 * SPOTS * 4096
-SORT_COST = 10**10
+SORT_COST = 20 * 10**9
 ROWS = A_DEV * QUARTER
 BLOCK = ROWS + LABELS
 TABLE_COST = 4 * 10**9
@@ -149,6 +150,8 @@
     first = jnp.concatenate(rows[:N_SRC], axis=0)
     second = jnp.concatenate(rows[N_SRC:], axis=0)
     spot, a, b, rank = first[:, :MOST], first[:, MOST:], second[:, :MOST], second[:, MOST:]
+    b += (me_ref[1] * HALF).astype(F32)
+    b = jnp.where(b < NB, b, b - NB)
     lane = lax.broadcasted_iota(I32, (MOST, MOST), 1)
     row = lax.broadcasted_iota(I32, (MOST, MOST), 0)
     lane_f = lane.astype(F32)
@@ -182,14 +185,23 @@
         field = jnp.where(source == 0, spot[i : i + 1] - 1.0, a[i : i + 1] + 8.0 * i)
         field = jnp.where(source == 2, b[i : i + 1], field)
         fields.append(jnp.where(source == 3, 1.0, field).astype(BF16))
-    for line in range(LIST // MOST):
-        found = jnp.zeros((N_SRC, MOST), F32)
-        for i in range(N_SRC):
-            here = (places[i] == lane_f + float(line * MOST)).astype(F32).astype(BF16)
-            found += jnp.dot(fields[i], here, preferred_element_type=F32)
+    field = jnp.concatenate(fields, axis=1)
+
+    def fill(line):
+        here = [(place == lane_f + float(line * MOST)).astype(F32).astype(BF16) for place in places]
+        found = jnp.dot(field, jnp.concatenate(here, axis=0), preferred_element_type=F32)
         code = found[0:1] * 4096.0 + found[1:2] * 64.0 + found[2:3]
         code = jnp.where(found[3:4] > 0.0, code, NOWHERE)
         listed[line : line + 1, :] = code.astype(I32)
+
+    for line in range(LIST // MOST // 2):
+        fill(line)
+
+    @pl.when(jnp.max(starts) > LIST // 2)
+    def _():
+        for line in range(LIST // MOST // 2, LIST // MOST):
+            fill(line)
+
     listed[LIST // MOST : LIST // MOST + 1, :] = starts[:1].astype(I32)
 
 
@@ -209,29 +221,45 @@
     )(me, *lefts)
 
 
+STEPS = NB // PART
 N_RIGHT = 9
 
 
 def products_kernel(me_ref, listed, *refs):
     lefts, rights, refs = refs[:N_SRC], refs[N_SRC : N_SRC + N_RIGHT], refs[N_SRC + N_RIGHT :]
-    away_ref, home_ref, left, right, total, left_sems, right_sems = refs
+    away_refs, home_refs, refs = refs[:N_X], refs[N_X : 2 * N_X], refs[2 * N_X :]
+    left, right, total, left_sems, right_sems = refs
     core = me_ref[1]
     copies = [
         pltpu.make_async_copy(lefts[i].at[pl.ds(0, ROWS)], left.at[i], left_sems.at[i])
         for i in range(N_SRC)
     ]
-    copies.append(pltpu.make_async_copy(rights[0], right.at[0], right_sems.at[0]))
-    i = 1
-    for first in (core * HALF, (1 - core) * HALF):
-        for quarter, skip, size in ((1, 0, HALF), (3, 0, HALF), (2, 0, HALF // 2), (2, HALF // 2, HALF // 2)):
-            spot = right.at[quarter, pl.ds(pl.multiple_of(first + skip, HALF // 2), size)]
-            copies.append(pltpu.make_async_copy(rights[i], spot, right_sems.at[i]))
-            i += 1
-    for copy in copies:
+    fetches = []
+    for step in range(STEPS):
+        first = (core * HALF + step * PART) & (NB - 1)
+        back, far_back, far_ahead, ahead = rights[1 + step // 2 * 4 : 5 + step // 2 * 4]
+        side = pl.ds(step % 2 * PART, PART)
+        sources = [
+            rights[0].at[pl.ds(pl.multiple_of(first, PART), PART)],
+            back.at[side],
+            far_ahead if step % 2 else far_back,
+            ahead.at[side],
+        ]
+        fetches.append(
+            [
+                pltpu.make_async_copy(
+                    source, right.at[q, pl.ds(step * PART, PART)], right_sems.at[4 * step + q]
+                )
+                for q, source in enumerate(sources)
+            ]
+        )
+    for copy in copies + fetches[0]:
         copy.start()
     total[...] = jnp.zeros_like(total)
     for copy in copies:
         copy.wait()
+    for fetch in fetches[1]:
+        fetch.start()
 
     def step(i, carry):
         sums = []
@@ -252,24 +280,37 @@
                 total[spots[u]] += value[u * QUARTER : (u + 1) * QUARTER]
         return carry
 
-    lax.fori_loop(0, (listed[LIST // MOST, NB] + GROUP * WIDE - 1) // (GROUP * WIDE), step, 0)
-    home_ref[...] = total[pl.ds(pl.multiple_of(core * SPOTS, SPOTS), SPOTS)].astype(BF16)
-    away_ref[...] = total[pl.ds(pl.multiple_of((1 - core) * SPOTS, SPOTS), SPOTS)].astype(BF16)
+    done = 0
+    for part in range(STEPS):
+        for fetch in fetches[part]:
+            fetch.wait()
+        if part + 2 < STEPS:
+            for fetch in fetches[part + 2]:
+                fetch.start()
+        end = listed[LIST // MOST, (part + 1) * PART]
+        end = end // (GROUP * WIDE) if part < STEPS - 1 else (end + GROUP * WIDE - 1) // (GROUP * WIDE)
+        lax.fori_loop(done, end, step, 0)
+        done = end
+    for refs, owner_core in ((away_refs, 1 - core), (home_refs, core)):
+        for shift, ref in enumerate(refs):
+            first = pl.multiple_of(owner_core * SPOTS + shift * OWN_DEV, OWN_DEV)
+            ref[...] = total[pl.ds(first, OWN_DEV)].astype(ref.dtype)
 
 
 def products(me, listed, lefts, rights):
-    shape = (SPOTS, QUARTER, TILE)
+    shape = (OWN_DEV, QUARTER, TILE)
+    types = [BF16] * N_X + [F32] + [BF16] * (N_X - 1)
     return pl.pallas_call(
         products_kernel,
-        out_shape=[jax.ShapeDtypeStruct(shape, BF16)] * 2,
+        out_shape=[jax.ShapeDtypeStruct(shape, kind) for kind in types],
         in_specs=[SMEM] * 2 + [ANY] * (N_SRC + N_RIGHT),
-        out_specs=[VMEM] * 2,
+        out_specs=[VMEM] * (2 * N_X),
         scratch_shapes=[
             pltpu.VMEM((N_SRC, ROWS, TILE), BF16),
             pltpu.VMEM((N_REP, NB, QUARTER, TILE), BF16),
             pltpu.VMEM((2 * SPOTS + 1, QUARTER, TILE), F32),
             pltpu.SemaphoreType.DMA((N_SRC,)),
-            pltpu.SemaphoreType.DMA((N_RIGHT,)),
+            pltpu.SemaphoreType.DMA((N_REP * STEPS,)),
         ],
         compiler_params=pltpu.CompilerParams(vmem_limit_bytes=VMEM_LIMIT),
         cost_estimate=pl.CostEstimate(
@@ -305,7 +346,7 @@
         blocks += [own, other]
     far_back = shift_by(back[: HALF // 2], "rep", N_REP, 1)
     far_ahead = shift_by(ahead[HALF // 2 :], "rep", N_REP, -1)
-    parts = [back, ahead, far_back, far_ahead]
+    parts = [back, far_back, far_ahead, ahead]
     return blocks + [apart(own, "z", N_Z)], parts + [other_core(part) for part in parts]
 
 
@@ -315,15 +356,16 @@
     half = lax.dynamic_slice_in_dim(integrals, core * HALF, HALF, 0)
     table = product_table(x[None], a_index, b_index, live, owner, target)
     parts = [pieces[0]] + [shift_by(pieces[s], "rep", N_REP, s) for s in range(1, N_REP)]
-    half, table, *parts = lax.optimization_barrier((half, table, *parts))
-    lefts, rights = gather(join_k(table, parts), half)
+    joined, half = lax.optimization_barrier((join_k(table, parts), half))
+    lefts, rights = gather(joined, half)
     me = jnp.stack([z, core])
-    away, home = products(me, sort_products(me, lefts), lefts, [integrals] + rights)
-    sums = home.astype(F32) + other_core(away).astype(F32)
-    sums = sums.reshape(N_X, OWN_DEV, QUARTER, TILE)
-    total = sums[0]
-    for step in range(1, N_X):
-        total = total + shift_by(sums[step].astype(BF16), "x", N_X, step).astype(F32)
+    sums = products(me, sort_products(me, lefts), lefts, [integrals] + rights)
+    total = None
+    for shift in (2, 1, 3, 0):
+        part = sums[N_X + shift].astype(F32) + other_core(sums[shift]).astype(F32)
+        if shift > 0:
+            part = shift_by(part.astype(BF16), "x", N_X, shift).astype(F32)
+        total = part if total is None else total + part
     return total
 
 

time: 94.7 us -> 91.7 us (0.968)
  waiting for transfers between devices: 21.9 us -> 12.5 us
  starting transfers between devices: 43.7 us -> 49.5 us
  other arithmetic: 3.24 us -> 4.61 us
    ppermute x10, waiting for transfers between devices: 14.2 us -> 7.56 us  [shift_by(): lax.ppermute(value, axis, [(i, (i + step) % size) for i in range(size)])]
    convert_element_type x0 -> x3, other arithmetic: none -> 3.05 us  [body(): part = shift_by(part.astype(BF16), 'x', N_X, shift).astype(F32)]
    ppermute x10, starting transfers between devices: 14.1 us -> 16.5 us  [shift_by(): lax.ppermute(value, axis, [(i, (i + step) % size) for i in range(size)])]
    ppermute x6 -> x9, waiting for transfers between devices: 2.86 us -> 0.78 us  [other_core(): return lax.ppermute(value, 'core', [(0, 1), (1, 0)])]
    unnamed x24 -> x28, local copies, waits for them, and re-layouts: 0.99 us -> 3.05 us
    ppermute x6 -> x9, starting transfers between devices: 9.74 us -> 11.7 us  [other_core(): return lax.ppermute(value, 'core', [(0, 1), (1, 0)])]
    another operation x1 -> x0, other arithmetic: 1.68 us -> none
    ppermute x7, starting transfers between devices: 19.8 us -> 21.4 us  [apart(): return lax.ppermute(value, (axis, 'core'), perm)]
  transfers between devices with their start and end apart: 23 -> 26, of which waited for: 7 -> 6; matrix products, arithmetic and copies ran while one was open for 2% -> 4% of each run, Pallas kernels for 9% -> 7%
where the time goes in v4:
time: 91.7 us; the launch traced here: 91.5 us
  starting transfers between devices  49.5 us (54%)
  Pallas kernels  21.4 us (23%)
  waiting for transfers between devices  12.5 us (14%)
  other arithmetic  4.61 us (5%)
  local copies, waits for them, and re-layouts  3.22 us (4%)
    ppermute x7, starting transfers between devices, apart(): return lax.ppermute(value, (axis, 'core'), perm)  21.4 us
    ppermute x10, starting transfers between devices, shift_by(): lax.ppermute(value, axis, [(i, (i + step) % size) for i in range(size)])  16.5 us
    pallas_call x1, Pallas kernels, products(): pl.pallas_call(products_kernel, out_shape=[jax.ShapeDtypeStruct(shape, ki...  11.8 us
    ppermute x9, starting transfers between devices, other_core(): return lax.ppermute(value, 'core', [(0, 1), (1, 0)])  11.7 us
    ppermute x10, waiting for transfers between devices, shift_by(): lax.ppermute(value, axis, [(i, (i + step) % size) for i in range(size)])  7.56 us
    ppermute x7, waiting for transfers between devices, apart(): return lax.ppermute(value, (axis, 'core'), perm)  4.21 us
    pallas_call x1, Pallas kernels, sort_products(): pl.pallas_call(sort_kernel, out_shape=jax.ShapeDtypeStruct((LIST // MOST...  3.65 us
    convert_element_type x3, other arithmetic, body(): part = shift_by(part.astype(BF16), 'x', N_X, shift).astype(F32)  3.05 us
  transfers between devices with their start and end apart: 26, of which 6 were waited for; matrix products, arithmetic and copies ran while one was open for 4% of the time, Pallas kernels for 7%

profile of v4, /device:TPU:1, one launch (start us, length us, event | category | flops | bytes accessed | tf_op | source)
XLA Modules:
  0.0 91.5 jit_solution(15305881700640172666)
XLA Ops:
  0.0 1.8 %spread_rows.1 = (bf16[4,64,128]{2,1,0:T(8,128)(2,1)}, bf16[4,64,128]{2,1,0:T(8,128)(2,1)}, bf16[4,64,128]{2,1,0:T(8,128)(2,1)}, bf16[4,64,128]{2,1,0:T(8,128)(2,1)}) custom-call(s32[1]{0:T(128)} %bitcast.2.rep_ref, bf16[8,64,256]{2,1,0:T(8,128)(2,1)} %bitcast.6), custom_call_target="tpu_custom_call" | custom-call | tf_op jit(solution)/shard_map/spread_rows/pallas_call | solution.py:101
  1.8 2.1 %collective-permute-start = (bf16[4,64,128]{2,1,0:T(8,128)(2,1)}, bf16[4,64,128]{2,1,0:T(8,128)(2,1)S(1)}, u32[]{:S(2)}, u32[]{:S(2)}) collective-permute-start(bf16[4,64,128]{2,1,0:T(8,128)(2,1)} %get-tuple-element.30), channel_id=1, source_target_pairs={{0,64},{64,128},{128,192},{192,0},{1,65},{65,129},{129,193},{193,1... | collective-permute-start | bytes 196616 | tf_op jit(solution)/shard_map/ppermute | solution.py:324
  3.9 2.6 %collective-permute-start.1 = (bf16[4,64,128]{2,1,0:T(8,128)(2,1)}, bf16[4,64,128]{2,1,0:T(8,128)(2,1)S(1)}, u32[]{:S(2)}, u32[]{:S(2)}) collective-permute-start(bf16[4,64,128]{2,1,0:T(8,128)(2,1)} %get-tuple-element.31), channel_id=1, source_target_pairs={{0,128},{64,192},{128,0},{192,64},{1,129},{65,193},{129,1},{193,65... | collective-permute-start | bytes 196616 | tf_op jit(solution)/shard_map/ppermute | solution.py:324
  6.6 1.1 %collective-permute-start.2 = (bf16[4,64,128]{2,1,0:T(8,128)(2,1)}, bf16[4,64,128]{2,1,0:T(8,128)(2,1)S(1)}, u32[]{:S(2)}, u32[]{:S(2)}) collective-permute-start(bf16[4,64,128]{2,1,0:T(8,128)(2,1)} %get-tuple-element.32), channel_id=1, source_target_pairs={{0,192},{64,0},{128,64},{192,128},{1,193},{65,1},{129,65},{193,129... | collective-permute-start | bytes 196616 | tf_op jit(solution)/shard_map/ppermute | solution.py:324
  7.6 2.4 %product_table.1.table_ref = bf16[16,256]{1,0:T(8,128)(2,1)} custom-call(s32[1]{0:T(128)} %bitcast.4.x_ref, s32[384]{0:T(512)} %a_ref.1, s32[384]{0:T(512)} %b_ref.1, s32[384]{0:T(512)} %live_ref.1, s32[48]{0:T(128)} %bitcast.7, s32[48]{0:T(128)} %target_ref.1), custom_call_target="tpu_custom_call" | custom-call | flops 4000000000 | bytes 65536 | tf_op jit(solution)/shard_map/product_table/pallas_call | solution.py:77
  10.0 0.1 constant_dynamic-slice_fusion
  10.1 0.0 collective-permute-done.refs_1_
  10.1 0.0 collective-permute-done.1.refs_2_
  10.2 0.0 collective-permute-done.2.refs_3_
  10.2 0.6 copy-done.4
  10.8 0.0 copy-done.5
  10.8 0.6 copy-done.6
  11.4 1.8 %join_k.1.refs_0_ = bf16[528,256]{1,0:T(8,128)(2,1)} custom-call(bf16[16,256]{1,0:T(8,128)(2,1)} %product_table.1.table_ref, bf16[4,64,128]{2,1,0:T(8,128)(2,1)} %get-tuple-element.29.refs_0_, bf16[4,64,128]{2,1,0:T(8,128)(2,1)} %copy-done.4, bf16[4,64,128]{2,1,0:T(8,128)(2,1)} %copy-done.5, bf16[4,64,128]{2,1,0:T(8,128)(2,1)} %copy-done.6), custom_call_target="tpu_custom_call" | custom-call | tf_op jit(solution)/shard_map/join_k/pallas_call | solution.py:124
  13.2 1.4 %collective-permute-start.13 = (bf16[32,64,256]{2,1,0:T(8,128)(2,1)S(1)}, bf16[32,64,256]{2,1,0:T(8,128)(2,1)S(1)}, u32[]{:S(2)}, u32[]{:S(2)}) collective-permute-start(bf16[32,64,256]{2,1,0:T(8,128)(2,1)S(1)} %constant_dynamic-slice_fusion), channel_id=1, source_target_pairs={{0,192},{64,0},{128,64},{192,128},{1,193},{65,1},{129,65},{193,129... | collective-permute-start | bytes 3145736 | tf_op jit(solution)/shard_map/ppermute | solution.py:324
  14.6 0.1 collective-permute-start.11
  14.7 2.7 %collective-permute-start.4 = (bf16[528,256]{1,0:T(8,128)(2,1)}, bf16[528,256]{1,0:T(8,128)(2,1)S(1)}, u32[]{:S(2)}, u32[]{:S(2)}) collective-permute-start(bf16[528,256]{1,0:T(8,128)(2,1)} %join_k.1.refs_0_), channel_id=1, source_target_pairs={{0,1},{1,0},{2,3},{3,2},{4,5},{5,4},{6,7},{7,6},{8,9},{9,8},{10,11... | collective-permute-start | bytes 811016 | tf_op jit(solution)/shard_map/ppermute | solution.py:336
  17.4 5.4 %collective-permute-start.3 = (bf16[528,256]{1,0:T(8,128)(2,1)}, bf16[528,256]{1,0:T(8,128)(2,1)S(1)}, u32[]{:S(2)}, u32[]{:S(2)}) collective-permute-start(bf16[528,256]{1,0:T(8,128)(2,1)} %join_k.1.refs_0_), channel_id=1, source_target_pairs={{0,8},{1,57},{8,16},{9,1},{16,24},{17,9},{24,32},{25,17},{32,40},{... | collective-permute-start | bytes 811016 | tf_op jit(solution)/shard_map/ppermute | solution.py:332
  22.8 0.0 collective-permute-done.4
  22.8 1.4 %collective-permute-start.5 = (bf16[528,256]{1,0:T(8,128)(2,1)S(1)}, bf16[528,256]{1,0:T(8,128)(2,1)S(1)}, u32[]{:S(2)}, u32[]{:S(2)}) collective-permute-start(bf16[528,256]{1,0:T(8,128)(2,1)S(1)} %collective-permute-done.4), channel_id=1, source_target_pairs={{0,8},{1,57},{8,16},{9,1},{16,24},{17,9},{24,32},{25,17},{32,40},{... | collective-permute-start | bytes 811016 | tf_op jit(solution)/shard_map/ppermute | solution.py:332
  24.2 2.3 %collective-permute-done.3.refs_1_ = bf16[528,256]{1,0:T(8,128)(2,1)S(1)} collective-permute-done((bf16[528,256]{1,0:T(8,128)(2,1)}, bf16[528,256]{1,0:T(8,128)(2,1)S(1)}, u32[]{:S(2)}, u32[]{:S(2)}) %collective-permute-start.3) | collective-permute-done | bytes 270368 | tf_op jit(solution)/shard_map/ppermute | solution.py:332
  26.6 3.3 %collective-permute-start.6 = (bf16[528,256]{1,0:T(8,128)(2,1)S(1)}, bf16[528,256]{1,0:T(8,128)(2,1)S(1)}, u32[]{:S(2)}, u32[]{:S(2)}) collective-permute-start(bf16[528,256]{1,0:T(8,128)(2,1)S(1)} %collective-permute-done.3.refs_1_), channel_id=1, source_target_pairs={{0,8},{1,57},{8,16},{9,1},{16,24},{17,9},{24,32},{25,17},{32,40},{... | collective-permute-start | bytes 811016 | tf_op jit(solution)/shard_map/ppermute | solution.py:332
  29.9 0.0 collective-permute-done.5.refs_2_
  29.9 2.9 %collective-permute-start.7 = (bf16[528,256]{1,0:T(8,128)(2,1)S(1)}, bf16[528,256]{1,0:T(8,128)(2,1)}, u32[]{:S(2)}, u32[]{:S(2)}) collective-permute-start(bf16[528,256]{1,0:T(8,128)(2,1)S(1)} %collective-permute-done.5.refs_2_), channel_id=1, source_target_pairs={{0,8},{1,57},{8,16},{9,1},{16,24},{17,9},{24,32},{25,17},{32,40},{... | collective-permute-start | bytes 811016 | tf_op jit(solution)/shard_map/ppermute | solution.py:332
  32.8 0.5 collective-permute-done.6.refs_3_
  33.3 3.4 %collective-permute-start.8 = (bf16[528,256]{1,0:T(8,128)(2,1)S(1)}, bf16[528,256]{1,0:T(8,128)(2,1)}, u32[]{:S(2)}, u32[]{:S(2)}) collective-permute-start(bf16[528,256]{1,0:T(8,128)(2,1)S(1)} %collective-permute-done.6.refs_3_), channel_id=1, source_target_pairs={{0,8},{1,57},{8,16},{9,1},{16,24},{17,9},{24,32},{25,17},{32,40},{... | collective-permute-start | bytes 811016 | tf_op jit(solution)/shard_map/ppermute | solution.py:332
  36.7 0.0 collective-permute-done.13.refs_12_
  36.7 3.0 %collective-permute-start.14 = (bf16[16,64,256]{2,1,0:T(8,128)(2,1)S(1)}, bf16[16,64,256]{2,1,0:T(8,128)(2,1)S(1)}, u32[]{:S(2)}, u32[]{:S(2)}) collective-permute-start(bf16[16,64,256]{2,1,0:T(8,128)(2,1)S(1)} %slice.9), channel_id=1, source_target_pairs={{0,192},{64,0},{128,64},{192,128},{1,193},{65,1},{129,65},{193,129... | collective-permute-start | bytes 1572872 | tf_op jit(solution)/shard_map/ppermute | solution.py:324
  39.8 0.0 collective-permute-done.11.refs_9_
  39.8 0.1 collective-permute-start.12
  39.9 0.9 copy-done.3
  40.8 0.0 collective-permute-done.7.refs_4_
  40.8 4.2 %collective-permute-start.9 = (bf16[528,256]{1,0:T(8,128)(2,1)}, bf16[528,256]{1,0:T(8,128)(2,1)}, u32[]{:S(2)}, u32[]{:S(2)}) collective-permute-start(bf16[528,256]{1,0:T(8,128)(2,1)} %collective-permute-done.7.refs_4_), channel_id=1, source_target_pairs={{0,8},{1,57},{8,16},{9,1},{16,24},{17,9},{24,32},{25,17},{32,40},{... | collective-permute-start | bytes 811016 | tf_op jit(solution)/shard_map/ppermute | solution.py:332
  45.0 0.0 collective-permute-done.8.refs_5_
  45.0 0.7 collective-permute-start.10
  45.7 0.6 pad_add_fusion.me_ref
  46.3 1.0 %collective-permute-start.18 = (bf16[32,64,256]{2,1,0:T(8,128)(2,1)S(1)}, bf16[32,64,256]{2,1,0:T(8,128)(2,1)}, u32[]{:S(2)}, u32[]{:S(2)}) collective-permute-start(bf16[32,64,256]{2,1,0:T(8,128)(2,1)S(1)} %collective-permute-done.13.refs_12_), channel_id=1, source_target_pairs={{0,1},{1,0},{2,3},{3,2},{4,5},{5,4},{6,7},{7,6},{8,9},{9,8},{10,11... | collective-permute-start | bytes 3145736 | tf_op jit(solution)/shard_map/ppermute | solution.py:336
  47.4 1.4 %collective-permute-done.9.refs_6_ = bf16[528,256]{1,0:T(8,128)(2,1)} collective-permute-done((bf16[528,256]{1,0:T(8,128)(2,1)}, bf16[528,256]{1,0:T(8,128)(2,1)}, u32[]{:S(2)}, u32[]{:S(2)}) %collective-permute-start.9) | collective-permute-done | bytes 270368 | tf_op jit(solution)/shard_map/ppermute | solution.py:332
  48.7 4.8 %collective-permute-start.15 = (bf16[32,64,256]{2,1,0:T(8,128)(2,1)}, bf16[32,64,256]{2,1,0:T(8,128)(2,1)}, u32[]{:S(2)}, u32[]{:S(2)}) collective-permute-start(bf16[32,64,256]{2,1,0:T(8,128)(2,1)} %copy-done.3), channel_id=1, source_target_pairs={{0,1},{1,0},{2,3},{3,2},{4,5},{5,4},{6,7},{7,6},{8,9},{9,8},{10,11... | collective-permute-start | bytes 3145736 | tf_op jit(solution)/shard_map/ppermute | solution.py:336
  53.5 0.0 collective-permute-done.14.refs_11_
  53.5 0.1 collective-permute-start.17
  53.6 0.0 collective-permute-done.12.refs_10_
  53.6 1.8 %collective-permute-start.16 = (bf16[16,64,256]{2,1,0:T(8,128)(2,1)S(1)}, bf16[16,64,256]{2,1,0:T(8,128)(2,1)S(1)}, u32[]{:S(2)}, u32[]{:S(2)}) collective-permute-start(bf16[16,64,256]{2,1,0:T(8,128)(2,1)S(1)} %collective-permute-done.12.refs_10_), channel_id=1, source_target_pairs={{0,1},{1,0},{2,3},{3,2},{4,5},{5,4},{6,7},{7,6},{8,9},{9,8},{10,11... | collective-permute-start | bytes 1572872 | tf_op jit(solution)/shard_map/ppermute | solution.py:336
  55.5 0.0 collective-permute-done.10.refs_7_
  55.5 3.6 %sort_products.1.listed = s32[11,128]{1,0:T(8,128)} custom-call(s32[2]{0:T(128)} %pad_add_fusion.me_ref, bf16[528,256]{1,0:T(8,128)(2,1)} %join_k.1.refs_0_, bf16[528,256]{1,0:T(8,128)(2,1)} %copy-done.11, bf16[528,256]{1,0:T(8,128)(2,1)} %copy-done.12, bf16[528,256]{1,0:T(8,128)(2,1)} %copy-done.13, bf16[528,256]{1,0:T(8,128)(2,1)} %collective-permute-done.7.refs_4_, ...), custom_call_target="tpu_custom_call" | custom-call | flops 20000000000 | bytes 65536 | tf_op jit(solution)/shard_map/sort_products/pallas_call | solution.py:209
  59.2 0.0 collective-permute-done.18.refs_16_
  59.2 0.0 collective-permute-done.16.refs_14_
  59.2 0.7 copy-done.9
  59.9 0.2 copy-done.10
  60.2 11.8 %products.1 = (bf16[8,64,256]{2,1,0:T(8,128)(2,1)}, bf16[8,64,256]{2,1,0:T(8,128)(2,1)}, bf16[8,64,256]{2,1,0:T(8,128)(2,1)}, bf16[8,64,256]{2,1,0:T(8,128)(2,1)...) custom-call(s32[2]{0:T(128)} %pad_add_fusion.me_ref, ...), custom_call_target="tpu_custom_call" | custom-call | flops 3221225472 | bytes 10485760 | tf_op jit(solution)/shard_map/products/pallas_call | solution.py:303
  71.9 0.5 collective-permute-start.19
  72.5 0.1 collective-permute-start.21
  72.6 0.4 collective-permute-start.23
  73.0 0.1 collective-permute-start.25
  73.1 0.8 collective-permute-done.19
  73.9 1.0 %add_convert_fusion.2 = bf16[8,64,256]{2,1,0:T(8,128)(2,1)S(1)} fusion(bf16[8,64,256]{2,1,0:T(8,128)(2,1)S(1)} %collective-permute-done.19, bf16[8,64,256]{2,1,0:T(8,128)(2,1)} %get-tuple-element.35), kind=kLoop, calls=%fused_computation.3 | loop fusion | flops 524288 | bytes 786432 | tf_op jit(solution)/shard_map/convert_element_type | solution.py:367
  74.9 3.3 %collective-permute-start.20 = (bf16[8,64,256]{2,1,0:T(8,128)(2,1)S(1)}, bf16[8,64,256]{2,1,0:T(8,128)(2,1)S(1)}, u32[]{:S(2)}, u32[]{:S(2)}) collective-permute-start(bf16[8,64,256]{2,1,0:T(8,128)(2,1)S(1)} %add_convert_fusion.2), channel_id=1, source_target_pairs={{0,4},{2,6},{4,0},{6,2},{1,5},{3,7},{5,1},{7,3},{8,12},{10,14},{12... | collective-permute-start | bytes 786440 | tf_op jit(solution)/shard_map/ppermute | solution.py:324
  78.1 1.0 %add_convert_fusion.1 = bf16[8,64,256]{2,1,0:T(8,128)(2,1)S(1)} fusion(bf16[8,64,256]{2,1,0:T(8,128)(2,1)S(1)} %collective-permute-done.21, bf16[8,64,256]{2,1,0:T(8,128)(2,1)} %get-tuple-element.37), kind=kLoop, calls=%fused_computation.2 | loop fusion | flops 524288 | bytes 786432 | tf_op jit(solution)/shard_map/convert_element_type | solution.py:367
  79.2 0.4 collective-permute-start.22
  79.6 1.0 %add_convert_fusion = bf16[8,64,256]{2,1,0:T(8,128)(2,1)S(1)} fusion(bf16[8,64,256]{2,1,0:T(8,128)(2,1)S(1)} %collective-permute-done.23, bf16[8,64,256]{2,1,0:T(8,128)(2,1)} %get-tuple-element.39), kind=kLoop, calls=%fused_computation.1 | loop fusion | flops 524288 | bytes 786432 | tf_op jit(solution)/shard_map/convert_element_type | solution.py:367
  80.6 2.4 %collective-permute-start.24 = (bf16[8,64,256]{2,1,0:T(8,128)(2,1)S(1)}, bf16[8,64,256]{2,1,0:T(8,128)(2,1)S(1)}, u32[]{:S(2)}, u32[]{:S(2)}) collective-permute-start(bf16[8,64,256]{2,1,0:T(8,128)(2,1)S(1)} %add_convert_fusion), channel_id=1, source_target_pairs={{0,6},{2,0},{4,2},{6,4},{1,7},{3,1},{5,3},{7,5},{8,14},{10,8},{12,... | collective-permute-start | bytes 786440 | tf_op jit(solution)/shard_map/ppermute | solution.py:324
  83.0 0.0 collective-permute-done.25
  83.0 1.4 %collective-permute-done.20 = bf16[8,64,256]{2,1,0:T(8,128)(2,1)S(1)} collective-permute-done((bf16[8,64,256]{2,1,0:T(8,128)(2,1)S(1)}, bf16[8,64,256]{2,1,0:T(8,128)(2,1)S(1)}, u32[]{:S(2)}, u32[]{:S(2)}) %collective-permute-start.20) | collective-permute-done | bytes 262176 | tf_op jit(solution)/shard_map/ppermute | solution.py:324
  84.4 6.1 %collective-permute-done.22 = bf16[8,64,256]{2,1,0:T(8,128)(2,1)S(1)} collective-permute-done((bf16[8,64,256]{2,1,0:T(8,128)(2,1)S(1)}, bf16[8,64,256]{2,1,0:T(8,128)(2,1)S(1)}, u32[]{:S(2)}, u32[]{:S(2)}) %collective-permute-start.22) | collective-permute-done | bytes 262176 | tf_op jit(solution)/shard_map/ppermute | solution.py:324
  90.5 0.9 %add_add_fusion = f32[8,64,256]{2,1,0:T(8,128)} fusion(f32[8,64,256]{2,1,0:T(8,128)S(1)} %copy-done.1, bf16[8,64,256]{2,1,0:T(8,128)(2,1)S(1)} %collective-permute-done.25, bf16[8,64,256]{2,1,0:T(8,128)(2,1)S(1)} %collective-permute-done.24, bf16[8,64,256]{2,1,0:T(8,128)(2,1)S(1)} %collective-permute-done.22, bf16[8,64,256]{2,1,0:T(8,128)(2,1)S(1)} %collective-permute-done.20), kind=kLoop, calls=%fused_computation | loop fusion | flops 1048576 | bytes 2097152 | tf_op jit(solution)/shard_map/add | solution.py:368
  (29 shorter events, 0.1 us)
Async XLA Ops:
  1.8 8.3 %collective-permute-start = (bf16[4,64,128]{2,1,0:T(8,128)(2,1)}, bf16[4,64,128]{2,1,0:T(8,128)(2,1)S(1)}, u32[]{:S(2)}, u32[]{:S(2)}) collective-permute-start(bf16[4,64,128]{2,1,0:T(8,128)(2,1)} %get-tuple-element.30), channel_id=1, source_target_pairs={{0,64},{64,128},{128,192},{192,0},{1,65},{65,129},{129,193},{193,1... | collective-permute-start | bytes 196616 | tf_op jit(solution)/shard_map/ppermute | solution.py:324
  3.9 6.2 %collective-permute-start.1 = (bf16[4,64,128]{2,1,0:T(8,128)(2,1)}, bf16[4,64,128]{2,1,0:T(8,128)(2,1)S(1)}, u32[]{:S(2)}, u32[]{:S(2)}) collective-permute-start(bf16[4,64,128]{2,1,0:T(8,128)(2,1)} %get-tuple-element.31), channel_id=1, source_target_pairs={{0,128},{64,192},{128,0},{192,64},{1,129},{65,193},{129,1},{193,65... | collective-permute-start | bytes 196616 | tf_op jit(solution)/shard_map/ppermute | solution.py:324
  6.6 3.6 %collective-permute-start.2 = (bf16[4,64,128]{2,1,0:T(8,128)(2,1)}, bf16[4,64,128]{2,1,0:T(8,128)(2,1)S(1)}, u32[]{:S(2)}, u32[]{:S(2)}) collective-permute-start(bf16[4,64,128]{2,1,0:T(8,128)(2,1)} %get-tuple-element.32), channel_id=1, source_target_pairs={{0,192},{64,0},{128,64},{192,128},{1,193},{65,1},{129,65},{193,129... | collective-permute-start | bytes 196616 | tf_op jit(solution)/shard_map/ppermute | solution.py:324
  7.6 2.4 %copy-start = (bf16[64,64,256]{2,1,0:T(8,128)(2,1)S(1)}, bf16[64,64,256]{2,1,0:T(8,128)(2,1)}, u32[]{:S(2)}) copy-start(bf16[64,64,256]{2,1,0:T(8,128)(2,1)} %refs_8_.1) | copy-start | bytes 6291460
  10.1 0.6 copy-start.4
  10.2 0.6 copy-start.5
  10.8 0.6 copy-start.6
  13.2 23.5 %collective-permute-start.13 = (bf16[32,64,256]{2,1,0:T(8,128)(2,1)S(1)}, bf16[32,64,256]{2,1,0:T(8,128)(2,1)S(1)}, u32[]{:S(2)}, u32[]{:S(2)}) collective-permute-start(bf16[32,64,256]{2,1,0:T(8,128)(2,1)S(1)} %constant_dynamic-slice_fusion), channel_id=1, source_target_pairs={{0,192},{64,0},{128,64},{192,128},{1,193},{65,1},{129,65},{193,129... | collective-permute-start | bytes 3145736 | tf_op jit(solution)/shard_map/ppermute | solution.py:324
  14.6 25.2 %collective-permute-start.11 = (bf16[32,64,256]{2,1,0:T(8,128)(2,1)S(1)}, bf16[32,64,256]{2,1,0:T(8,128)(2,1)S(1)}, u32[]{:S(2)}, u32[]{:S(2)}) collective-permute-start(bf16[32,64,256]{2,1,0:T(8,128)(2,1)S(1)} %constant_dynamic-slice_fusion), channel_id=1, source_target_pairs={{0,64},{64,128},{128,192},{192,0},{1,65},{65,129},{129,193},{193,1... | collective-permute-start | bytes 3145736 | tf_op jit(solution)/shard_map/ppermute | solution.py:324
  14.7 8.2 %collective-permute-start.4 = (bf16[528,256]{1,0:T(8,128)(2,1)}, bf16[528,256]{1,0:T(8,128)(2,1)S(1)}, u32[]{:S(2)}, u32[]{:S(2)}) collective-permute-start(bf16[528,256]{1,0:T(8,128)(2,1)} %join_k.1.refs_0_), channel_id=1, source_target_pairs={{0,1},{1,0},{2,3},{3,2},{4,5},{5,4},{6,7},{7,6},{8,9},{9,8},{10,11... | collective-permute-start | bytes 811016 | tf_op jit(solution)/shard_map/ppermute | solution.py:336
  17.4 9.2 %collective-permute-start.3 = (bf16[528,256]{1,0:T(8,128)(2,1)}, bf16[528,256]{1,0:T(8,128)(2,1)S(1)}, u32[]{:S(2)}, u32[]{:S(2)}) collective-permute-start(bf16[528,256]{1,0:T(8,128)(2,1)} %join_k.1.refs_0_), channel_id=1, source_target_pairs={{0,8},{1,57},{8,16},{9,1},{16,24},{17,9},{24,32},{25,17},{32,40},{... | collective-permute-start | bytes 811016 | tf_op jit(solution)/shard_map/ppermute | solution.py:332
  22.8 7.0 %collective-permute-start.5 = (bf16[528,256]{1,0:T(8,128)(2,1)S(1)}, bf16[528,256]{1,0:T(8,128)(2,1)S(1)}, u32[]{:S(2)}, u32[]{:S(2)}) collective-permute-start(bf16[528,256]{1,0:T(8,128)(2,1)S(1)} %collective-permute-done.4), channel_id=1, source_target_pairs={{0,8},{1,57},{8,16},{9,1},{16,24},{17,9},{24,32},{25,17},{32,40},{... | collective-permute-start | bytes 811016 | tf_op jit(solution)/shard_map/ppermute | solution.py:332
  26.6 28.9 %copy-start.11 = (bf16[528,256]{1,0:T(8,128)(2,1)}, bf16[528,256]{1,0:T(8,128)(2,1)S(1)}, u32[]{:S(2)}) copy-start(bf16[528,256]{1,0:T(8,128)(2,1)S(1)} %collective-permute-done.3.refs_1_) | copy-start | bytes 811012
  26.6 6.7 %collective-permute-start.6 = (bf16[528,256]{1,0:T(8,128)(2,1)S(1)}, bf16[528,256]{1,0:T(8,128)(2,1)S(1)}, u32[]{:S(2)}, u32[]{:S(2)}) collective-permute-start(bf16[528,256]{1,0:T(8,128)(2,1)S(1)} %collective-permute-done.3.refs_1_), channel_id=1, source_target_pairs={{0,8},{1,57},{8,16},{9,1},{16,24},{17,9},{24,32},{25,17},{32,40},{... | collective-permute-start | bytes 811016 | tf_op jit(solution)/shard_map/ppermute | solution.py:332
  29.9 10.9 %copy-start.12 = (bf16[528,256]{1,0:T(8,128)(2,1)}, bf16[528,256]{1,0:T(8,128)(2,1)S(1)}, u32[]{:S(2)}) copy-start(bf16[528,256]{1,0:T(8,128)(2,1)S(1)} %collective-permute-done.5.refs_2_) | copy-start | bytes 811012
  29.9 10.9 %collective-permute-start.7 = (bf16[528,256]{1,0:T(8,128)(2,1)S(1)}, bf16[528,256]{1,0:T(8,128)(2,1)}, u32[]{:S(2)}, u32[]{:S(2)}) collective-permute-start(bf16[528,256]{1,0:T(8,128)(2,1)S(1)} %collective-permute-done.5.refs_2_), channel_id=1, source_target_pairs={{0,8},{1,57},{8,16},{9,1},{16,24},{17,9},{24,32},{25,17},{32,40},{... | collective-permute-start | bytes 811016 | tf_op jit(solution)/shard_map/ppermute | solution.py:332
  33.3 11.7 %copy-start.13 = (bf16[528,256]{1,0:T(8,128)(2,1)}, bf16[528,256]{1,0:T(8,128)(2,1)S(1)}, u32[]{:S(2)}) copy-start(bf16[528,256]{1,0:T(8,128)(2,1)S(1)} %collective-permute-done.6.refs_3_) | copy-start | bytes 811012
  33.3 11.7 %collective-permute-start.8 = (bf16[528,256]{1,0:T(8,128)(2,1)S(1)}, bf16[528,256]{1,0:T(8,128)(2,1)}, u32[]{:S(2)}, u32[]{:S(2)}) collective-permute-start(bf16[528,256]{1,0:T(8,128)(2,1)S(1)} %collective-permute-done.6.refs_3_), channel_id=1, source_target_pairs={{0,8},{1,57},{8,16},{9,1},{16,24},{17,9},{24,32},{25,17},{32,40},{... | collective-permute-start | bytes 811016 | tf_op jit(solution)/shard_map/ppermute | solution.py:332
  36.7 22.4 %copy-start.2 = (bf16[32,64,256]{2,1,0:T(8,128)(2,1)}, bf16[32,64,256]{2,1,0:T(8,128)(2,1)S(1)}, u32[]{:S(2)}) copy-start(bf16[32,64,256]{2,1,0:T(8,128)(2,1)S(1)} %collective-permute-done.13.refs_12_) | copy-start | bytes 3145732
  36.7 16.8 %collective-permute-start.14 = (bf16[16,64,256]{2,1,0:T(8,128)(2,1)S(1)}, bf16[16,64,256]{2,1,0:T(8,128)(2,1)S(1)}, u32[]{:S(2)}, u32[]{:S(2)}) collective-permute-start(bf16[16,64,256]{2,1,0:T(8,128)(2,1)S(1)} %slice.9), channel_id=1, source_target_pairs={{0,192},{64,0},{128,64},{192,128},{1,193},{65,1},{129,65},{193,129... | collective-permute-start | bytes 1572872 | tf_op jit(solution)/shard_map/ppermute | solution.py:324
  39.8 1.0 %copy-start.3 = (bf16[32,64,256]{2,1,0:T(8,128)(2,1)}, bf16[32,64,256]{2,1,0:T(8,128)(2,1)S(1)}, u32[]{:S(2)}) copy-start(bf16[32,64,256]{2,1,0:T(8,128)(2,1)S(1)} %collective-permute-done.11.refs_9_) | copy-start | bytes 3145732
  39.8 13.8 %collective-permute-start.12 = (bf16[16,64,256]{2,1,0:T(8,128)(2,1)S(1)}, bf16[16,64,256]{2,1,0:T(8,128)(2,1)S(1)}, u32[]{:S(2)}, u32[]{:S(2)}) collective-permute-start(bf16[16,64,256]{2,1,0:T(8,128)(2,1)S(1)} %slice.8), channel_id=1, source_target_pairs={{0,64},{64,128},{128,192},{192,0},{1,65},{65,129},{129,193},{193,1... | collective-permute-start | bytes 1572872 | tf_op jit(solution)/shard_map/ppermute | solution.py:324
  40.8 7.9 %collective-permute-start.9 = (bf16[528,256]{1,0:T(8,128)(2,1)}, bf16[528,256]{1,0:T(8,128)(2,1)}, u32[]{:S(2)}, u32[]{:S(2)}) collective-permute-start(bf16[528,256]{1,0:T(8,128)(2,1)} %collective-permute-done.7.refs_4_), channel_id=1, source_target_pairs={{0,8},{1,57},{8,16},{9,1},{16,24},{17,9},{24,32},{25,17},{32,40},{... | collective-permute-start | bytes 811016 | tf_op jit(solution)/shard_map/ppermute | solution.py:332
  45.0 10.5 %collective-permute-start.10 = (bf16[528,256]{1,0:T(8,128)(2,1)}, bf16[528,256]{1,0:T(8,128)(2,1)}, u32[]{:S(2)}, u32[]{:S(2)}) collective-permute-start(bf16[528,256]{1,0:T(8,128)(2,1)} %collective-permute-done.8.refs_5_), channel_id=1, source_target_pairs={{0,8},{1,57},{8,16},{9,1},{16,24},{17,9},{24,32},{25,17},{32,40},{... | collective-permute-start | bytes 811016 | tf_op jit(solution)/shard_map/ppermute | solution.py:332
  46.3 12.8 %collective-permute-start.18 = (bf16[32,64,256]{2,1,0:T(8,128)(2,1)S(1)}, bf16[32,64,256]{2,1,0:T(8,128)(2,1)}, u32[]{:S(2)}, u32[]{:S(2)}) collective-permute-start(bf16[32,64,256]{2,1,0:T(8,128)(2,1)S(1)} %collective-permute-done.13.refs_12_), channel_id=1, source_target_pairs={{0,1},{1,0},{2,3},{3,2},{4,5},{5,4},{6,7},{7,6},{8,9},{9,8},{10,11... | collective-permute-start | bytes 3145736 | tf_op jit(solution)/shard_map/ppermute | solution.py:336
  48.7 10.5 %collective-permute-start.15 = (bf16[32,64,256]{2,1,0:T(8,128)(2,1)}, bf16[32,64,256]{2,1,0:T(8,128)(2,1)}, u32[]{:S(2)}, u32[]{:S(2)}) collective-permute-start(bf16[32,64,256]{2,1,0:T(8,128)(2,1)} %copy-done.3), channel_id=1, source_target_pairs={{0,1},{1,0},{2,3},{3,2},{4,5},{5,4},{6,7},{7,6},{8,9},{9,8},{10,11... | collective-permute-start | bytes 3145736 | tf_op jit(solution)/shard_map/ppermute | solution.py:336
  53.5 5.6 %copy-start.7 = (bf16[16,64,256]{2,1,0:T(8,128)(2,1)}, bf16[16,64,256]{2,1,0:T(8,128)(2,1)S(1)}, u32[]{:S(2)}) copy-start(bf16[16,64,256]{2,1,0:T(8,128)(2,1)S(1)} %collective-permute-done.14.refs_11_) | copy-start | bytes 1572868
  53.5 5.6 %collective-permute-start.17 = (bf16[16,64,256]{2,1,0:T(8,128)(2,1)S(1)}, bf16[16,64,256]{2,1,0:T(8,128)(2,1)S(1)}, u32[]{:S(2)}, u32[]{:S(2)}) collective-permute-start(bf16[16,64,256]{2,1,0:T(8,128)(2,1)S(1)} %collective-permute-done.14.refs_11_), channel_id=1, source_target_pairs={{0,1},{1,0},{2,3},{3,2},{4,5},{5,4},{6,7},{7,6},{8,9},{9,8},{10,11... | collective-permute-start | bytes 1572872 | tf_op jit(solution)/shard_map/ppermute | solution.py:336
  53.6 5.5 %copy-start.8 = (bf16[16,64,256]{2,1,0:T(8,128)(2,1)}, bf16[16,64,256]{2,1,0:T(8,128)(2,1)S(1)}, u32[]{:S(2)}) copy-start(bf16[16,64,256]{2,1,0:T(8,128)(2,1)S(1)} %collective-permute-done.12.refs_10_) | copy-start | bytes 1572868
  53.6 5.6 %collective-permute-start.16 = (bf16[16,64,256]{2,1,0:T(8,128)(2,1)S(1)}, bf16[16,64,256]{2,1,0:T(8,128)(2,1)S(1)}, u32[]{:S(2)}, u32[]{:S(2)}) collective-permute-start(bf16[16,64,256]{2,1,0:T(8,128)(2,1)S(1)} %collective-permute-done.12.refs_10_), channel_id=1, source_target_pairs={{0,1},{1,0},{2,3},{3,2},{4,5},{5,4},{6,7},{7,6},{8,9},{9,8},{10,11... | collective-permute-start | bytes 1572872 | tf_op jit(solution)/shard_map/ppermute | solution.py:336
  59.2 0.8 copy-start.9
  59.2 1.0 %copy-start.10 = (bf16[16,64,256]{2,1,0:T(8,128)(2,1)}, bf16[16,64,256]{2,1,0:T(8,128)(2,1)S(1)}, u32[]{:S(2)}) copy-start(bf16[16,64,256]{2,1,0:T(8,128)(2,1)S(1)} %collective-permute-done.16.refs_14_) | copy-start | bytes 1572868
  71.9 18.6 %copy-start.1 = (f32[8,64,256]{2,1,0:T(8,128)S(1)}, f32[8,64,256]{2,1,0:T(8,128)}, u32[]{:S(2)}) copy-start(f32[8,64,256]{2,1,0:T(8,128)} %get-tuple-element.41) | copy-start | bytes 1572868
  71.9 1.9 %collective-permute-start.19 = (bf16[8,64,256]{2,1,0:T(8,128)(2,1)}, bf16[8,64,256]{2,1,0:T(8,128)(2,1)S(1)}, u32[]{:S(2)}, u32[]{:S(2)}) collective-permute-start(bf16[8,64,256]{2,1,0:T(8,128)(2,1)} %get-tuple-element.36), channel_id=1, source_target_pairs={{0,1},{1,0},{2,3},{3,2},{4,5},{5,4},{6,7},{7,6},{8,9},{9,8},{10,11... | collective-permute-start | bytes 786440 | tf_op jit(solution)/shard_map/ppermute | solution.py:336
  72.5 5.7 %collective-permute-start.21 = (bf16[8,64,256]{2,1,0:T(8,128)(2,1)}, bf16[8,64,256]{2,1,0:T(8,128)(2,1)S(1)}, u32[]{:S(2)}, u32[]{:S(2)}) collective-permute-start(bf16[8,64,256]{2,1,0:T(8,128)(2,1)} %get-tuple-element.38), channel_id=1, source_target_pairs={{0,1},{1,0},{2,3},{3,2},{4,5},{5,4},{6,7},{7,6},{8,9},{9,8},{10,11... | collective-permute-start | bytes 786440 | tf_op jit(solution)/shard_map/ppermute | solution.py:336
  72.6 7.0 %collective-permute-start.23 = (bf16[8,64,256]{2,1,0:T(8,128)(2,1)}, bf16[8,64,256]{2,1,0:T(8,128)(2,1)S(1)}, u32[]{:S(2)}, u32[]{:S(2)}) collective-permute-start(bf16[8,64,256]{2,1,0:T(8,128)(2,1)} %get-tuple-element.40), channel_id=1, source_target_pairs={{0,1},{1,0},{2,3},{3,2},{4,5},{5,4},{6,7},{7,6},{8,9},{9,8},{10,11... | collective-permute-start | bytes 786440 | tf_op jit(solution)/shard_map/ppermute | solution.py:336
  73.0 10.0 %collective-permute-start.25 = (bf16[8,64,256]{2,1,0:T(8,128)(2,1)}, bf16[8,64,256]{2,1,0:T(8,128)(2,1)S(1)}, u32[]{:S(2)}, u32[]{:S(2)}) collective-permute-start(bf16[8,64,256]{2,1,0:T(8,128)(2,1)} %get-tuple-element.42), channel_id=1, source_target_pairs={{0,1},{1,0},{2,3},{3,2},{4,5},{5,4},{6,7},{7,6},{8,9},{9,8},{10,11... | collective-permute-start | bytes 786440 | tf_op jit(solution)/shard_map/ppermute | solution.py:336
  74.9 9.5 %collective-permute-start.20 = (bf16[8,64,256]{2,1,0:T(8,128)(2,1)S(1)}, bf16[8,64,256]{2,1,0:T(8,128)(2,1)S(1)}, u32[]{:S(2)}, u32[]{:S(2)}) collective-permute-start(bf16[8,64,256]{2,1,0:T(8,128)(2,1)S(1)} %add_convert_fusion.2), channel_id=1, source_target_pairs={{0,4},{2,6},{4,0},{6,2},{1,5},{3,7},{5,1},{7,3},{8,12},{10,14},{12... | collective-permute-start | bytes 786440 | tf_op jit(solution)/shard_map/ppermute | solution.py:324
  79.2 11.4 %collective-permute-start.22 = (bf16[8,64,256]{2,1,0:T(8,128)(2,1)S(1)}, bf16[8,64,256]{2,1,0:T(8,128)(2,1)S(1)}, u32[]{:S(2)}, u32[]{:S(2)}) collective-permute-start(bf16[8,64,256]{2,1,0:T(8,128)(2,1)S(1)} %add_convert_fusion.1), channel_id=1, source_target_pairs={{0,2},{2,4},{4,6},{6,0},{1,3},{3,5},{5,7},{7,1},{8,10},{10,12},{12... | collective-permute-start | bytes 786440 | tf_op jit(solution)/shard_map/ppermute | solution.py:324
  80.6 10.0 %collective-permute-start.24 = (bf16[8,64,256]{2,1,0:T(8,128)(2,1)S(1)}, bf16[8,64,256]{2,1,0:T(8,128)(2,1)S(1)}, u32[]{:S(2)}, u32[]{:S(2)}) collective-permute-start(bf16[8,64,256]{2,1,0:T(8,128)(2,1)S(1)} %add_convert_fusion), channel_id=1, source_target_pairs={{0,6},{2,0},{4,2},{6,4},{1,7},{3,1},{5,3},{7,5},{8,14},{10,8},{12,... | collective-permute-start | bytes 786440 | tf_op jit(solution)/shard_map/ppermute | solution.py:324

commit v5 on v4

--- a/solution.py
+++ b/solution.py
@@ -26,7 +26,8 @@
 SORT_COST = 20 * 10**9
 ROWS = A_DEV * QUARTER
 BLOCK = ROWS + LABELS
-TABLE_COST = 4 * 10**9
+JOIN_COST = 20 * 10**9
+TABLE_COST = 8 * 10**9
 VMEM_LIMIT = 56 * 1024 * 1024
 BF16 = jnp.bfloat16
 F32 = jnp.float32
@@ -126,6 +127,7 @@
         out_shape=jax.ShapeDtypeStruct((BLOCK, TILE), BF16),
         in_specs=[VMEM] * (N_REP + 1),
         out_specs=VMEM,
+        cost_estimate=pl.CostEstimate(flops=JOIN_COST, bytes_accessed=1 << 19, transcendentals=0),
         name="join_k",
     )(table, *parts)
 
@@ -356,8 +358,8 @@
     half = lax.dynamic_slice_in_dim(integrals, core * HALF, HALF, 0)
     table = product_table(x[None], a_index, b_index, live, owner, target)
     parts = [pieces[0]] + [shift_by(pieces[s], "rep", N_REP, s) for s in range(1, N_REP)]
-    joined, half = lax.optimization_barrier((join_k(table, parts), half))
-    lefts, rights = gather(joined, half)
+    half, table = lax.optimization_barrier((half, table))
+    lefts, rights = gather(join_k(table, parts), half)
     me = jnp.stack([z, core])
     sums = products(me, sort_products(me, lefts), lefts, [integrals] + rights)
     total = None

time: 91.7 us -> 90.4 us (0.986)
  starting transfers between devices: 49.5 us -> 43.7 us
  waiting for transfers between devices: 12.5 us -> 16.5 us
    ppermute x10, waiting for transfers between devices: 7.56 us -> 11 us  [shift_by(): lax.ppermute(value, axis, [(i, (i + step) % size) for i in range(size)])]
    ppermute x9, starting transfers between devices: 11.7 us -> 8.42 us  [other_core(): return lax.ppermute(value, 'core', [(0, 1), (1, 0)])]
    ppermute x10, starting transfers between devices: 16.5 us -> 14.6 us  [shift_by(): lax.ppermute(value, axis, [(i, (i + step) % size) for i in range(size)])]
    slice x1, local copies, waits for them, and re-layouts: 0.04 us -> 1.08 us  [gather(): far_back = shift_by(back[:HALF // 2], 'rep', N_REP, 1)]
    unnamed x28 -> x26, local copies, waits for them, and re-layouts: 3.05 us -> 2.25 us
  transfers between devices with their start and end apart: 26 -> 26, of which waited for: 6 -> 8; matrix products, arithmetic and copies ran while one was open for 4% -> 6% of each run, Pallas kernels for 7% -> 9%
where the time goes in v5:
time: 90.4 us; the launch traced here: 89.4 us
  starting transfers between devices  43.7 us (48%)
  Pallas kernels  20.9 us (23%)
  waiting for transfers between devices  16.5 us (18%)
  other arithmetic  4.64 us (5%)
  local copies, waits for them, and re-layouts  3.47 us (4%)
    ppermute x7, starting transfers between devices, apart(): return lax.ppermute(value, (axis, 'core'), perm)  20.6 us
    ppermute x10, starting transfers between devices, shift_by(): lax.ppermute(value, axis, [(i, (i + step) % size) for i in range(size)])  14.6 us
    pallas_call x1, Pallas kernels, products(): pl.pallas_call(products_kernel, out_shape=[jax.ShapeDtypeStruct(shape, ki...  11.3 us
    ppermute x10, waiting for transfers between devices, shift_by(): lax.ppermute(value, axis, [(i, (i + step) % size) for i in range(size)])  11 us
    ppermute x9, starting transfers between devices, other_core(): return lax.ppermute(value, 'core', [(0, 1), (1, 0)])  8.42 us
    ppermute x7, waiting for transfers between devices, apart(): return lax.ppermute(value, (axis, 'core'), perm)  4.73 us
    pallas_call x1, Pallas kernels, sort_products(): pl.pallas_call(sort_kernel, out_shape=jax.ShapeDtypeStruct((LIST // MOST...  3.64 us
    convert_element_type x3, other arithmetic, body(): part = shift_by(part.astype(BF16), 'x', N_X, shift).astype(F32)  3.05 us
  transfers between devices with their start and end apart: 26, of which 8 were waited for; matrix products, arithmetic and copies ran while one was open for 6% of the time, Pallas kernels for 9%

profile of v5, /device:TPU:1, one launch (start us, length us, event | category | flops | bytes accessed | tf_op | source)
XLA Modules:
  0.0 89.4 jit_solution(5014259856846600296)
XLA Ops:
  0.0 1.8 %spread_rows.1 = (bf16[4,64,128]{2,1,0:T(8,128)(2,1)}, bf16[4,64,128]{2,1,0:T(8,128)(2,1)}, bf16[4,64,128]{2,1,0:T(8,128)(2,1)}, bf16[4,64,128]{2,1,0:T(8,128)(2,1)}) custom-call(s32[1]{0:T(128)} %bitcast.2.rep_ref, bf16[8,64,256]{2,1,0:T(8,128)(2,1)} %bitcast.6), custom_call_target="tpu_custom_call" | custom-call | tf_op jit(solution)/shard_map/spread_rows/pallas_call | solution.py:102
  1.8 2.1 %collective-permute-start = (bf16[4,64,128]{2,1,0:T(8,128)(2,1)}, bf16[4,64,128]{2,1,0:T(8,128)(2,1)S(1)}, u32[]{:S(2)}, u32[]{:S(2)}) collective-permute-start(bf16[4,64,128]{2,1,0:T(8,128)(2,1)} %get-tuple-element.31), channel_id=1, source_target_pairs={{0,64},{64,128},{128,192},{192,0},{1,65},{65,129},{129,193},{193,1... | collective-permute-start | bytes 196616 | tf_op jit(solution)/shard_map/ppermute | solution.py:326
  3.9 2.6 %collective-permute-start.1 = (bf16[4,64,128]{2,1,0:T(8,128)(2,1)}, bf16[4,64,128]{2,1,0:T(8,128)(2,1)S(1)}, u32[]{:S(2)}, u32[]{:S(2)}) collective-permute-start(bf16[4,64,128]{2,1,0:T(8,128)(2,1)} %get-tuple-element.32), channel_id=1, source_target_pairs={{0,128},{64,192},{128,0},{192,64},{1,129},{65,193},{129,1},{193,65... | collective-permute-start | bytes 196616 | tf_op jit(solution)/shard_map/ppermute | solution.py:326
  6.6 1.1 %collective-permute-start.2 = (bf16[4,64,128]{2,1,0:T(8,128)(2,1)}, bf16[4,64,128]{2,1,0:T(8,128)(2,1)S(1)}, u32[]{:S(2)}, u32[]{:S(2)}) collective-permute-start(bf16[4,64,128]{2,1,0:T(8,128)(2,1)} %get-tuple-element.33), channel_id=1, source_target_pairs={{0,192},{64,0},{128,64},{192,128},{1,193},{65,1},{129,65},{193,129... | collective-permute-start | bytes 196616 | tf_op jit(solution)/shard_map/ppermute | solution.py:326
  7.6 2.4 %product_table.1.table_ref = bf16[16,256]{1,0:T(8,128)(2,1)} custom-call(s32[1]{0:T(128)} %bitcast.4.x_ref, s32[384]{0:T(512)} %a_ref.1, s32[384]{0:T(512)} %b_ref.1, s32[384]{0:T(512)} %live_ref.1, s32[48]{0:T(128)} %bitcast.7, s32[48]{0:T(128)} %target_ref.1), custom_call_target="tpu_custom_call" | custom-call | flops 8000000000 | bytes 65536 | tf_op jit(solution)/shard_map/product_table/pallas_call | solution.py:78
  10.0 0.1 constant_dynamic-slice_fusion
  10.1 0.1 collective-permute-start.13
  10.2 1.5 %collective-permute-start.11 = (bf16[32,64,256]{2,1,0:T(8,128)(2,1)S(1)}, bf16[32,64,256]{2,1,0:T(8,128)(2,1)}, u32[]{:S(2)}, u32[]{:S(2)}) collective-permute-start(bf16[32,64,256]{2,1,0:T(8,128)(2,1)S(1)} %constant_dynamic-slice_fusion), channel_id=1, source_target_pairs={{0,64},{64,128},{128,192},{192,0},{1,65},{65,129},{129,193},{193,1... | collective-permute-start | bytes 3145736 | tf_op jit(solution)/shard_map/ppermute | solution.py:326
  11.7 0.0 collective-permute-done.refs_1_
  11.7 0.0 collective-permute-done.2.refs_3_
  11.7 0.6 copy-done.10
  12.3 0.0 copy-done.11
  12.3 0.6 copy-done.12
  12.9 1.8 %join_k.1.refs_0_ = bf16[528,256]{1,0:T(8,128)(2,1)} custom-call(bf16[16,256]{1,0:T(8,128)(2,1)} %product_table.1.table_ref, bf16[4,64,128]{2,1,0:T(8,128)(2,1)} %get-tuple-element.30.refs_0_, bf16[4,64,128]{2,1,0:T(8,128)(2,1)} %copy-done.10, bf16[4,64,128]{2,1,0:T(8,128)(2,1)} %copy-done.11, bf16[4,64,128]{2,1,0:T(8,128)(2,1)} %copy-done.12), custom_call_target="tpu_custom_call" | custom-call | flops 20000000000 | bytes 524288 | tf_op jit(solution)/shard_map/join_k/pallas_call | solution.py:125
  14.7 2.1 %collective-permute-start.4 = (bf16[528,256]{1,0:T(8,128)(2,1)}, bf16[528,256]{1,0:T(8,128)(2,1)S(1)}, u32[]{:S(2)}, u32[]{:S(2)}) collective-permute-start(bf16[528,256]{1,0:T(8,128)(2,1)} %join_k.1.refs_0_), channel_id=1, source_target_pairs={{0,1},{1,0},{2,3},{3,2},{4,5},{5,4},{6,7},{7,6},{8,9},{9,8},{10,11... | collective-permute-start | bytes 811016 | tf_op jit(solution)/shard_map/ppermute | solution.py:338
  16.8 5.6 %collective-permute-start.3 = (bf16[528,256]{1,0:T(8,128)(2,1)}, bf16[528,256]{1,0:T(8,128)(2,1)S(1)}, u32[]{:S(2)}, u32[]{:S(2)}) collective-permute-start(bf16[528,256]{1,0:T(8,128)(2,1)} %join_k.1.refs_0_), channel_id=1, source_target_pairs={{0,8},{1,57},{8,16},{9,1},{16,24},{17,9},{24,32},{25,17},{32,40},{... | collective-permute-start | bytes 811016 | tf_op jit(solution)/shard_map/ppermute | solution.py:334
  22.4 1.4 %collective-permute-start.5 = (bf16[528,256]{1,0:T(8,128)(2,1)S(1)}, bf16[528,256]{1,0:T(8,128)(2,1)S(1)}, u32[]{:S(2)}, u32[]{:S(2)}) collective-permute-start(bf16[528,256]{1,0:T(8,128)(2,1)S(1)} %collective-permute-done.4), channel_id=1, source_target_pairs={{0,8},{1,57},{8,16},{9,1},{16,24},{17,9},{24,32},{25,17},{32,40},{... | collective-permute-start | bytes 811016 | tf_op jit(solution)/shard_map/ppermute | solution.py:334
  23.8 2.3 %collective-permute-done.3.refs_1_ = bf16[528,256]{1,0:T(8,128)(2,1)S(1)} collective-permute-done((bf16[528,256]{1,0:T(8,128)(2,1)}, bf16[528,256]{1,0:T(8,128)(2,1)S(1)}, u32[]{:S(2)}, u32[]{:S(2)}) %collective-permute-start.3) | collective-permute-done | bytes 270368 | tf_op jit(solution)/shard_map/ppermute | solution.py:334
  26.1 3.4 %collective-permute-start.6 = (bf16[528,256]{1,0:T(8,128)(2,1)S(1)}, bf16[528,256]{1,0:T(8,128)(2,1)S(1)}, u32[]{:S(2)}, u32[]{:S(2)}) collective-permute-start(bf16[528,256]{1,0:T(8,128)(2,1)S(1)} %collective-permute-done.3.refs_1_), channel_id=1, source_target_pairs={{0,8},{1,57},{8,16},{9,1},{16,24},{17,9},{24,32},{25,17},{32,40},{... | collective-permute-start | bytes 811016 | tf_op jit(solution)/shard_map/ppermute | solution.py:334
  29.5 0.0 collective-permute-done.5.refs_2_
  29.5 2.9 %collective-permute-start.7 = (bf16[528,256]{1,0:T(8,128)(2,1)S(1)}, bf16[528,256]{1,0:T(8,128)(2,1)}, u32[]{:S(2)}, u32[]{:S(2)}) collective-permute-start(bf16[528,256]{1,0:T(8,128)(2,1)S(1)} %collective-permute-done.5.refs_2_), channel_id=1, source_target_pairs={{0,8},{1,57},{8,16},{9,1},{16,24},{17,9},{24,32},{25,17},{32,40},{... | collective-permute-start | bytes 811016 | tf_op jit(solution)/shard_map/ppermute | solution.py:334
  32.4 0.5 collective-permute-done.6.refs_3_
  32.9 3.5 %collective-permute-start.8 = (bf16[528,256]{1,0:T(8,128)(2,1)S(1)}, bf16[528,256]{1,0:T(8,128)(2,1)}, u32[]{:S(2)}, u32[]{:S(2)}) collective-permute-start(bf16[528,256]{1,0:T(8,128)(2,1)S(1)} %collective-permute-done.6.refs_3_), channel_id=1, source_target_pairs={{0,8},{1,57},{8,16},{9,1},{16,24},{17,9},{24,32},{25,17},{32,40},{... | collective-permute-start | bytes 811016 | tf_op jit(solution)/shard_map/ppermute | solution.py:334
  36.4 0.0 collective-permute-done.13.refs_12_
  36.5 0.9 collective-permute-start.14
  37.4 1.1 %slice.8 = bf16[16,64,256]{2,1,0:T(8,128)(2,1)S(1)} slice(bf16[32,64,256]{2,1,0:T(8,128)(2,1)} %collective-permute-done.11.refs_9_), slice={[0:16], [0:64], [0:256]} | slice | bytes 1048576 | tf_op jit(solution)/shard_map/slice | solution.py:349
  38.5 0.7 collective-permute-start.12
  39.2 0.0 collective-permute-done.7.refs_4_
  39.2 2.7 %collective-permute-start.9 = (bf16[528,256]{1,0:T(8,128)(2,1)}, bf16[528,256]{1,0:T(8,128)(2,1)}, u32[]{:S(2)}, u32[]{:S(2)}) collective-permute-start(bf16[528,256]{1,0:T(8,128)(2,1)} %collective-permute-done.7.refs_4_), channel_id=1, source_target_pairs={{0,8},{1,57},{8,16},{9,1},{16,24},{17,9},{24,32},{25,17},{32,40},{... | collective-permute-start | bytes 811016 | tf_op jit(solution)/shard_map/ppermute | solution.py:334
  41.9 1.2 %collective-permute-start.10 = (bf16[528,256]{1,0:T(8,128)(2,1)}, bf16[528,256]{1,0:T(8,128)(2,1)}, u32[]{:S(2)}, u32[]{:S(2)}) collective-permute-start(bf16[528,256]{1,0:T(8,128)(2,1)} %collective-permute-done.8.refs_5_), channel_id=1, source_target_pairs={{0,8},{1,57},{8,16},{9,1},{16,24},{17,9},{24,32},{25,17},{32,40},{... | collective-permute-start | bytes 811016 | tf_op jit(solution)/shard_map/ppermute | solution.py:334
  43.1 0.7 pad_add_fusion.me_ref
  43.7 0.0 collective-permute-start.18
  43.7 1.9 %collective-permute-done.9.refs_6_ = bf16[528,256]{1,0:T(8,128)(2,1)} collective-permute-done((bf16[528,256]{1,0:T(8,128)(2,1)}, bf16[528,256]{1,0:T(8,128)(2,1)}, u32[]{:S(2)}, u32[]{:S(2)}) %collective-permute-start.9) | collective-permute-done | bytes 270368 | tf_op jit(solution)/shard_map/ppermute | solution.py:334
  45.6 4.2 %collective-permute-start.15 = (bf16[32,64,256]{2,1,0:T(8,128)(2,1)}, bf16[32,64,256]{2,1,0:T(8,128)(2,1)}, u32[]{:S(2)}, u32[]{:S(2)}) collective-permute-start(bf16[32,64,256]{2,1,0:T(8,128)(2,1)} %collective-permute-done.11.refs_9_), channel_id=1, source_target_pairs={{0,1},{1,0},{2,3},{3,2},{4,5},{5,4},{6,7},{7,6},{8,9},{9,8},{10,11... | collective-permute-start | bytes 3145736 | tf_op jit(solution)/shard_map/ppermute | solution.py:338
  49.8 0.6 collective-permute-done.14.refs_11_
  50.4 0.1 collective-permute-start.17
  50.5 2.6 %collective-permute-done.12.refs_10_ = bf16[16,64,256]{2,1,0:T(8,128)(2,1)S(1)} collective-permute-done((bf16[16,64,256]{2,1,0:T(8,128)(2,1)S(1)}, bf16[16,64,256]{2,1,0:T(8,128)(2,1)S(1)}, u32[]{:S(2)}, u32[]{:S(2)}) %collective-permute-start.12) | collective-permute-done | bytes 524320 | tf_op jit(solution)/shard_map/ppermute | solution.py:326
  53.1 1.0 %collective-permute-start.16 = (bf16[16,64,256]{2,1,0:T(8,128)(2,1)S(1)}, bf16[16,64,256]{2,1,0:T(8,128)(2,1)S(1)}, u32[]{:S(2)}, u32[]{:S(2)}) collective-permute-start(bf16[16,64,256]{2,1,0:T(8,128)(2,1)S(1)} %collective-permute-done.12.refs_10_), channel_id=1, source_target_pairs={{0,1},{1,0},{2,3},{3,2},{4,5},{5,4},{6,7},{7,6},{8,9},{9,8},{10,11... | collective-permute-start | bytes 1572872 | tf_op jit(solution)/shard_map/ppermute | solution.py:338
  54.1 0.0 collective-permute-done.10.refs_7_
  54.1 3.6 %sort_products.1.listed = s32[11,128]{1,0:T(8,128)} custom-call(s32[2]{0:T(128)} %pad_add_fusion.me_ref, bf16[528,256]{1,0:T(8,128)(2,1)} %join_k.1.refs_0_, bf16[528,256]{1,0:T(8,128)(2,1)} %copy-done.7, bf16[528,256]{1,0:T(8,128)(2,1)} %copy-done.8, bf16[528,256]{1,0:T(8,128)(2,1)} %copy-done.9, bf16[528,256]{1,0:T(8,128)(2,1)} %collective-permute-done.7.refs_4_, ...), custom_call_target="tpu_custom_call" | custom-call | flops 20000000000 | bytes 65536 | tf_op jit(solution)/shard_map/sort_products/pallas_call | solution.py:211
  57.8 0.0 collective-permute-done.17.refs_15_
  57.8 0.0 collective-permute-done.18.refs_16_
  57.8 0.0 collective-permute-done.15.refs_13_
  57.8 0.7 copy-done.5
  58.6 0.2 copy-done.6
  58.8 11.3 %products.1 = (bf16[8,64,256]{2,1,0:T(8,128)(2,1)}, bf16[8,64,256]{2,1,0:T(8,128)(2,1)}, bf16[8,64,256]{2,1,0:T(8,128)(2,1)}, bf16[8,64,256]{2,1,0:T(8,128)(2,1)...) custom-call(s32[2]{0:T(128)} %pad_add_fusion.me_ref, ...), custom_call_target="tpu_custom_call" | custom-call | flops 3221225472 | bytes 10485760 | tf_op jit(solution)/shard_map/products/pallas_call | solution.py:305
  70.1 0.1 collective-permute-start.19
  70.2 0.5 collective-permute-start.21
  70.7 0.1 collective-permute-start.23
  70.8 0.4 collective-permute-start.25
  71.2 0.7 collective-permute-done.19
  72.0 1.0 %add_convert_fusion.2 = bf16[8,64,256]{2,1,0:T(8,128)(2,1)S(1)} fusion(bf16[8,64,256]{2,1,0:T(8,128)(2,1)S(1)} %collective-permute-done.19, bf16[8,64,256]{2,1,0:T(8,128)(2,1)} %get-tuple-element.35), kind=kLoop, calls=%fused_computation.3 | loop fusion | flops 524288 | bytes 786432 | tf_op jit(solution)/shard_map/convert_element_type | solution.py:369
  73.0 2.8 %collective-permute-start.20 = (bf16[8,64,256]{2,1,0:T(8,128)(2,1)S(1)}, bf16[8,64,256]{2,1,0:T(8,128)(2,1)S(1)}, u32[]{:S(2)}, u32[]{:S(2)}) collective-permute-start(bf16[8,64,256]{2,1,0:T(8,128)(2,1)S(1)} %add_convert_fusion.2), channel_id=1, source_target_pairs={{0,4},{2,6},{4,0},{6,2},{1,5},{3,7},{5,1},{7,3},{8,12},{10,14},{12... | collective-permute-start | bytes 786440 | tf_op jit(solution)/shard_map/ppermute | solution.py:326
  75.8 0.0 collective-permute-done.21
  75.8 1.0 %add_convert_fusion.1 = bf16[8,64,256]{2,1,0:T(8,128)(2,1)S(1)} fusion(bf16[8,64,256]{2,1,0:T(8,128)(2,1)S(1)} %collective-permute-done.21, bf16[8,64,256]{2,1,0:T(8,128)(2,1)} %get-tuple-element.37), kind=kLoop, calls=%fused_computation.2 | loop fusion | flops 524288 | bytes 786432 | tf_op jit(solution)/shard_map/convert_element_type | solution.py:369
  76.9 0.4 collective-permute-start.22
  77.3 0.0 collective-permute-done.23
  77.3 1.0 %add_convert_fusion = bf16[8,64,256]{2,1,0:T(8,128)(2,1)S(1)} fusion(bf16[8,64,256]{2,1,0:T(8,128)(2,1)S(1)} %collective-permute-done.23, bf16[8,64,256]{2,1,0:T(8,128)(2,1)} %get-tuple-element.39), kind=kLoop, calls=%fused_computation.1 | loop fusion | flops 524288 | bytes 786432 | tf_op jit(solution)/shard_map/convert_element_type | solution.py:369
  78.3 2.4 %collective-permute-start.24 = (bf16[8,64,256]{2,1,0:T(8,128)(2,1)S(1)}, bf16[8,64,256]{2,1,0:T(8,128)(2,1)S(1)}, u32[]{:S(2)}, u32[]{:S(2)}) collective-permute-start(bf16[8,64,256]{2,1,0:T(8,128)(2,1)S(1)} %add_convert_fusion), channel_id=1, source_target_pairs={{0,6},{2,0},{4,2},{6,4},{1,7},{3,1},{5,3},{7,5},{8,14},{10,8},{12,... | collective-permute-start | bytes 786440 | tf_op jit(solution)/shard_map/ppermute | solution.py:326
  80.7 0.0 collective-permute-done.25
  80.7 1.6 %collective-permute-done.20 = bf16[8,64,256]{2,1,0:T(8,128)(2,1)S(1)} collective-permute-done((bf16[8,64,256]{2,1,0:T(8,128)(2,1)S(1)}, bf16[8,64,256]{2,1,0:T(8,128)(2,1)S(1)}, u32[]{:S(2)}, u32[]{:S(2)}) %collective-permute-start.20) | collective-permute-done | bytes 262176 | tf_op jit(solution)/shard_map/ppermute | solution.py:326
  82.3 6.1 %collective-permute-done.22 = bf16[8,64,256]{2,1,0:T(8,128)(2,1)S(1)} collective-permute-done((bf16[8,64,256]{2,1,0:T(8,128)(2,1)S(1)}, bf16[8,64,256]{2,1,0:T(8,128)(2,1)S(1)}, u32[]{:S(2)}, u32[]{:S(2)}) %collective-permute-start.22) | collective-permute-done | bytes 262176 | tf_op jit(solution)/shard_map/ppermute | solution.py:326
  88.4 0.0 collective-permute-done.24
  88.4 0.9 %add_add_fusion = f32[8,64,256]{2,1,0:T(8,128)} fusion(f32[8,64,256]{2,1,0:T(8,128)S(1)} %copy-done.1, bf16[8,64,256]{2,1,0:T(8,128)(2,1)S(1)} %collective-permute-done.25, bf16[8,64,256]{2,1,0:T(8,128)(2,1)S(1)} %collective-permute-done.24, bf16[8,64,256]{2,1,0:T(8,128)(2,1)S(1)} %collective-permute-done.22, bf16[8,64,256]{2,1,0:T(8,128)(2,1)S(1)} %collective-permute-done.20), kind=kLoop, calls=%fused_computation | loop fusion | flops 1048576 | bytes 2097152 | tf_op jit(solution)/shard_map/add | solution.py:370
  (27 shorter events, 0.1 us)
Async XLA Ops:
  1.8 9.9 %collective-permute-start = (bf16[4,64,128]{2,1,0:T(8,128)(2,1)}, bf16[4,64,128]{2,1,0:T(8,128)(2,1)S(1)}, u32[]{:S(2)}, u32[]{:S(2)}) collective-permute-start(bf16[4,64,128]{2,1,0:T(8,128)(2,1)} %get-tuple-element.31), channel_id=1, source_target_pairs={{0,64},{64,128},{128,192},{192,0},{1,65},{65,129},{129,193},{193,1... | collective-permute-start | bytes 196616 | tf_op jit(solution)/shard_map/ppermute | solution.py:326
  3.9 7.7 %collective-permute-start.1 = (bf16[4,64,128]{2,1,0:T(8,128)(2,1)}, bf16[4,64,128]{2,1,0:T(8,128)(2,1)S(1)}, u32[]{:S(2)}, u32[]{:S(2)}) collective-permute-start(bf16[4,64,128]{2,1,0:T(8,128)(2,1)} %get-tuple-element.32), channel_id=1, source_target_pairs={{0,128},{64,192},{128,0},{192,64},{1,129},{65,193},{129,1},{193,65... | collective-permute-start | bytes 196616 | tf_op jit(solution)/shard_map/ppermute | solution.py:326
  6.6 5.1 %collective-permute-start.2 = (bf16[4,64,128]{2,1,0:T(8,128)(2,1)}, bf16[4,64,128]{2,1,0:T(8,128)(2,1)S(1)}, u32[]{:S(2)}, u32[]{:S(2)}) collective-permute-start(bf16[4,64,128]{2,1,0:T(8,128)(2,1)} %get-tuple-element.33), channel_id=1, source_target_pairs={{0,192},{64,0},{128,64},{192,128},{1,193},{65,1},{129,65},{193,129... | collective-permute-start | bytes 196616 | tf_op jit(solution)/shard_map/ppermute | solution.py:326
  7.6 2.4 %copy-start = (bf16[64,64,256]{2,1,0:T(8,128)(2,1)S(1)}, bf16[64,64,256]{2,1,0:T(8,128)(2,1)}, u32[]{:S(2)}) copy-start(bf16[64,64,256]{2,1,0:T(8,128)(2,1)} %refs_8_.1) | copy-start | bytes 6291460
  10.1 26.3 %collective-permute-start.13 = (bf16[32,64,256]{2,1,0:T(8,128)(2,1)S(1)}, bf16[32,64,256]{2,1,0:T(8,128)(2,1)S(1)}, u32[]{:S(2)}, u32[]{:S(2)}) collective-permute-start(bf16[32,64,256]{2,1,0:T(8,128)(2,1)S(1)} %constant_dynamic-slice_fusion), channel_id=1, source_target_pairs={{0,192},{64,0},{128,64},{192,128},{1,193},{65,1},{129,65},{193,129... | collective-permute-start | bytes 3145736 | tf_op jit(solution)/shard_map/ppermute | solution.py:326
  10.2 27.2 %collective-permute-start.11 = (bf16[32,64,256]{2,1,0:T(8,128)(2,1)S(1)}, bf16[32,64,256]{2,1,0:T(8,128)(2,1)}, u32[]{:S(2)}, u32[]{:S(2)}) collective-permute-start(bf16[32,64,256]{2,1,0:T(8,128)(2,1)S(1)} %constant_dynamic-slice_fusion), channel_id=1, source_target_pairs={{0,64},{64,128},{128,192},{192,0},{1,65},{65,129},{129,193},{193,1... | collective-permute-start | bytes 3145736 | tf_op jit(solution)/shard_map/ppermute | solution.py:326
  11.7 0.6 copy-start.10
  11.7 0.6 copy-start.11
  12.3 0.6 copy-start.12
  14.7 7.7 %collective-permute-start.4 = (bf16[528,256]{1,0:T(8,128)(2,1)}, bf16[528,256]{1,0:T(8,128)(2,1)S(1)}, u32[]{:S(2)}, u32[]{:S(2)}) collective-permute-start(bf16[528,256]{1,0:T(8,128)(2,1)} %join_k.1.refs_0_), channel_id=1, source_target_pairs={{0,1},{1,0},{2,3},{3,2},{4,5},{5,4},{6,7},{7,6},{8,9},{9,8},{10,11... | collective-permute-start | bytes 811016 | tf_op jit(solution)/shard_map/ppermute | solution.py:338
  16.8 9.3 %collective-permute-start.3 = (bf16[528,256]{1,0:T(8,128)(2,1)}, bf16[528,256]{1,0:T(8,128)(2,1)S(1)}, u32[]{:S(2)}, u32[]{:S(2)}) collective-permute-start(bf16[528,256]{1,0:T(8,128)(2,1)} %join_k.1.refs_0_), channel_id=1, source_target_pairs={{0,8},{1,57},{8,16},{9,1},{16,24},{17,9},{24,32},{25,17},{32,40},{... | collective-permute-start | bytes 811016 | tf_op jit(solution)/shard_map/ppermute | solution.py:334
  22.4 7.1 %collective-permute-start.5 = (bf16[528,256]{1,0:T(8,128)(2,1)S(1)}, bf16[528,256]{1,0:T(8,128)(2,1)S(1)}, u32[]{:S(2)}, u32[]{:S(2)}) collective-permute-start(bf16[528,256]{1,0:T(8,128)(2,1)S(1)} %collective-permute-done.4), channel_id=1, source_target_pairs={{0,8},{1,57},{8,16},{9,1},{16,24},{17,9},{24,32},{25,17},{32,40},{... | collective-permute-start | bytes 811016 | tf_op jit(solution)/shard_map/ppermute | solution.py:334
  26.1 28.0 %copy-start.7 = (bf16[528,256]{1,0:T(8,128)(2,1)}, bf16[528,256]{1,0:T(8,128)(2,1)S(1)}, u32[]{:S(2)}) copy-start(bf16[528,256]{1,0:T(8,128)(2,1)S(1)} %collective-permute-done.3.refs_1_) | copy-start | bytes 811012
  26.1 6.8 %collective-permute-start.6 = (bf16[528,256]{1,0:T(8,128)(2,1)S(1)}, bf16[528,256]{1,0:T(8,128)(2,1)S(1)}, u32[]{:S(2)}, u32[]{:S(2)}) collective-permute-start(bf16[528,256]{1,0:T(8,128)(2,1)S(1)} %collective-permute-done.3.refs_1_), channel_id=1, source_target_pairs={{0,8},{1,57},{8,16},{9,1},{16,24},{17,9},{24,32},{25,17},{32,40},{... | collective-permute-start | bytes 811016 | tf_op jit(solution)/shard_map/ppermute | solution.py:334
  29.5 9.7 %copy-start.8 = (bf16[528,256]{1,0:T(8,128)(2,1)}, bf16[528,256]{1,0:T(8,128)(2,1)S(1)}, u32[]{:S(2)}) copy-start(bf16[528,256]{1,0:T(8,128)(2,1)S(1)} %collective-permute-done.5.refs_2_) | copy-start | bytes 811012
  29.5 9.7 %collective-permute-start.7 = (bf16[528,256]{1,0:T(8,128)(2,1)S(1)}, bf16[528,256]{1,0:T(8,128)(2,1)}, u32[]{:S(2)}, u32[]{:S(2)}) collective-permute-start(bf16[528,256]{1,0:T(8,128)(2,1)S(1)} %collective-permute-done.5.refs_2_), channel_id=1, source_target_pairs={{0,8},{1,57},{8,16},{9,1},{16,24},{17,9},{24,32},{25,17},{32,40},{... | collective-permute-start | bytes 811016 | tf_op jit(solution)/shard_map/ppermute | solution.py:334
  32.9 6.3 %copy-start.9 = (bf16[528,256]{1,0:T(8,128)(2,1)}, bf16[528,256]{1,0:T(8,128)(2,1)S(1)}, u32[]{:S(2)}) copy-start(bf16[528,256]{1,0:T(8,128)(2,1)S(1)} %collective-permute-done.6.refs_3_) | copy-start | bytes 811012
  32.9 9.0 %collective-permute-start.8 = (bf16[528,256]{1,0:T(8,128)(2,1)S(1)}, bf16[528,256]{1,0:T(8,128)(2,1)}, u32[]{:S(2)}, u32[]{:S(2)}) collective-permute-start(bf16[528,256]{1,0:T(8,128)(2,1)S(1)} %collective-permute-done.6.refs_3_), channel_id=1, source_target_pairs={{0,8},{1,57},{8,16},{9,1},{16,24},{17,9},{24,32},{25,17},{32,40},{... | collective-permute-start | bytes 811016 | tf_op jit(solution)/shard_map/ppermute | solution.py:334
  36.4 21.3 %copy-start.2 = (bf16[32,64,256]{2,1,0:T(8,128)(2,1)}, bf16[32,64,256]{2,1,0:T(8,128)(2,1)S(1)}, u32[]{:S(2)}) copy-start(bf16[32,64,256]{2,1,0:T(8,128)(2,1)S(1)} %collective-permute-done.13.refs_12_) | copy-start | bytes 3145732
  36.5 13.9 %collective-permute-start.14 = (bf16[16,64,256]{2,1,0:T(8,128)(2,1)S(1)}, bf16[16,64,256]{2,1,0:T(8,128)(2,1)S(1)}, u32[]{:S(2)}, u32[]{:S(2)}) collective-permute-start(bf16[16,64,256]{2,1,0:T(8,128)(2,1)S(1)} %slice.9), channel_id=1, source_target_pairs={{0,192},{64,0},{128,64},{192,128},{1,193},{65,1},{129,65},{193,129... | collective-permute-start | bytes 1572872 | tf_op jit(solution)/shard_map/ppermute | solution.py:326
  38.5 14.6 %collective-permute-start.12 = (bf16[16,64,256]{2,1,0:T(8,128)(2,1)S(1)}, bf16[16,64,256]{2,1,0:T(8,128)(2,1)S(1)}, u32[]{:S(2)}, u32[]{:S(2)}) collective-permute-start(bf16[16,64,256]{2,1,0:T(8,128)(2,1)S(1)} %slice.8), channel_id=1, source_target_pairs={{0,64},{64,128},{128,192},{192,0},{1,65},{65,129},{129,193},{193,1... | collective-permute-start | bytes 1572872 | tf_op jit(solution)/shard_map/ppermute | solution.py:326
  39.2 6.4 %collective-permute-start.9 = (bf16[528,256]{1,0:T(8,128)(2,1)}, bf16[528,256]{1,0:T(8,128)(2,1)}, u32[]{:S(2)}, u32[]{:S(2)}) collective-permute-start(bf16[528,256]{1,0:T(8,128)(2,1)} %collective-permute-done.7.refs_4_), channel_id=1, source_target_pairs={{0,8},{1,57},{8,16},{9,1},{16,24},{17,9},{24,32},{25,17},{32,40},{... | collective-permute-start | bytes 811016 | tf_op jit(solution)/shard_map/ppermute | solution.py:334
  41.9 12.2 %collective-permute-start.10 = (bf16[528,256]{1,0:T(8,128)(2,1)}, bf16[528,256]{1,0:T(8,128)(2,1)}, u32[]{:S(2)}, u32[]{:S(2)}) collective-permute-start(bf16[528,256]{1,0:T(8,128)(2,1)} %collective-permute-done.8.refs_5_), channel_id=1, source_target_pairs={{0,8},{1,57},{8,16},{9,1},{16,24},{17,9},{24,32},{25,17},{32,40},{... | collective-permute-start | bytes 811016 | tf_op jit(solution)/shard_map/ppermute | solution.py:334
  43.7 14.1 %collective-permute-start.18 = (bf16[32,64,256]{2,1,0:T(8,128)(2,1)S(1)}, bf16[32,64,256]{2,1,0:T(8,128)(2,1)}, u32[]{:S(2)}, u32[]{:S(2)}) collective-permute-start(bf16[32,64,256]{2,1,0:T(8,128)(2,1)S(1)} %collective-permute-done.13.refs_12_), channel_id=1, source_target_pairs={{0,1},{1,0},{2,3},{3,2},{4,5},{5,4},{6,7},{7,6},{8,9},{9,8},{10,11... | collective-permute-start | bytes 3145736 | tf_op jit(solution)/shard_map/ppermute | solution.py:338
  45.6 12.2 %collective-permute-start.15 = (bf16[32,64,256]{2,1,0:T(8,128)(2,1)}, bf16[32,64,256]{2,1,0:T(8,128)(2,1)}, u32[]{:S(2)}, u32[]{:S(2)}) collective-permute-start(bf16[32,64,256]{2,1,0:T(8,128)(2,1)} %collective-permute-done.11.refs_9_), channel_id=1, source_target_pairs={{0,1},{1,0},{2,3},{3,2},{4,5},{5,4},{6,7},{7,6},{8,9},{9,8},{10,11... | collective-permute-start | bytes 3145736 | tf_op jit(solution)/shard_map/ppermute | solution.py:338
  50.4 7.4 %copy-start.3 = (bf16[16,64,256]{2,1,0:T(8,128)(2,1)}, bf16[16,64,256]{2,1,0:T(8,128)(2,1)S(1)}, u32[]{:S(2)}) copy-start(bf16[16,64,256]{2,1,0:T(8,128)(2,1)S(1)} %collective-permute-done.14.refs_11_) | copy-start | bytes 1572868
  50.4 7.4 %collective-permute-start.17 = (bf16[16,64,256]{2,1,0:T(8,128)(2,1)S(1)}, bf16[16,64,256]{2,1,0:T(8,128)(2,1)S(1)}, u32[]{:S(2)}, u32[]{:S(2)}) collective-permute-start(bf16[16,64,256]{2,1,0:T(8,128)(2,1)S(1)} %collective-permute-done.14.refs_11_), channel_id=1, source_target_pairs={{0,1},{1,0},{2,3},{3,2},{4,5},{5,4},{6,7},{7,6},{8,9},{9,8},{10,11... | collective-permute-start | bytes 1572872 | tf_op jit(solution)/shard_map/ppermute | solution.py:338
  53.1 4.7 %copy-start.4 = (bf16[16,64,256]{2,1,0:T(8,128)(2,1)}, bf16[16,64,256]{2,1,0:T(8,128)(2,1)S(1)}, u32[]{:S(2)}) copy-start(bf16[16,64,256]{2,1,0:T(8,128)(2,1)S(1)} %collective-permute-done.12.refs_10_) | copy-start | bytes 1572868
  53.1 4.7 %collective-permute-start.16 = (bf16[16,64,256]{2,1,0:T(8,128)(2,1)S(1)}, bf16[16,64,256]{2,1,0:T(8,128)(2,1)S(1)}, u32[]{:S(2)}, u32[]{:S(2)}) collective-permute-start(bf16[16,64,256]{2,1,0:T(8,128)(2,1)S(1)} %collective-permute-done.12.refs_10_), channel_id=1, source_target_pairs={{0,1},{1,0},{2,3},{3,2},{4,5},{5,4},{6,7},{7,6},{8,9},{9,8},{10,11... | collective-permute-start | bytes 1572872 | tf_op jit(solution)/shard_map/ppermute | solution.py:338
  57.8 0.8 copy-start.5
  57.8 1.0 %copy-start.6 = (bf16[16,64,256]{2,1,0:T(8,128)(2,1)}, bf16[16,64,256]{2,1,0:T(8,128)(2,1)S(1)}, u32[]{:S(2)}) copy-start(bf16[16,64,256]{2,1,0:T(8,128)(2,1)S(1)} %collective-permute-done.16.refs_14_) | copy-start | bytes 1572868
  70.1 18.3 %copy-start.1 = (f32[8,64,256]{2,1,0:T(8,128)S(1)}, f32[8,64,256]{2,1,0:T(8,128)}, u32[]{:S(2)}) copy-start(f32[8,64,256]{2,1,0:T(8,128)} %get-tuple-element.41) | copy-start | bytes 1572868
  70.1 1.8 %collective-permute-start.19 = (bf16[8,64,256]{2,1,0:T(8,128)(2,1)}, bf16[8,64,256]{2,1,0:T(8,128)(2,1)S(1)}, u32[]{:S(2)}, u32[]{:S(2)}) collective-permute-start(bf16[8,64,256]{2,1,0:T(8,128)(2,1)} %get-tuple-element.36), channel_id=1, source_target_pairs={{0,1},{1,0},{2,3},{3,2},{4,5},{5,4},{6,7},{7,6},{8,9},{9,8},{10,11... | collective-permute-start | bytes 786440 | tf_op jit(solution)/shard_map/ppermute | solution.py:338
  70.2 5.6 %collective-permute-start.21 = (bf16[8,64,256]{2,1,0:T(8,128)(2,1)}, bf16[8,64,256]{2,1,0:T(8,128)(2,1)S(1)}, u32[]{:S(2)}, u32[]{:S(2)}) collective-permute-start(bf16[8,64,256]{2,1,0:T(8,128)(2,1)} %get-tuple-element.38), channel_id=1, source_target_pairs={{0,1},{1,0},{2,3},{3,2},{4,5},{5,4},{6,7},{7,6},{8,9},{9,8},{10,11... | collective-permute-start | bytes 786440 | tf_op jit(solution)/shard_map/ppermute | solution.py:338
  70.7 6.5 %collective-permute-start.23 = (bf16[8,64,256]{2,1,0:T(8,128)(2,1)}, bf16[8,64,256]{2,1,0:T(8,128)(2,1)S(1)}, u32[]{:S(2)}, u32[]{:S(2)}) collective-permute-start(bf16[8,64,256]{2,1,0:T(8,128)(2,1)} %get-tuple-element.40), channel_id=1, source_target_pairs={{0,1},{1,0},{2,3},{3,2},{4,5},{5,4},{6,7},{7,6},{8,9},{9,8},{10,11... | collective-permute-start | bytes 786440 | tf_op jit(solution)/shard_map/ppermute | solution.py:338
  70.8 9.9 %collective-permute-start.25 = (bf16[8,64,256]{2,1,0:T(8,128)(2,1)}, bf16[8,64,256]{2,1,0:T(8,128)(2,1)S(1)}, u32[]{:S(2)}, u32[]{:S(2)}) collective-permute-start(bf16[8,64,256]{2,1,0:T(8,128)(2,1)} %get-tuple-element.42), channel_id=1, source_target_pairs={{0,1},{1,0},{2,3},{3,2},{4,5},{5,4},{6,7},{7,6},{8,9},{9,8},{10,11... | collective-permute-start | bytes 786440 | tf_op jit(solution)/shard_map/ppermute | solution.py:338
  73.0 9.4 %collective-permute-start.20 = (bf16[8,64,256]{2,1,0:T(8,128)(2,1)S(1)}, bf16[8,64,256]{2,1,0:T(8,128)(2,1)S(1)}, u32[]{:S(2)}, u32[]{:S(2)}) collective-permute-start(bf16[8,64,256]{2,1,0:T(8,128)(2,1)S(1)} %add_convert_fusion.2), channel_id=1, source_target_pairs={{0,4},{2,6},{4,0},{6,2},{1,5},{3,7},{5,1},{7,3},{8,12},{10,14},{12... | collective-permute-start | bytes 786440 | tf_op jit(solution)/shard_map/ppermute | solution.py:326
  76.9 11.6 %collective-permute-start.22 = (bf16[8,64,256]{2,1,0:T(8,128)(2,1)S(1)}, bf16[8,64,256]{2,1,0:T(8,128)(2,1)S(1)}, u32[]{:S(2)}, u32[]{:S(2)}) collective-permute-start(bf16[8,64,256]{2,1,0:T(8,128)(2,1)S(1)} %add_convert_fusion.1), channel_id=1, source_target_pairs={{0,2},{2,4},{4,6},{6,0},{1,3},{3,5},{5,7},{7,1},{8,10},{10,12},{12... | collective-permute-start | bytes 786440 | tf_op jit(solution)/shard_map/ppermute | solution.py:326
  78.3 10.2 %collective-permute-start.24 = (bf16[8,64,256]{2,1,0:T(8,128)(2,1)S(1)}, bf16[8,64,256]{2,1,0:T(8,128)(2,1)S(1)}, u32[]{:S(2)}, u32[]{:S(2)}) collective-permute-start(bf16[8,64,256]{2,1,0:T(8,128)(2,1)S(1)} %add_convert_fusion), channel_id=1, source_target_pairs={{0,6},{2,0},{4,2},{6,4},{1,7},{3,1},{5,3},{7,5},{8,14},{10,8},{12,... | collective-permute-start | bytes 786440 | tf_op jit(solution)/shard_map/ppermute | solution.py:326

commit v6 on v5

--- a/solution.py
+++ b/solution.py
@@ -20,7 +20,7 @@
 LABELS = 2 * N_Z
 SPOTS = N_X * OWN_DEV
 GROUP = 4
-WIDE = 8
+WIDE = 16
 LIST = 1280
 NOWHERE = 2.0 * SPOTS * 4096
 SORT_COST = 20 * 10**9
@@ -28,7 +28,7 @@
 BLOCK = ROWS + LABELS
 JOIN_COST = 20 * 10**9
 TABLE_COST = 8 * 10**9
-VMEM_LIMIT = 56 * 1024 * 1024
+VMEM_LIMIT = 52 * 1024 * 1024
 BF16 = jnp.bfloat16
 F32 = jnp.float32
 I32 = jnp.int32
@@ -268,8 +268,8 @@
         for w in range(WIDE):
             spots, rows = [], []
             for u in range(GROUP):
-                at = (i % 4) * GROUP * WIDE + w * GROUP + u
-                code = listed[i // 4, at]
+                at = (i % 2) * GROUP * WIDE + w * GROUP + u
+                code = listed[i // 2, at]
                 first = pl.multiple_of(((code >> 6) & 7) * QUARTER, QUARTER)
                 rows.append(left[(code >> 9) & 7, pl.ds(first, QUARTER), :])
                 spots.append(code >> 12)

time: 90.4 us -> 88.7 us (0.981)
  other arithmetic: 4.64 us -> 1.82 us
  Pallas kernels: 20.9 us -> 18.5 us
  waiting for transfers between devices: 16.5 us -> 18.2 us
    convert_element_type x3, other arithmetic: 3.05 us -> 0.21 us  [body(): part = shift_by(part.astype(BF16), 'x', N_X, shift).astype(F32)]
    pallas_call x1, Pallas kernels: 11.3 us -> 8.84 us  [products(): pl.pallas_call(products_kernel, out_shape=[jax.ShapeDtypeStruct(shape, ki...]
    ppermute x10, waiting for transfers between devices: 11 us -> 12.9 us  [shift_by(): lax.ppermute(value, axis, [(i, (i + step) % size) for i in range(size)])]
    unnamed x26 -> x30, local copies, waits for them, and re-layouts: 2.25 us -> 2.94 us
  transfers between devices with their start and end apart: 26 -> 26, of which waited for: 8 -> 9; matrix products, arithmetic and copies ran while one was open for 6% -> 2% of each run, Pallas kernels for 9% -> 9%
where the time goes in v6:
time: 88.7 us; the launch traced here: 87.2 us
  starting transfers between devices  44.4 us (50%)
  Pallas kernels  18.5 us (21%)
  waiting for transfers between devices  18.2 us (21%)
  local copies, waits for them, and re-layouts  4.16 us (5%)
  other arithmetic  1.82 us (2%)
    ppermute x7, starting transfers between devices, apart(): return lax.ppermute(value, (axis, 'core'), perm)  20.6 us
    ppermute x10, starting transfers between devices, shift_by(): lax.ppermute(value, axis, [(i, (i + step) % size) for i in range(size)])  15 us
    ppermute x10, waiting for transfers between devices, shift_by(): lax.ppermute(value, axis, [(i, (i + step) % size) for i in range(size)])  12.9 us
    pallas_call x1, Pallas kernels, products(): pl.pallas_call(products_kernel, out_shape=[jax.ShapeDtypeStruct(shape, ki...  8.84 us
    ppermute x9, starting transfers between devices, other_core(): return lax.ppermute(value, 'core', [(0, 1), (1, 0)])  8.74 us
    ppermute x7, waiting for transfers between devices, apart(): return lax.ppermute(value, (axis, 'core'), perm)  4.73 us
    pallas_call x1, Pallas kernels, sort_products(): pl.pallas_call(sort_kernel, out_shape=jax.ShapeDtypeStruct((LIST // MOST...  3.64 us
    unnamed x30, local copies, waits for them, and re-layouts  2.94 us
  transfers between devices with their start and end apart: 26, of which 9 were waited for; matrix products, arithmetic and copies ran while one was open for 2% of the time, Pallas kernels for 9%

profile of v6, /device:TPU:1, one launch (start us, length us, event | category | flops | bytes accessed | tf_op | source)
XLA Modules:
  0.0 87.2 jit_solution(7595016773342161607)
XLA Ops:
  0.0 1.8 %spread_rows.1 = (bf16[4,64,128]{2,1,0:T(8,128)(2,1)}, bf16[4,64,128]{2,1,0:T(8,128)(2,1)}, bf16[4,64,128]{2,1,0:T(8,128)(2,1)}, bf16[4,64,128]{2,1,0:T(8,128)(2,1)}) custom-call(s32[1]{0:T(128)} %bitcast.2.rep_ref, bf16[8,64,256]{2,1,0:T(8,128)(2,1)} %bitcast.6), custom_call_target="tpu_custom_call" | custom-call | tf_op jit(solution)/shard_map/spread_rows/pallas_call | solution.py:102
  1.8 2.1 %collective-permute-start = (bf16[4,64,128]{2,1,0:T(8,128)(2,1)}, bf16[4,64,128]{2,1,0:T(8,128)(2,1)S(1)}, u32[]{:S(2)}, u32[]{:S(2)}) collective-permute-start(bf16[4,64,128]{2,1,0:T(8,128)(2,1)} %get-tuple-element.31), channel_id=1, source_target_pairs={{0,64},{64,128},{128,192},{192,0},{1,65},{65,129},{129,193},{193,1... | collective-permute-start | bytes 196616 | tf_op jit(solution)/shard_map/ppermute | solution.py:326
  3.9 2.6 %collective-permute-start.1 = (bf16[4,64,128]{2,1,0:T(8,128)(2,1)}, bf16[4,64,128]{2,1,0:T(8,128)(2,1)S(1)}, u32[]{:S(2)}, u32[]{:S(2)}) collective-permute-start(bf16[4,64,128]{2,1,0:T(8,128)(2,1)} %get-tuple-element.32), channel_id=1, source_target_pairs={{0,128},{64,192},{128,0},{192,64},{1,129},{65,193},{129,1},{193,65... | collective-permute-start | bytes 196616 | tf_op jit(solution)/shard_map/ppermute | solution.py:326
  6.6 1.1 %collective-permute-start.2 = (bf16[4,64,128]{2,1,0:T(8,128)(2,1)}, bf16[4,64,128]{2,1,0:T(8,128)(2,1)S(1)}, u32[]{:S(2)}, u32[]{:S(2)}) collective-permute-start(bf16[4,64,128]{2,1,0:T(8,128)(2,1)} %get-tuple-element.33), channel_id=1, source_target_pairs={{0,192},{64,0},{128,64},{192,128},{1,193},{65,1},{129,65},{193,129... | collective-permute-start | bytes 196616 | tf_op jit(solution)/shard_map/ppermute | solution.py:326
  7.6 2.4 %product_table.1.table_ref = bf16[16,256]{1,0:T(8,128)(2,1)} custom-call(s32[1]{0:T(128)} %bitcast.4.x_ref, s32[384]{0:T(512)} %a_ref.1, s32[384]{0:T(512)} %b_ref.1, s32[384]{0:T(512)} %live_ref.1, s32[48]{0:T(128)} %bitcast.7, s32[48]{0:T(128)} %target_ref.1), custom_call_target="tpu_custom_call" | custom-call | flops 8000000000 | bytes 65536 | tf_op jit(solution)/shard_map/product_table/pallas_call | solution.py:78
  10.0 0.1 constant_dynamic-slice_fusion
  10.1 0.1 collective-permute-start.13
  10.2 1.5 %collective-permute-start.11 = (bf16[32,64,256]{2,1,0:T(8,128)(2,1)S(1)}, bf16[32,64,256]{2,1,0:T(8,128)(2,1)}, u32[]{:S(2)}, u32[]{:S(2)}) collective-permute-start(bf16[32,64,256]{2,1,0:T(8,128)(2,1)S(1)} %constant_dynamic-slice_fusion), channel_id=1, source_target_pairs={{0,64},{64,128},{128,192},{192,0},{1,65},{65,129},{129,193},{193,1... | collective-permute-start | bytes 3145736 | tf_op jit(solution)/shard_map/ppermute | solution.py:326
  11.7 0.0 collective-permute-done.refs_1_
  11.7 0.0 collective-permute-done.1.refs_2_
  11.7 0.0 collective-permute-done.2.refs_3_
  11.7 0.6 copy-done.12
  12.3 0.0 copy-done.13
  12.3 0.6 copy-done.14
  12.9 1.8 %join_k.1.refs_0_ = bf16[528,256]{1,0:T(8,128)(2,1)} custom-call(bf16[16,256]{1,0:T(8,128)(2,1)} %product_table.1.table_ref, bf16[4,64,128]{2,1,0:T(8,128)(2,1)} %get-tuple-element.30.refs_0_, bf16[4,64,128]{2,1,0:T(8,128)(2,1)} %copy-done.12, bf16[4,64,128]{2,1,0:T(8,128)(2,1)} %copy-done.13, bf16[4,64,128]{2,1,0:T(8,128)(2,1)} %copy-done.14), custom_call_target="tpu_custom_call" | custom-call | flops 20000000000 | bytes 524288 | tf_op jit(solution)/shard_map/join_k/pallas_call | solution.py:125
  14.7 2.1 %collective-permute-start.4 = (bf16[528,256]{1,0:T(8,128)(2,1)}, bf16[528,256]{1,0:T(8,128)(2,1)S(1)}, u32[]{:S(2)}, u32[]{:S(2)}) collective-permute-start(bf16[528,256]{1,0:T(8,128)(2,1)} %join_k.1.refs_0_), channel_id=1, source_target_pairs={{0,1},{1,0},{2,3},{3,2},{4,5},{5,4},{6,7},{7,6},{8,9},{9,8},{10,11... | collective-permute-start | bytes 811016 | tf_op jit(solution)/shard_map/ppermute | solution.py:338
  16.8 5.6 %collective-permute-start.3 = (bf16[528,256]{1,0:T(8,128)(2,1)}, bf16[528,256]{1,0:T(8,128)(2,1)S(1)}, u32[]{:S(2)}, u32[]{:S(2)}) collective-permute-start(bf16[528,256]{1,0:T(8,128)(2,1)} %join_k.1.refs_0_), channel_id=1, source_target_pairs={{0,8},{1,57},{8,16},{9,1},{16,24},{17,9},{24,32},{25,17},{32,40},{... | collective-permute-start | bytes 811016 | tf_op jit(solution)/shard_map/ppermute | solution.py:334
  22.4 0.0 collective-permute-done.4
  22.4 1.4 %collective-permute-start.5 = (bf16[528,256]{1,0:T(8,128)(2,1)S(1)}, bf16[528,256]{1,0:T(8,128)(2,1)S(1)}, u32[]{:S(2)}, u32[]{:S(2)}) collective-permute-start(bf16[528,256]{1,0:T(8,128)(2,1)S(1)} %collective-permute-done.4), channel_id=1, source_target_pairs={{0,8},{1,57},{8,16},{9,1},{16,24},{17,9},{24,32},{25,17},{32,40},{... | collective-permute-start | bytes 811016 | tf_op jit(solution)/shard_map/ppermute | solution.py:334
  23.8 2.3 %collective-permute-done.3.refs_1_ = bf16[528,256]{1,0:T(8,128)(2,1)S(1)} collective-permute-done((bf16[528,256]{1,0:T(8,128)(2,1)}, bf16[528,256]{1,0:T(8,128)(2,1)S(1)}, u32[]{:S(2)}, u32[]{:S(2)}) %collective-permute-start.3) | collective-permute-done | bytes 270368 | tf_op jit(solution)/shard_map/ppermute | solution.py:334
  26.1 3.4 %collective-permute-start.6 = (bf16[528,256]{1,0:T(8,128)(2,1)S(1)}, bf16[528,256]{1,0:T(8,128)(2,1)S(1)}, u32[]{:S(2)}, u32[]{:S(2)}) collective-permute-start(bf16[528,256]{1,0:T(8,128)(2,1)S(1)} %collective-permute-done.3.refs_1_), channel_id=1, source_target_pairs={{0,8},{1,57},{8,16},{9,1},{16,24},{17,9},{24,32},{25,17},{32,40},{... | collective-permute-start | bytes 811016 | tf_op jit(solution)/shard_map/ppermute | solution.py:334
  29.5 0.0 collective-permute-done.5.refs_2_
  29.5 2.9 %collective-permute-start.7 = (bf16[528,256]{1,0:T(8,128)(2,1)S(1)}, bf16[528,256]{1,0:T(8,128)(2,1)}, u32[]{:S(2)}, u32[]{:S(2)}) collective-permute-start(bf16[528,256]{1,0:T(8,128)(2,1)S(1)} %collective-permute-done.5.refs_2_), channel_id=1, source_target_pairs={{0,8},{1,57},{8,16},{9,1},{16,24},{17,9},{24,32},{25,17},{32,40},{... | collective-permute-start | bytes 811016 | tf_op jit(solution)/shard_map/ppermute | solution.py:334
  32.4 0.5 collective-permute-done.6.refs_3_
  32.9 3.5 %collective-permute-start.8 = (bf16[528,256]{1,0:T(8,128)(2,1)S(1)}, bf16[528,256]{1,0:T(8,128)(2,1)}, u32[]{:S(2)}, u32[]{:S(2)}) collective-permute-start(bf16[528,256]{1,0:T(8,128)(2,1)S(1)} %collective-permute-done.6.refs_3_), channel_id=1, source_target_pairs={{0,8},{1,57},{8,16},{9,1},{16,24},{17,9},{24,32},{25,17},{32,40},{... | collective-permute-start | bytes 811016 | tf_op jit(solution)/shard_map/ppermute | solution.py:334
  36.4 0.0 collective-permute-done.13.refs_12_
  36.5 0.9 %collective-permute-start.14 = (bf16[16,64,256]{2,1,0:T(8,128)(2,1)S(1)}, bf16[16,64,256]{2,1,0:T(8,128)(2,1)S(1)}, u32[]{:S(2)}, u32[]{:S(2)}) collective-permute-start(bf16[16,64,256]{2,1,0:T(8,128)(2,1)S(1)} %slice.9), channel_id=1, source_target_pairs={{0,192},{64,0},{128,64},{192,128},{1,193},{65,1},{129,65},{193,129... | collective-permute-start | bytes 1572872 | tf_op jit(solution)/shard_map/ppermute | solution.py:326
  37.4 0.0 collective-permute-done.11.refs_9_
  37.4 1.1 %slice.8 = bf16[16,64,256]{2,1,0:T(8,128)(2,1)S(1)} slice(bf16[32,64,256]{2,1,0:T(8,128)(2,1)} %collective-permute-done.11.refs_9_), slice={[0:16], [0:64], [0:256]} | slice | bytes 1048576 | tf_op jit(solution)/shard_map/slice | solution.py:349
  38.5 0.7 collective-permute-start.12
  39.2 2.7 %collective-permute-start.9 = (bf16[528,256]{1,0:T(8,128)(2,1)}, bf16[528,256]{1,0:T(8,128)(2,1)S(1)}, u32[]{:S(2)}, u32[]{:S(2)}) collective-permute-start(bf16[528,256]{1,0:T(8,128)(2,1)} %collective-permute-done.7.refs_4_), channel_id=1, source_target_pairs={{0,8},{1,57},{8,16},{9,1},{16,24},{17,9},{24,32},{25,17},{32,40},{... | collective-permute-start | bytes 811016 | tf_op jit(solution)/shard_map/ppermute | solution.py:334
  41.9 1.2 %collective-permute-start.10 = (bf16[528,256]{1,0:T(8,128)(2,1)}, bf16[528,256]{1,0:T(8,128)(2,1)}, u32[]{:S(2)}, u32[]{:S(2)}) collective-permute-start(bf16[528,256]{1,0:T(8,128)(2,1)} %collective-permute-done.8.refs_5_), channel_id=1, source_target_pairs={{0,8},{1,57},{8,16},{9,1},{16,24},{17,9},{24,32},{25,17},{32,40},{... | collective-permute-start | bytes 811016 | tf_op jit(solution)/shard_map/ppermute | solution.py:334
  43.1 0.7 pad_add_fusion.me_ref
  43.7 0.0 collective-permute-start.18
  43.7 1.9 %collective-permute-done.9.refs_6_ = bf16[528,256]{1,0:T(8,128)(2,1)S(1)} collective-permute-done((bf16[528,256]{1,0:T(8,128)(2,1)}, bf16[528,256]{1,0:T(8,128)(2,1)S(1)}, u32[]{:S(2)}, u32[]{:S(2)}) %collective-permute-start.9) | collective-permute-done | bytes 270368 | tf_op jit(solution)/shard_map/ppermute | solution.py:334
  45.6 4.1 %collective-permute-start.15 = (bf16[32,64,256]{2,1,0:T(8,128)(2,1)}, bf16[32,64,256]{2,1,0:T(8,128)(2,1)}, u32[]{:S(2)}, u32[]{:S(2)}) collective-permute-start(bf16[32,64,256]{2,1,0:T(8,128)(2,1)} %collective-permute-done.11.refs_9_), channel_id=1, source_target_pairs={{0,1},{1,0},{2,3},{3,2},{4,5},{5,4},{6,7},{7,6},{8,9},{9,8},{10,11... | collective-permute-start | bytes 3145736 | tf_op jit(solution)/shard_map/ppermute | solution.py:338
  49.7 0.7 collective-permute-done.14.refs_11_
  50.4 0.1 collective-permute-start.17
  50.5 2.7 %collective-permute-done.12.refs_10_ = bf16[16,64,256]{2,1,0:T(8,128)(2,1)} collective-permute-done((bf16[16,64,256]{2,1,0:T(8,128)(2,1)S(1)}, bf16[16,64,256]{2,1,0:T(8,128)(2,1)}, u32[]{:S(2)}, u32[]{:S(2)}) %collective-permute-start.12) | collective-permute-done | bytes 524320 | tf_op jit(solution)/shard_map/ppermute | solution.py:326
  53.2 1.0 %collective-permute-start.16 = (bf16[16,64,256]{2,1,0:T(8,128)(2,1)}, bf16[16,64,256]{2,1,0:T(8,128)(2,1)S(1)}, u32[]{:S(2)}, u32[]{:S(2)}) collective-permute-start(bf16[16,64,256]{2,1,0:T(8,128)(2,1)} %collective-permute-done.12.refs_10_), channel_id=1, source_target_pairs={{0,1},{1,0},{2,3},{3,2},{4,5},{5,4},{6,7},{7,6},{8,9},{9,8},{10,11... | collective-permute-start | bytes 1572872 | tf_op jit(solution)/shard_map/ppermute | solution.py:338
  54.2 3.6 %sort_products.1.listed = s32[11,128]{1,0:T(8,128)} custom-call(s32[2]{0:T(128)} %pad_add_fusion.me_ref, bf16[528,256]{1,0:T(8,128)(2,1)} %join_k.1.refs_0_, bf16[528,256]{1,0:T(8,128)(2,1)} %copy-done.8, bf16[528,256]{1,0:T(8,128)(2,1)} %copy-done.9, bf16[528,256]{1,0:T(8,128)(2,1)} %copy-done.10, bf16[528,256]{1,0:T(8,128)(2,1)} %collective-permute-done.7.refs_4_, ...), custom_call_target="tpu_custom_call" | custom-call | flops 20000000000 | bytes 65536 | tf_op jit(solution)/shard_map/sort_products/pallas_call | solution.py:211
  57.9 0.0 collective-permute-done.18.refs_16_
  57.9 0.0 collective-permute-done.16.refs_14_
  57.9 0.7 copy-done.6
  58.7 0.2 copy-done.7
  58.9 0.7 copy-done.1
  59.6 8.8 %products.1 = (bf16[8,64,256]{2,1,0:T(8,128)(2,1)S(1)}, bf16[8,64,256]{2,1,0:T(8,128)(2,1)S(1)}, bf16[8,64,256]{2,1,0:T(8,128)(2,1)S(1)}, bf16[8,64,256]{2,1,0:T...) custom-call(s32[2]{0:T(128)S(1)} %copy-done, ...), custom_call_target="tpu_custom_call" | custom-call | flops 3221225472 | bytes 10485760 | tf_op jit(solution)/shard_map/products/pallas_call | solution.py:305
  68.5 0.9 %collective-permute-start.19 = (bf16[8,64,256]{2,1,0:T(8,128)(2,1)S(1)}, bf16[8,64,256]{2,1,0:T(8,128)(2,1)S(1)}, u32[]{:S(2)}, u32[]{:S(2)}) collective-permute-start(bf16[8,64,256]{2,1,0:T(8,128)(2,1)S(1)} %get-tuple-element.36), channel_id=1, source_target_pairs={{0,1},{1,0},{2,3},{3,2},{4,5},{5,4},{6,7},{7,6},{8,9},{9,8},{10,11... | collective-permute-start | bytes 786440 | tf_op jit(solution)/shard_map/ppermute | solution.py:338
  69.4 0.1 collective-permute-start.21
  69.5 0.4 collective-permute-start.23
  69.9 0.1 collective-permute-start.25
  70.0 0.6 collective-permute-done.19
  70.5 0.1 add_convert_fusion.2
  70.6 3.2 %collective-permute-start.20 = (bf16[8,64,256]{2,1,0:T(8,128)(2,1)S(1)}, bf16[8,64,256]{2,1,0:T(8,128)(2,1)S(1)}, u32[]{:S(2)}, u32[]{:S(2)}) collective-permute-start(bf16[8,64,256]{2,1,0:T(8,128)(2,1)S(1)} %add_convert_fusion.2), channel_id=1, source_target_pairs={{0,4},{2,6},{4,0},{6,2},{1,5},{3,7},{5,1},{7,3},{8,12},{10,14},{12... | collective-permute-start | bytes 786440 | tf_op jit(solution)/shard_map/ppermute | solution.py:326
  73.8 0.1 add_convert_fusion.1
  73.9 0.8 collective-permute-start.22
  74.7 0.0 collective-permute-done.23
  74.7 0.1 add_convert_fusion
  74.8 2.0 %collective-permute-start.24 = (bf16[8,64,256]{2,1,0:T(8,128)(2,1)S(1)}, bf16[8,64,256]{2,1,0:T(8,128)(2,1)S(1)}, u32[]{:S(2)}, u32[]{:S(2)}) collective-permute-start(bf16[8,64,256]{2,1,0:T(8,128)(2,1)S(1)} %add_convert_fusion), channel_id=1, source_target_pairs={{0,6},{2,0},{4,2},{6,4},{1,7},{3,1},{5,3},{7,5},{8,14},{10,8},{12,... | collective-permute-start | bytes 786440 | tf_op jit(solution)/shard_map/ppermute | solution.py:326
  76.8 0.0 collective-permute-done.25
  76.8 3.3 %collective-permute-done.20 = bf16[8,64,256]{2,1,0:T(8,128)(2,1)S(1)} collective-permute-done((bf16[8,64,256]{2,1,0:T(8,128)(2,1)S(1)}, bf16[8,64,256]{2,1,0:T(8,128)(2,1)S(1)}, u32[]{:S(2)}, u32[]{:S(2)}) %collective-permute-start.20) | collective-permute-done | bytes 262176 | tf_op jit(solution)/shard_map/ppermute | solution.py:326
  80.0 6.1 %collective-permute-done.22 = bf16[8,64,256]{2,1,0:T(8,128)(2,1)S(1)} collective-permute-done((bf16[8,64,256]{2,1,0:T(8,128)(2,1)S(1)}, bf16[8,64,256]{2,1,0:T(8,128)(2,1)S(1)}, u32[]{:S(2)}, u32[]{:S(2)}) %collective-permute-start.22) | collective-permute-done | bytes 262176 | tf_op jit(solution)/shard_map/ppermute | solution.py:326
  86.2 0.1 collective-permute-done.24
  86.3 1.0 %add_add_fusion = f32[8,64,256]{2,1,0:T(8,128)} fusion(f32[8,64,256]{2,1,0:T(8,128)S(1)} %copy-done.3, bf16[8,64,256]{2,1,0:T(8,128)(2,1)S(1)} %collective-permute-done.25, bf16[8,64,256]{2,1,0:T(8,128)(2,1)S(1)} %collective-permute-done.24, bf16[8,64,256]{2,1,0:T(8,128)(2,1)S(1)} %collective-permute-done.22, bf16[8,64,256]{2,1,0:T(8,128)(2,1)S(1)} %collective-permute-done.20), kind=kLoop, calls=%fused_computation | loop fusion | flops 1048576 | bytes 2097152 | tf_op jit(solution)/shard_map/add | solution.py:370
  (31 shorter events, 0.1 us)
Async XLA Ops:
  1.8 9.9 %collective-permute-start = (bf16[4,64,128]{2,1,0:T(8,128)(2,1)}, bf16[4,64,128]{2,1,0:T(8,128)(2,1)S(1)}, u32[]{:S(2)}, u32[]{:S(2)}) collective-permute-start(bf16[4,64,128]{2,1,0:T(8,128)(2,1)} %get-tuple-element.31), channel_id=1, source_target_pairs={{0,64},{64,128},{128,192},{192,0},{1,65},{65,129},{129,193},{193,1... | collective-permute-start | bytes 196616 | tf_op jit(solution)/shard_map/ppermute | solution.py:326
  3.9 7.7 %collective-permute-start.1 = (bf16[4,64,128]{2,1,0:T(8,128)(2,1)}, bf16[4,64,128]{2,1,0:T(8,128)(2,1)S(1)}, u32[]{:S(2)}, u32[]{:S(2)}) collective-permute-start(bf16[4,64,128]{2,1,0:T(8,128)(2,1)} %get-tuple-element.32), channel_id=1, source_target_pairs={{0,128},{64,192},{128,0},{192,64},{1,129},{65,193},{129,1},{193,65... | collective-permute-start | bytes 196616 | tf_op jit(solution)/shard_map/ppermute | solution.py:326
  6.6 5.1 %collective-permute-start.2 = (bf16[4,64,128]{2,1,0:T(8,128)(2,1)}, bf16[4,64,128]{2,1,0:T(8,128)(2,1)S(1)}, u32[]{:S(2)}, u32[]{:S(2)}) collective-permute-start(bf16[4,64,128]{2,1,0:T(8,128)(2,1)} %get-tuple-element.33), channel_id=1, source_target_pairs={{0,192},{64,0},{128,64},{192,128},{1,193},{65,1},{129,65},{193,129... | collective-permute-start | bytes 196616 | tf_op jit(solution)/shard_map/ppermute | solution.py:326
  7.6 2.4 %copy-start.2 = (bf16[64,64,256]{2,1,0:T(8,128)(2,1)S(1)}, bf16[64,64,256]{2,1,0:T(8,128)(2,1)}, u32[]{:S(2)}) copy-start(bf16[64,64,256]{2,1,0:T(8,128)(2,1)} %refs_8_.1) | copy-start | bytes 6291460
  10.1 26.3 %collective-permute-start.13 = (bf16[32,64,256]{2,1,0:T(8,128)(2,1)S(1)}, bf16[32,64,256]{2,1,0:T(8,128)(2,1)S(1)}, u32[]{:S(2)}, u32[]{:S(2)}) collective-permute-start(bf16[32,64,256]{2,1,0:T(8,128)(2,1)S(1)} %constant_dynamic-slice_fusion), channel_id=1, source_target_pairs={{0,192},{64,0},{128,64},{192,128},{1,193},{65,1},{129,65},{193,129... | collective-permute-start | bytes 3145736 | tf_op jit(solution)/shard_map/ppermute | solution.py:326
  10.2 27.2 %collective-permute-start.11 = (bf16[32,64,256]{2,1,0:T(8,128)(2,1)S(1)}, bf16[32,64,256]{2,1,0:T(8,128)(2,1)}, u32[]{:S(2)}, u32[]{:S(2)}) collective-permute-start(bf16[32,64,256]{2,1,0:T(8,128)(2,1)S(1)} %constant_dynamic-slice_fusion), channel_id=1, source_target_pairs={{0,64},{64,128},{128,192},{192,0},{1,65},{65,129},{129,193},{193,1... | collective-permute-start | bytes 3145736 | tf_op jit(solution)/shard_map/ppermute | solution.py:326
  11.7 0.6 copy-start.12
  11.7 0.6 copy-start.13
  12.3 0.6 copy-start.14
  14.7 7.7 %collective-permute-start.4 = (bf16[528,256]{1,0:T(8,128)(2,1)}, bf16[528,256]{1,0:T(8,128)(2,1)S(1)}, u32[]{:S(2)}, u32[]{:S(2)}) collective-permute-start(bf16[528,256]{1,0:T(8,128)(2,1)} %join_k.1.refs_0_), channel_id=1, source_target_pairs={{0,1},{1,0},{2,3},{3,2},{4,5},{5,4},{6,7},{7,6},{8,9},{9,8},{10,11... | collective-permute-start | bytes 811016 | tf_op jit(solution)/shard_map/ppermute | solution.py:338
  16.8 9.3 %collective-permute-start.3 = (bf16[528,256]{1,0:T(8,128)(2,1)}, bf16[528,256]{1,0:T(8,128)(2,1)S(1)}, u32[]{:S(2)}, u32[]{:S(2)}) collective-permute-start(bf16[528,256]{1,0:T(8,128)(2,1)} %join_k.1.refs_0_), channel_id=1, source_target_pairs={{0,8},{1,57},{8,16},{9,1},{16,24},{17,9},{24,32},{25,17},{32,40},{... | collective-permute-start | bytes 811016 | tf_op jit(solution)/shard_map/ppermute | solution.py:334
  22.4 7.1 %collective-permute-start.5 = (bf16[528,256]{1,0:T(8,128)(2,1)S(1)}, bf16[528,256]{1,0:T(8,128)(2,1)S(1)}, u32[]{:S(2)}, u32[]{:S(2)}) collective-permute-start(bf16[528,256]{1,0:T(8,128)(2,1)S(1)} %collective-permute-done.4), channel_id=1, source_target_pairs={{0,8},{1,57},{8,16},{9,1},{16,24},{17,9},{24,32},{25,17},{32,40},{... | collective-permute-start | bytes 811016 | tf_op jit(solution)/shard_map/ppermute | solution.py:334
  26.1 28.1 %copy-start.8 = (bf16[528,256]{1,0:T(8,128)(2,1)}, bf16[528,256]{1,0:T(8,128)(2,1)S(1)}, u32[]{:S(2)}) copy-start(bf16[528,256]{1,0:T(8,128)(2,1)S(1)} %collective-permute-done.3.refs_1_) | copy-start | bytes 811012
  26.1 6.8 %collective-permute-start.6 = (bf16[528,256]{1,0:T(8,128)(2,1)S(1)}, bf16[528,256]{1,0:T(8,128)(2,1)S(1)}, u32[]{:S(2)}, u32[]{:S(2)}) collective-permute-start(bf16[528,256]{1,0:T(8,128)(2,1)S(1)} %collective-permute-done.3.refs_1_), channel_id=1, source_target_pairs={{0,8},{1,57},{8,16},{9,1},{16,24},{17,9},{24,32},{25,17},{32,40},{... | collective-permute-start | bytes 811016 | tf_op jit(solution)/shard_map/ppermute | solution.py:334
  29.5 9.7 %copy-start.9 = (bf16[528,256]{1,0:T(8,128)(2,1)}, bf16[528,256]{1,0:T(8,128)(2,1)S(1)}, u32[]{:S(2)}) copy-start(bf16[528,256]{1,0:T(8,128)(2,1)S(1)} %collective-permute-done.5.refs_2_) | copy-start | bytes 811012
  29.5 9.7 %collective-permute-start.7 = (bf16[528,256]{1,0:T(8,128)(2,1)S(1)}, bf16[528,256]{1,0:T(8,128)(2,1)}, u32[]{:S(2)}, u32[]{:S(2)}) collective-permute-start(bf16[528,256]{1,0:T(8,128)(2,1)S(1)} %collective-permute-done.5.refs_2_), channel_id=1, source_target_pairs={{0,8},{1,57},{8,16},{9,1},{16,24},{17,9},{24,32},{25,17},{32,40},{... | collective-permute-start | bytes 811016 | tf_op jit(solution)/shard_map/ppermute | solution.py:334
  32.9 6.3 %copy-start.10 = (bf16[528,256]{1,0:T(8,128)(2,1)}, bf16[528,256]{1,0:T(8,128)(2,1)S(1)}, u32[]{:S(2)}) copy-start(bf16[528,256]{1,0:T(8,128)(2,1)S(1)} %collective-permute-done.6.refs_3_) | copy-start | bytes 811012
  32.9 9.0 %collective-permute-start.8 = (bf16[528,256]{1,0:T(8,128)(2,1)S(1)}, bf16[528,256]{1,0:T(8,128)(2,1)}, u32[]{:S(2)}, u32[]{:S(2)}) collective-permute-start(bf16[528,256]{1,0:T(8,128)(2,1)S(1)} %collective-permute-done.6.refs_3_), channel_id=1, source_target_pairs={{0,8},{1,57},{8,16},{9,1},{16,24},{17,9},{24,32},{25,17},{32,40},{... | collective-permute-start | bytes 811016 | tf_op jit(solution)/shard_map/ppermute | solution.py:334
  36.4 21.4 %copy-start.4 = (bf16[32,64,256]{2,1,0:T(8,128)(2,1)}, bf16[32,64,256]{2,1,0:T(8,128)(2,1)S(1)}, u32[]{:S(2)}) copy-start(bf16[32,64,256]{2,1,0:T(8,128)(2,1)S(1)} %collective-permute-done.13.refs_12_) | copy-start | bytes 3145732
  36.5 13.9 %collective-permute-start.14 = (bf16[16,64,256]{2,1,0:T(8,128)(2,1)S(1)}, bf16[16,64,256]{2,1,0:T(8,128)(2,1)S(1)}, u32[]{:S(2)}, u32[]{:S(2)}) collective-permute-start(bf16[16,64,256]{2,1,0:T(8,128)(2,1)S(1)} %slice.9), channel_id=1, source_target_pairs={{0,192},{64,0},{128,64},{192,128},{1,193},{65,1},{129,65},{193,129... | collective-permute-start | bytes 1572872 | tf_op jit(solution)/shard_map/ppermute | solution.py:326
  38.5 14.7 %collective-permute-start.12 = (bf16[16,64,256]{2,1,0:T(8,128)(2,1)S(1)}, bf16[16,64,256]{2,1,0:T(8,128)(2,1)}, u32[]{:S(2)}, u32[]{:S(2)}) collective-permute-start(bf16[16,64,256]{2,1,0:T(8,128)(2,1)S(1)} %slice.8), channel_id=1, source_target_pairs={{0,64},{64,128},{128,192},{192,0},{1,65},{65,129},{129,193},{193,1... | collective-permute-start | bytes 1572872 | tf_op jit(solution)/shard_map/ppermute | solution.py:326
  39.2 6.4 %collective-permute-start.9 = (bf16[528,256]{1,0:T(8,128)(2,1)}, bf16[528,256]{1,0:T(8,128)(2,1)S(1)}, u32[]{:S(2)}, u32[]{:S(2)}) collective-permute-start(bf16[528,256]{1,0:T(8,128)(2,1)} %collective-permute-done.7.refs_4_), channel_id=1, source_target_pairs={{0,8},{1,57},{8,16},{9,1},{16,24},{17,9},{24,32},{25,17},{32,40},{... | collective-permute-start | bytes 811016 | tf_op jit(solution)/shard_map/ppermute | solution.py:334
  41.9 12.3 %collective-permute-start.10 = (bf16[528,256]{1,0:T(8,128)(2,1)}, bf16[528,256]{1,0:T(8,128)(2,1)}, u32[]{:S(2)}, u32[]{:S(2)}) collective-permute-start(bf16[528,256]{1,0:T(8,128)(2,1)} %collective-permute-done.8.refs_5_), channel_id=1, source_target_pairs={{0,8},{1,57},{8,16},{9,1},{16,24},{17,9},{24,32},{25,17},{32,40},{... | collective-permute-start | bytes 811016 | tf_op jit(solution)/shard_map/ppermute | solution.py:334
  43.7 15.2 %copy-start = (s32[2]{0:T(128)S(1)}, s32[2]{0:T(128)}, u32[]{:S(2)}) copy-start(s32[2]{0:T(128)} %pad_add_fusion.me_ref) | copy-start | bytes 28
  43.7 14.2 %collective-permute-start.18 = (bf16[32,64,256]{2,1,0:T(8,128)(2,1)S(1)}, bf16[32,64,256]{2,1,0:T(8,128)(2,1)}, u32[]{:S(2)}, u32[]{:S(2)}) collective-permute-start(bf16[32,64,256]{2,1,0:T(8,128)(2,1)S(1)} %collective-permute-done.13.refs_12_), channel_id=1, source_target_pairs={{0,1},{1,0},{2,3},{3,2},{4,5},{5,4},{6,7},{7,6},{8,9},{9,8},{10,11... | collective-permute-start | bytes 3145736 | tf_op jit(solution)/shard_map/ppermute | solution.py:338
  45.6 4.1 %copy-start.11 = (bf16[528,256]{1,0:T(8,128)(2,1)}, bf16[528,256]{1,0:T(8,128)(2,1)S(1)}, u32[]{:S(2)}) copy-start(bf16[528,256]{1,0:T(8,128)(2,1)S(1)} %collective-permute-done.9.refs_6_) | copy-start | bytes 811012
  45.6 12.3 %collective-permute-start.15 = (bf16[32,64,256]{2,1,0:T(8,128)(2,1)}, bf16[32,64,256]{2,1,0:T(8,128)(2,1)}, u32[]{:S(2)}, u32[]{:S(2)}) collective-permute-start(bf16[32,64,256]{2,1,0:T(8,128)(2,1)} %collective-permute-done.11.refs_9_), channel_id=1, source_target_pairs={{0,1},{1,0},{2,3},{3,2},{4,5},{5,4},{6,7},{7,6},{8,9},{9,8},{10,11... | collective-permute-start | bytes 3145736 | tf_op jit(solution)/shard_map/ppermute | solution.py:338
  50.4 7.5 %copy-start.5 = (bf16[16,64,256]{2,1,0:T(8,128)(2,1)}, bf16[16,64,256]{2,1,0:T(8,128)(2,1)S(1)}, u32[]{:S(2)}) copy-start(bf16[16,64,256]{2,1,0:T(8,128)(2,1)S(1)} %collective-permute-done.14.refs_11_) | copy-start | bytes 1572868
  50.4 7.5 %collective-permute-start.17 = (bf16[16,64,256]{2,1,0:T(8,128)(2,1)S(1)}, bf16[16,64,256]{2,1,0:T(8,128)(2,1)S(1)}, u32[]{:S(2)}, u32[]{:S(2)}) collective-permute-start(bf16[16,64,256]{2,1,0:T(8,128)(2,1)S(1)} %collective-permute-done.14.refs_11_), channel_id=1, source_target_pairs={{0,1},{1,0},{2,3},{3,2},{4,5},{5,4},{6,7},{7,6},{8,9},{9,8},{10,11... | collective-permute-start | bytes 1572872 | tf_op jit(solution)/shard_map/ppermute | solution.py:338
  53.2 4.7 %collective-permute-start.16 = (bf16[16,64,256]{2,1,0:T(8,128)(2,1)}, bf16[16,64,256]{2,1,0:T(8,128)(2,1)S(1)}, u32[]{:S(2)}, u32[]{:S(2)}) collective-permute-start(bf16[16,64,256]{2,1,0:T(8,128)(2,1)} %collective-permute-done.12.refs_10_), channel_id=1, source_target_pairs={{0,1},{1,0},{2,3},{3,2},{4,5},{5,4},{6,7},{7,6},{8,9},{9,8},{10,11... | collective-permute-start | bytes 1572872 | tf_op jit(solution)/shard_map/ppermute | solution.py:338
  57.9 0.8 copy-start.6
  57.9 1.0 %copy-start.7 = (bf16[16,64,256]{2,1,0:T(8,128)(2,1)}, bf16[16,64,256]{2,1,0:T(8,128)(2,1)S(1)}, u32[]{:S(2)}) copy-start(bf16[16,64,256]{2,1,0:T(8,128)(2,1)S(1)} %collective-permute-done.16.refs_14_) | copy-start | bytes 1572868
  58.9 0.7 copy-start.1
  68.5 17.8 %copy-start.3 = (f32[8,64,256]{2,1,0:T(8,128)S(1)}, f32[8,64,256]{2,1,0:T(8,128)}, u32[]{:S(2)}) copy-start(f32[8,64,256]{2,1,0:T(8,128)} %get-tuple-element.41) | copy-start | bytes 1572868
  68.5 2.1 %collective-permute-start.19 = (bf16[8,64,256]{2,1,0:T(8,128)(2,1)S(1)}, bf16[8,64,256]{2,1,0:T(8,128)(2,1)S(1)}, u32[]{:S(2)}, u32[]{:S(2)}) collective-permute-start(bf16[8,64,256]{2,1,0:T(8,128)(2,1)S(1)} %get-tuple-element.36), channel_id=1, source_target_pairs={{0,1},{1,0},{2,3},{3,2},{4,5},{5,4},{6,7},{7,6},{8,9},{9,8},{10,11... | collective-permute-start | bytes 786440 | tf_op jit(solution)/shard_map/ppermute | solution.py:338
  69.4 4.4 %collective-permute-start.21 = (bf16[8,64,256]{2,1,0:T(8,128)(2,1)S(1)}, bf16[8,64,256]{2,1,0:T(8,128)(2,1)S(1)}, u32[]{:S(2)}, u32[]{:S(2)}) collective-permute-start(bf16[8,64,256]{2,1,0:T(8,128)(2,1)S(1)} %get-tuple-element.38), channel_id=1, source_target_pairs={{0,1},{1,0},{2,3},{3,2},{4,5},{5,4},{6,7},{7,6},{8,9},{9,8},{10,11... | collective-permute-start | bytes 786440 | tf_op jit(solution)/shard_map/ppermute | solution.py:338
  69.5 5.2 %collective-permute-start.23 = (bf16[8,64,256]{2,1,0:T(8,128)(2,1)S(1)}, bf16[8,64,256]{2,1,0:T(8,128)(2,1)S(1)}, u32[]{:S(2)}, u32[]{:S(2)}) collective-permute-start(bf16[8,64,256]{2,1,0:T(8,128)(2,1)S(1)} %get-tuple-element.40), channel_id=1, source_target_pairs={{0,1},{1,0},{2,3},{3,2},{4,5},{5,4},{6,7},{7,6},{8,9},{9,8},{10,11... | collective-permute-start | bytes 786440 | tf_op jit(solution)/shard_map/ppermute | solution.py:338
  69.9 6.9 %collective-permute-start.25 = (bf16[8,64,256]{2,1,0:T(8,128)(2,1)S(1)}, bf16[8,64,256]{2,1,0:T(8,128)(2,1)S(1)}, u32[]{:S(2)}, u32[]{:S(2)}) collective-permute-start(bf16[8,64,256]{2,1,0:T(8,128)(2,1)S(1)} %get-tuple-element.42), channel_id=1, source_target_pairs={{0,1},{1,0},{2,3},{3,2},{4,5},{5,4},{6,7},{7,6},{8,9},{9,8},{10,11... | collective-permute-start | bytes 786440 | tf_op jit(solution)/shard_map/ppermute | solution.py:338
  70.6 9.4 %collective-permute-start.20 = (bf16[8,64,256]{2,1,0:T(8,128)(2,1)S(1)}, bf16[8,64,256]{2,1,0:T(8,128)(2,1)S(1)}, u32[]{:S(2)}, u32[]{:S(2)}) collective-permute-start(bf16[8,64,256]{2,1,0:T(8,128)(2,1)S(1)} %add_convert_fusion.2), channel_id=1, source_target_pairs={{0,4},{2,6},{4,0},{6,2},{1,5},{3,7},{5,1},{7,3},{8,12},{10,14},{12... | collective-permute-start | bytes 786440 | tf_op jit(solution)/shard_map/ppermute | solution.py:326
  73.9 12.3 %collective-permute-start.22 = (bf16[8,64,256]{2,1,0:T(8,128)(2,1)S(1)}, bf16[8,64,256]{2,1,0:T(8,128)(2,1)S(1)}, u32[]{:S(2)}, u32[]{:S(2)}) collective-permute-start(bf16[8,64,256]{2,1,0:T(8,128)(2,1)S(1)} %add_convert_fusion.1), channel_id=1, source_target_pairs={{0,2},{2,4},{4,6},{6,0},{1,3},{3,5},{5,7},{7,1},{8,10},{10,12},{12... | collective-permute-start | bytes 786440 | tf_op jit(solution)/shard_map/ppermute | solution.py:326
  74.8 11.5 %collective-permute-start.24 = (bf16[8,64,256]{2,1,0:T(8,128)(2,1)S(1)}, bf16[8,64,256]{2,1,0:T(8,128)(2,1)S(1)}, u32[]{:S(2)}, u32[]{:S(2)}) collective-permute-start(bf16[8,64,256]{2,1,0:T(8,128)(2,1)S(1)} %add_convert_fusion), channel_id=1, source_target_pairs={{0,6},{2,0},{4,2},{6,4},{1,7},{3,1},{5,3},{7,5},{8,14},{10,8},{12,... | collective-permute-start | bytes 786440 | tf_op jit(solution)/shard_map/ppermute | solution.py:326

commit v7 on v6

--- a/solution.py
+++ b/solution.py
@@ -346,6 +346,8 @@
     for distance in range(3):
         own, other = apart(own, "z", N_Z), apart(other, "z", N_Z)
         blocks += [own, other]
+        if distance == 1:
+            back, ahead, _ = lax.optimization_barrier((back, ahead, other))
     far_back = shift_by(back[: HALF // 2], "rep", N_REP, 1)
     far_ahead = shift_by(ahead[HALF // 2 :], "rep", N_REP, -1)
     parts = [back, far_back, far_ahead, ahead]

time: 88.7 us -> 86.3 us (0.973); the launches traced: 87.2 us -> 86.1 us
  waiting for transfers between devices: 18.2 us -> 15.4 us
  starting transfers between devices: 44.4 us -> 46.6 us
  local copies, waits for them, and re-layouts: 4.16 us -> 3.06 us
    ppermute x10, waiting for transfers between devices: 12.9 us -> 10.1 us  [shift_by(): lax.ppermute(value, axis, [(i, (i + step) % size) for i in range(size)])]
    ppermute x9, starting transfers between devices: 8.74 us -> 11.1 us  [other_core(): return lax.ppermute(value, 'core', [(0, 1), (1, 0)])]
    slice x1, local copies, waits for them, and re-layouts: 1.08 us -> 0.04 us  [gather(): far_back = shift_by(back[:HALF // 2], 'rep', N_REP, 1)]
    unnamed x30 -> x28, local copies, waits for them, and re-layouts: 2.94 us -> 2.88 us
  transfers between devices with their start and end apart: 26 -> 26, of which waited for: 9 -> 6; matrix products, arithmetic and copies ran while one was open for 2% -> 1% of each run, Pallas kernels for 9% -> 9%
where the time goes in v7:
time: 86.3 us; the launch traced here: 86.1 us
  starting transfers between devices  46.6 us (54%)
  Pallas kernels  19.1 us (22%)
  waiting for transfers between devices  15.4 us (18%)
  local copies, waits for them, and re-layouts  3.06 us (4%)
  other arithmetic  1.74 us (2%)
    ppermute x7, starting transfers between devices, apart(): return lax.ppermute(value, (axis, 'core'), perm)  21.4 us
    ppermute x10, starting transfers between devices, shift_by(): lax.ppermute(value, axis, [(i, (i + step) % size) for i in range(size)])  14.1 us
    ppermute x9, starting transfers between devices, other_core(): return lax.ppermute(value, 'core', [(0, 1), (1, 0)])  11.1 us
    ppermute x10, waiting for transfers between devices, shift_by(): lax.ppermute(value, axis, [(i, (i + step) % size) for i in range(size)])  10.1 us
    pallas_call x1, Pallas kernels, products(): pl.pallas_call(products_kernel, out_shape=[jax.ShapeDtypeStruct(shape, ki...  9.44 us
    ppermute x7, waiting for transfers between devices, apart(): return lax.ppermute(value, (axis, 'core'), perm)  4.71 us
    pallas_call x1, Pallas kernels, sort_products(): pl.pallas_call(sort_kernel, out_shape=jax.ShapeDtypeStruct((LIST // MOST...  3.65 us
    unnamed x28, local copies, waits for them, and re-layouts  2.88 us
  transfers between devices with their start and end apart: 26, of which 6 were waited for; matrix products, arithmetic and copies ran while one was open for 1% of the time, Pallas kernels for 9%

profile of v7, /device:TPU:1, one launch (start us, length us, event | category | flops | bytes accessed | tf_op | source)
XLA Modules:
  0.0 86.1 jit_solution(16332271494376084507)
XLA Ops:
  0.0 1.8 %spread_rows.1 = (bf16[4,64,128]{2,1,0:T(8,128)(2,1)}, bf16[4,64,128]{2,1,0:T(8,128)(2,1)}, bf16[4,64,128]{2,1,0:T(8,128)(2,1)}, bf16[4,64,128]{2,1,0:T(8,128)(2,1)}) custom-call(s32[1]{0:T(128)} %bitcast.2.rep_ref, bf16[8,64,256]{2,1,0:T(8,128)(2,1)} %bitcast.6), custom_call_target="tpu_custom_call" | custom-call | tf_op jit(solution)/shard_map/spread_rows/pallas_call | solution.py:102
  1.8 2.1 %collective-permute-start = (bf16[4,64,128]{2,1,0:T(8,128)(2,1)}, bf16[4,64,128]{2,1,0:T(8,128)(2,1)S(1)}, u32[]{:S(2)}, u32[]{:S(2)}) collective-permute-start(bf16[4,64,128]{2,1,0:T(8,128)(2,1)} %get-tuple-element.33), channel_id=1, source_target_pairs={{0,64},{64,128},{128,192},{192,0},{1,65},{65,129},{129,193},{193,1... | collective-permute-start | bytes 196616 | tf_op jit(solution)/shard_map/ppermute | solution.py:326
  3.9 2.6 %collective-permute-start.1 = (bf16[4,64,128]{2,1,0:T(8,128)(2,1)}, bf16[4,64,128]{2,1,0:T(8,128)(2,1)S(1)}, u32[]{:S(2)}, u32[]{:S(2)}) collective-permute-start(bf16[4,64,128]{2,1,0:T(8,128)(2,1)} %get-tuple-element.34), channel_id=1, source_target_pairs={{0,128},{64,192},{128,0},{192,64},{1,129},{65,193},{129,1},{193,65... | collective-permute-start | bytes 196616 | tf_op jit(solution)/shard_map/ppermute | solution.py:326
  6.6 1.1 %collective-permute-start.2 = (bf16[4,64,128]{2,1,0:T(8,128)(2,1)}, bf16[4,64,128]{2,1,0:T(8,128)(2,1)S(1)}, u32[]{:S(2)}, u32[]{:S(2)}) collective-permute-start(bf16[4,64,128]{2,1,0:T(8,128)(2,1)} %get-tuple-element.35), channel_id=1, source_target_pairs={{0,192},{64,0},{128,64},{192,128},{1,193},{65,1},{129,65},{193,129... | collective-permute-start | bytes 196616 | tf_op jit(solution)/shard_map/ppermute | solution.py:326
  7.6 2.4 %product_table.1.table_ref = bf16[16,256]{1,0:T(8,128)(2,1)} custom-call(s32[1]{0:T(128)} %bitcast.4.x_ref, s32[384]{0:T(512)} %a_ref.1, s32[384]{0:T(512)} %b_ref.1, s32[384]{0:T(512)} %live_ref.1, s32[48]{0:T(128)} %bitcast.7, s32[48]{0:T(128)} %target_ref.1), custom_call_target="tpu_custom_call" | custom-call | flops 8000000000 | bytes 65536 | tf_op jit(solution)/shard_map/product_table/pallas_call | solution.py:78
  10.0 0.1 constant_dynamic-slice_fusion
  10.1 0.1 collective-permute-start.12
  10.2 1.5 %collective-permute-start.11 = (bf16[32,64,256]{2,1,0:T(8,128)(2,1)S(1)}, bf16[32,64,256]{2,1,0:T(8,128)(2,1)S(1)}, u32[]{:S(2)}, u32[]{:S(2)}) collective-permute-start(bf16[32,64,256]{2,1,0:T(8,128)(2,1)S(1)} %constant_dynamic-slice_fusion), channel_id=1, source_target_pairs={{0,64},{64,128},{128,192},{192,0},{1,65},{65,129},{129,193},{193,1... | collective-permute-start | bytes 3145736 | tf_op jit(solution)/shard_map/ppermute | solution.py:326
  11.7 0.0 collective-permute-done.refs_1_
  11.7 0.0 collective-permute-done.1.refs_2_
  11.7 0.0 collective-permute-done.2.refs_3_
  11.7 0.6 copy-done.11
  12.3 0.0 copy-done.12
  12.3 0.6 copy-done.13
  12.9 1.8 %join_k.1.refs_0_ = bf16[528,256]{1,0:T(8,128)(2,1)} custom-call(bf16[16,256]{1,0:T(8,128)(2,1)} %product_table.1.table_ref, bf16[4,64,128]{2,1,0:T(8,128)(2,1)} %get-tuple-element.32.refs_0_, bf16[4,64,128]{2,1,0:T(8,128)(2,1)} %copy-done.11, bf16[4,64,128]{2,1,0:T(8,128)(2,1)} %copy-done.12, bf16[4,64,128]{2,1,0:T(8,128)(2,1)} %copy-done.13), custom_call_target="tpu_custom_call" | custom-call | flops 20000000000 | bytes 524288 | tf_op jit(solution)/shard_map/join_k/pallas_call | solution.py:125
  14.7 2.1 %collective-permute-start.4 = (bf16[528,256]{1,0:T(8,128)(2,1)}, bf16[528,256]{1,0:T(8,128)(2,1)S(1)}, u32[]{:S(2)}, u32[]{:S(2)}) collective-permute-start(bf16[528,256]{1,0:T(8,128)(2,1)} %join_k.1.refs_0_), channel_id=1, source_target_pairs={{0,1},{1,0},{2,3},{3,2},{4,5},{5,4},{6,7},{7,6},{8,9},{9,8},{10,11... | collective-permute-start | bytes 811016 | tf_op jit(solution)/shard_map/ppermute | solution.py:338
  16.8 5.6 %collective-permute-start.3 = (bf16[528,256]{1,0:T(8,128)(2,1)}, bf16[528,256]{1,0:T(8,128)(2,1)S(1)}, u32[]{:S(2)}, u32[]{:S(2)}) collective-permute-start(bf16[528,256]{1,0:T(8,128)(2,1)} %join_k.1.refs_0_), channel_id=1, source_target_pairs={{0,8},{1,57},{8,16},{9,1},{16,24},{17,9},{24,32},{25,17},{32,40},{... | collective-permute-start | bytes 811016 | tf_op jit(solution)/shard_map/ppermute | solution.py:334
  22.4 0.0 collective-permute-done.4
  22.4 1.4 %collective-permute-start.5 = (bf16[528,256]{1,0:T(8,128)(2,1)S(1)}, bf16[528,256]{1,0:T(8,128)(2,1)S(1)}, u32[]{:S(2)}, u32[]{:S(2)}) collective-permute-start(bf16[528,256]{1,0:T(8,128)(2,1)S(1)} %collective-permute-done.4), channel_id=1, source_target_pairs={{0,8},{1,57},{8,16},{9,1},{16,24},{17,9},{24,32},{25,17},{32,40},{... | collective-permute-start | bytes 811016 | tf_op jit(solution)/shard_map/ppermute | solution.py:334
  23.8 2.3 %collective-permute-done.3.refs_1_ = bf16[528,256]{1,0:T(8,128)(2,1)S(1)} collective-permute-done((bf16[528,256]{1,0:T(8,128)(2,1)}, bf16[528,256]{1,0:T(8,128)(2,1)S(1)}, u32[]{:S(2)}, u32[]{:S(2)}) %collective-permute-start.3) | collective-permute-done | bytes 270368 | tf_op jit(solution)/shard_map/ppermute | solution.py:334
  26.1 3.3 %collective-permute-start.6 = (bf16[528,256]{1,0:T(8,128)(2,1)S(1)}, bf16[528,256]{1,0:T(8,128)(2,1)S(1)}, u32[]{:S(2)}, u32[]{:S(2)}) collective-permute-start(bf16[528,256]{1,0:T(8,128)(2,1)S(1)} %collective-permute-done.3.refs_1_), channel_id=1, source_target_pairs={{0,8},{1,57},{8,16},{9,1},{16,24},{17,9},{24,32},{25,17},{32,40},{... | collective-permute-start | bytes 811016 | tf_op jit(solution)/shard_map/ppermute | solution.py:334
  29.4 0.0 collective-permute-done.5.refs_2_
  29.4 2.9 %collective-permute-start.7 = (bf16[528,256]{1,0:T(8,128)(2,1)S(1)}, bf16[528,256]{1,0:T(8,128)(2,1)}, u32[]{:S(2)}, u32[]{:S(2)}) collective-permute-start(bf16[528,256]{1,0:T(8,128)(2,1)S(1)} %collective-permute-done.5.refs_2_), channel_id=1, source_target_pairs={{0,8},{1,57},{8,16},{9,1},{16,24},{17,9},{24,32},{25,17},{32,40},{... | collective-permute-start | bytes 811016 | tf_op jit(solution)/shard_map/ppermute | solution.py:334
  32.3 0.5 collective-permute-done.6.refs_3_
  32.8 3.4 %collective-permute-start.8 = (bf16[528,256]{1,0:T(8,128)(2,1)S(1)}, bf16[528,256]{1,0:T(8,128)(2,1)}, u32[]{:S(2)}, u32[]{:S(2)}) collective-permute-start(bf16[528,256]{1,0:T(8,128)(2,1)S(1)} %collective-permute-done.6.refs_3_), channel_id=1, source_target_pairs={{0,8},{1,57},{8,16},{9,1},{16,24},{17,9},{24,32},{25,17},{32,40},{... | collective-permute-start | bytes 811016 | tf_op jit(solution)/shard_map/ppermute | solution.py:334
  36.2 0.0 collective-permute-done.7.refs_4_
  36.2 0.0 collective-permute-done.12.refs_12_
  36.2 0.0 collective-permute-done.11.refs_9_
  36.3 1.1 %collective-permute-start.14 = (bf16[16,64,256]{2,1,0:T(8,128)(2,1)S(1)}, bf16[16,64,256]{2,1,0:T(8,128)(2,1)}, u32[]{:S(2)}, u32[]{:S(2)}) collective-permute-start(bf16[16,64,256]{2,1,0:T(8,128)(2,1)S(1)} %slice.7), channel_id=1, source_target_pairs={{0,192},{64,0},{128,64},{192,128},{1,193},{65,1},{129,65},{193,129... | collective-permute-start | bytes 1572872 | tf_op jit(solution)/shard_map/ppermute | solution.py:326
  37.5 0.5 collective-permute-start.13
  38.0 3.9 %collective-permute-start.9 = (bf16[528,256]{1,0:T(8,128)(2,1)}, bf16[528,256]{1,0:T(8,128)(2,1)}, u32[]{:S(2)}, u32[]{:S(2)}) collective-permute-start(bf16[528,256]{1,0:T(8,128)(2,1)} %collective-permute-done.7.refs_4_), channel_id=1, source_target_pairs={{0,8},{1,57},{8,16},{9,1},{16,24},{17,9},{24,32},{25,17},{32,40},{... | collective-permute-start | bytes 811016 | tf_op jit(solution)/shard_map/ppermute | solution.py:334
  41.9 0.0 collective-permute-done.8.refs_5_
  41.9 0.9 %collective-permute-start.10 = (bf16[528,256]{1,0:T(8,128)(2,1)}, bf16[528,256]{1,0:T(8,128)(2,1)}, u32[]{:S(2)}, u32[]{:S(2)}) collective-permute-start(bf16[528,256]{1,0:T(8,128)(2,1)} %collective-permute-done.8.refs_5_), channel_id=1, source_target_pairs={{0,8},{1,57},{8,16},{9,1},{16,24},{17,9},{24,32},{25,17},{32,40},{... | collective-permute-start | bytes 811016 | tf_op jit(solution)/shard_map/ppermute | solution.py:334
  42.8 0.6 pad_add_fusion.me_ref
  43.4 0.3 collective-permute-start.15
  43.8 1.9 %collective-permute-done.9.refs_6_ = bf16[528,256]{1,0:T(8,128)(2,1)} collective-permute-done((bf16[528,256]{1,0:T(8,128)(2,1)}, bf16[528,256]{1,0:T(8,128)(2,1)}, u32[]{:S(2)}, u32[]{:S(2)}) %collective-permute-start.9) | collective-permute-done | bytes 270368 | tf_op jit(solution)/shard_map/ppermute | solution.py:334
  45.7 4.3 %collective-permute-start.18 = (bf16[32,64,256]{2,1,0:T(8,128)(2,1)S(1)}, bf16[32,64,256]{2,1,0:T(8,128)(2,1)}, u32[]{:S(2)}, u32[]{:S(2)}) collective-permute-start(bf16[32,64,256]{2,1,0:T(8,128)(2,1)S(1)} %collective-permute-done.12.refs_12_), channel_id=1, source_target_pairs={{0,1},{1,0},{2,3},{3,2},{4,5},{5,4},{6,7},{7,6},{8,9},{9,8},{10,11... | collective-permute-start | bytes 3145736 | tf_op jit(solution)/shard_map/ppermute | solution.py:338
  50.0 0.0 collective-permute-done.14.refs_11_
  50.0 0.9 %collective-permute-start.17 = (bf16[16,64,256]{2,1,0:T(8,128)(2,1)}, bf16[16,64,256]{2,1,0:T(8,128)(2,1)S(1)}, u32[]{:S(2)}, u32[]{:S(2)}) collective-permute-start(bf16[16,64,256]{2,1,0:T(8,128)(2,1)} %collective-permute-done.14.refs_11_), channel_id=1, source_target_pairs={{0,1},{1,0},{2,3},{3,2},{4,5},{5,4},{6,7},{7,6},{8,9},{9,8},{10,11... | collective-permute-start | bytes 1572872 | tf_op jit(solution)/shard_map/ppermute | solution.py:338
  50.8 2.4 %collective-permute-start.16 = (bf16[16,64,256]{2,1,0:T(8,128)(2,1)}, bf16[16,64,256]{2,1,0:T(8,128)(2,1)S(1)}, u32[]{:S(2)}, u32[]{:S(2)}) collective-permute-start(bf16[16,64,256]{2,1,0:T(8,128)(2,1)} %collective-permute-done.13.refs_10_), channel_id=1, source_target_pairs={{0,1},{1,0},{2,3},{3,2},{4,5},{5,4},{6,7},{7,6},{8,9},{9,8},{10,11... | collective-permute-start | bytes 1572872 | tf_op jit(solution)/shard_map/ppermute | solution.py:338
  53.2 3.6 %sort_products.1.listed = s32[11,128]{1,0:T(8,128)} custom-call(s32[2]{0:T(128)} %pad_add_fusion.me_ref, bf16[528,256]{1,0:T(8,128)(2,1)} %join_k.1.refs_0_, bf16[528,256]{1,0:T(8,128)(2,1)} %copy-done.8, bf16[528,256]{1,0:T(8,128)(2,1)} %copy-done.9, bf16[528,256]{1,0:T(8,128)(2,1)} %copy-done.10, bf16[528,256]{1,0:T(8,128)(2,1)} %collective-permute-done.7.refs_4_, ...), custom_call_target="tpu_custom_call" | custom-call | flops 20000000000 | bytes 65536 | tf_op jit(solution)/shard_map/sort_products/pallas_call | solution.py:211
  56.9 0.0 collective-permute-done.16.refs_14_
  56.9 0.0 copy-start.7
  56.9 0.7 copy-done.6
  57.7 0.2 copy-done.7
  57.9 0.7 copy-done.1
  58.6 9.4 %products.1 = (bf16[8,64,256]{2,1,0:T(8,128)(2,1)S(1)}, bf16[8,64,256]{2,1,0:T(8,128)(2,1)S(1)}, bf16[8,64,256]{2,1,0:T(8,128)(2,1)S(1)}, bf16[8,64,256]{2,1,0:T...) custom-call(s32[2]{0:T(128)S(1)} %copy-done, ...), custom_call_target="tpu_custom_call" | custom-call | flops 3221225472 | bytes 10485760 | tf_op jit(solution)/shard_map/products/pallas_call | solution.py:305
  68.0 0.1 collective-permute-start.19
  68.1 0.5 collective-permute-start.21
  68.6 0.1 collective-permute-start.23
  68.7 0.4 collective-permute-start.25
  69.1 0.5 collective-permute-done.19
  69.6 0.1 add_convert_fusion.2
  69.7 2.3 %collective-permute-start.20 = (bf16[8,64,256]{2,1,0:T(8,128)(2,1)S(1)}, bf16[8,64,256]{2,1,0:T(8,128)(2,1)S(1)}, u32[]{:S(2)}, u32[]{:S(2)}) collective-permute-start(bf16[8,64,256]{2,1,0:T(8,128)(2,1)S(1)} %add_convert_fusion.2), channel_id=1, source_target_pairs={{0,4},{2,6},{4,0},{6,2},{1,5},{3,7},{5,1},{7,3},{8,12},{10,14},{12... | collective-permute-start | bytes 786440 | tf_op jit(solution)/shard_map/ppermute | solution.py:326
  72.1 0.0 collective-permute-done.21
  72.1 0.1 add_convert_fusion.1
  72.1 0.7 collective-permute-start.22
  72.8 0.1 add_convert_fusion
  72.9 2.1 %collective-permute-start.24 = (bf16[8,64,256]{2,1,0:T(8,128)(2,1)S(1)}, bf16[8,64,256]{2,1,0:T(8,128)(2,1)S(1)}, u32[]{:S(2)}, u32[]{:S(2)}) collective-permute-start(bf16[8,64,256]{2,1,0:T(8,128)(2,1)S(1)} %add_convert_fusion), channel_id=1, source_target_pairs={{0,6},{2,0},{4,2},{6,4},{1,7},{3,1},{5,3},{7,5},{8,14},{10,8},{12,... | collective-permute-start | bytes 786440 | tf_op jit(solution)/shard_map/ppermute | solution.py:326
  75.0 0.0 collective-permute-done.25
  75.0 4.1 %collective-permute-done.20 = bf16[8,64,256]{2,1,0:T(8,128)(2,1)S(1)} collective-permute-done((bf16[8,64,256]{2,1,0:T(8,128)(2,1)S(1)}, bf16[8,64,256]{2,1,0:T(8,128)(2,1)S(1)}, u32[]{:S(2)}, u32[]{:S(2)}) %collective-permute-start.20) | collective-permute-done | bytes 262176 | tf_op jit(solution)/shard_map/ppermute | solution.py:326
  79.1 6.0 %collective-permute-done.22 = bf16[8,64,256]{2,1,0:T(8,128)(2,1)S(1)} collective-permute-done((bf16[8,64,256]{2,1,0:T(8,128)(2,1)S(1)}, bf16[8,64,256]{2,1,0:T(8,128)(2,1)S(1)}, u32[]{:S(2)}, u32[]{:S(2)}) %collective-permute-start.22) | collective-permute-done | bytes 262176 | tf_op jit(solution)/shard_map/ppermute | solution.py:326
  85.2 0.0 collective-permute-done.24
  85.2 0.9 %add_add_fusion = f32[8,64,256]{2,1,0:T(8,128)} fusion(f32[8,64,256]{2,1,0:T(8,128)S(1)} %copy-done.3, bf16[8,64,256]{2,1,0:T(8,128)(2,1)S(1)} %collective-permute-done.25, bf16[8,64,256]{2,1,0:T(8,128)(2,1)S(1)} %collective-permute-done.24, bf16[8,64,256]{2,1,0:T(8,128)(2,1)S(1)} %collective-permute-done.22, bf16[8,64,256]{2,1,0:T(8,128)(2,1)S(1)} %collective-permute-done.20), kind=kLoop, calls=%fused_computation | loop fusion | flops 1048576 | bytes 2097152 | tf_op jit(solution)/shard_map/add | solution.py:372
  (29 shorter events, 0.1 us)
Async XLA Ops:
  1.8 9.9 %collective-permute-start = (bf16[4,64,128]{2,1,0:T(8,128)(2,1)}, bf16[4,64,128]{2,1,0:T(8,128)(2,1)S(1)}, u32[]{:S(2)}, u32[]{:S(2)}) collective-permute-start(bf16[4,64,128]{2,1,0:T(8,128)(2,1)} %get-tuple-element.33), channel_id=1, source_target_pairs={{0,64},{64,128},{128,192},{192,0},{1,65},{65,129},{129,193},{193,1... | collective-permute-start | bytes 196616 | tf_op jit(solution)/shard_map/ppermute | solution.py:326
  3.9 7.7 %collective-permute-start.1 = (bf16[4,64,128]{2,1,0:T(8,128)(2,1)}, bf16[4,64,128]{2,1,0:T(8,128)(2,1)S(1)}, u32[]{:S(2)}, u32[]{:S(2)}) collective-permute-start(bf16[4,64,128]{2,1,0:T(8,128)(2,1)} %get-tuple-element.34), channel_id=1, source_target_pairs={{0,128},{64,192},{128,0},{192,64},{1,129},{65,193},{129,1},{193,65... | collective-permute-start | bytes 196616 | tf_op jit(solution)/shard_map/ppermute | solution.py:326
  6.6 5.1 %collective-permute-start.2 = (bf16[4,64,128]{2,1,0:T(8,128)(2,1)}, bf16[4,64,128]{2,1,0:T(8,128)(2,1)S(1)}, u32[]{:S(2)}, u32[]{:S(2)}) collective-permute-start(bf16[4,64,128]{2,1,0:T(8,128)(2,1)} %get-tuple-element.35), channel_id=1, source_target_pairs={{0,192},{64,0},{128,64},{192,128},{1,193},{65,1},{129,65},{193,129... | collective-permute-start | bytes 196616 | tf_op jit(solution)/shard_map/ppermute | solution.py:326
  7.6 2.4 %copy-start.2 = (bf16[64,64,256]{2,1,0:T(8,128)(2,1)S(1)}, bf16[64,64,256]{2,1,0:T(8,128)(2,1)}, u32[]{:S(2)}) copy-start(bf16[64,64,256]{2,1,0:T(8,128)(2,1)} %refs_8_.1) | copy-start | bytes 6291460
  10.1 26.1 %collective-permute-start.12 = (bf16[32,64,256]{2,1,0:T(8,128)(2,1)S(1)}, bf16[32,64,256]{2,1,0:T(8,128)(2,1)S(1)}, u32[]{:S(2)}, u32[]{:S(2)}) collective-permute-start(bf16[32,64,256]{2,1,0:T(8,128)(2,1)S(1)} %constant_dynamic-slice_fusion), channel_id=1, source_target_pairs={{0,192},{64,0},{128,64},{192,128},{1,193},{65,1},{129,65},{193,129... | collective-permute-start | bytes 3145736 | tf_op jit(solution)/shard_map/ppermute | solution.py:326
  10.2 26.0 %collective-permute-start.11 = (bf16[32,64,256]{2,1,0:T(8,128)(2,1)S(1)}, bf16[32,64,256]{2,1,0:T(8,128)(2,1)S(1)}, u32[]{:S(2)}, u32[]{:S(2)}) collective-permute-start(bf16[32,64,256]{2,1,0:T(8,128)(2,1)S(1)} %constant_dynamic-slice_fusion), channel_id=1, source_target_pairs={{0,64},{64,128},{128,192},{192,0},{1,65},{65,129},{129,193},{193,1... | collective-permute-start | bytes 3145736 | tf_op jit(solution)/shard_map/ppermute | solution.py:326
  11.7 0.6 copy-start.11
  11.7 0.6 copy-start.12
  12.3 0.6 copy-start.13
  14.7 7.7 %collective-permute-start.4 = (bf16[528,256]{1,0:T(8,128)(2,1)}, bf16[528,256]{1,0:T(8,128)(2,1)S(1)}, u32[]{:S(2)}, u32[]{:S(2)}) collective-permute-start(bf16[528,256]{1,0:T(8,128)(2,1)} %join_k.1.refs_0_), channel_id=1, source_target_pairs={{0,1},{1,0},{2,3},{3,2},{4,5},{5,4},{6,7},{7,6},{8,9},{9,8},{10,11... | collective-permute-start | bytes 811016 | tf_op jit(solution)/shard_map/ppermute | solution.py:338
  16.8 9.3 %collective-permute-start.3 = (bf16[528,256]{1,0:T(8,128)(2,1)}, bf16[528,256]{1,0:T(8,128)(2,1)S(1)}, u32[]{:S(2)}, u32[]{:S(2)}) collective-permute-start(bf16[528,256]{1,0:T(8,128)(2,1)} %join_k.1.refs_0_), channel_id=1, source_target_pairs={{0,8},{1,57},{8,16},{9,1},{16,24},{17,9},{24,32},{25,17},{32,40},{... | collective-permute-start | bytes 811016 | tf_op jit(solution)/shard_map/ppermute | solution.py:334
  22.4 7.0 %collective-permute-start.5 = (bf16[528,256]{1,0:T(8,128)(2,1)S(1)}, bf16[528,256]{1,0:T(8,128)(2,1)S(1)}, u32[]{:S(2)}, u32[]{:S(2)}) collective-permute-start(bf16[528,256]{1,0:T(8,128)(2,1)S(1)} %collective-permute-done.4), channel_id=1, source_target_pairs={{0,8},{1,57},{8,16},{9,1},{16,24},{17,9},{24,32},{25,17},{32,40},{... | collective-permute-start | bytes 811016 | tf_op jit(solution)/shard_map/ppermute | solution.py:334
  26.1 27.1 %copy-start.8 = (bf16[528,256]{1,0:T(8,128)(2,1)}, bf16[528,256]{1,0:T(8,128)(2,1)S(1)}, u32[]{:S(2)}) copy-start(bf16[528,256]{1,0:T(8,128)(2,1)S(1)} %collective-permute-done.3.refs_1_) | copy-start | bytes 811012
  26.1 6.7 %collective-permute-start.6 = (bf16[528,256]{1,0:T(8,128)(2,1)S(1)}, bf16[528,256]{1,0:T(8,128)(2,1)S(1)}, u32[]{:S(2)}, u32[]{:S(2)}) collective-permute-start(bf16[528,256]{1,0:T(8,128)(2,1)S(1)} %collective-permute-done.3.refs_1_), channel_id=1, source_target_pairs={{0,8},{1,57},{8,16},{9,1},{16,24},{17,9},{24,32},{25,17},{32,40},{... | collective-permute-start | bytes 811016 | tf_op jit(solution)/shard_map/ppermute | solution.py:334
  29.4 6.8 %copy-start.9 = (bf16[528,256]{1,0:T(8,128)(2,1)}, bf16[528,256]{1,0:T(8,128)(2,1)S(1)}, u32[]{:S(2)}) copy-start(bf16[528,256]{1,0:T(8,128)(2,1)S(1)} %collective-permute-done.5.refs_2_) | copy-start | bytes 811012
  29.4 6.8 %collective-permute-start.7 = (bf16[528,256]{1,0:T(8,128)(2,1)S(1)}, bf16[528,256]{1,0:T(8,128)(2,1)}, u32[]{:S(2)}, u32[]{:S(2)}) collective-permute-start(bf16[528,256]{1,0:T(8,128)(2,1)S(1)} %collective-permute-done.5.refs_2_), channel_id=1, source_target_pairs={{0,8},{1,57},{8,16},{9,1},{16,24},{17,9},{24,32},{25,17},{32,40},{... | collective-permute-start | bytes 811016 | tf_op jit(solution)/shard_map/ppermute | solution.py:334
  32.8 5.2 %copy-start.10 = (bf16[528,256]{1,0:T(8,128)(2,1)}, bf16[528,256]{1,0:T(8,128)(2,1)S(1)}, u32[]{:S(2)}) copy-start(bf16[528,256]{1,0:T(8,128)(2,1)S(1)} %collective-permute-done.6.refs_3_) | copy-start | bytes 811012
  32.8 9.1 %collective-permute-start.8 = (bf16[528,256]{1,0:T(8,128)(2,1)S(1)}, bf16[528,256]{1,0:T(8,128)(2,1)}, u32[]{:S(2)}, u32[]{:S(2)}) collective-permute-start(bf16[528,256]{1,0:T(8,128)(2,1)S(1)} %collective-permute-done.6.refs_3_), channel_id=1, source_target_pairs={{0,8},{1,57},{8,16},{9,1},{16,24},{17,9},{24,32},{25,17},{32,40},{... | collective-permute-start | bytes 811016 | tf_op jit(solution)/shard_map/ppermute | solution.py:334
  36.2 20.6 %copy-start.4 = (bf16[32,64,256]{2,1,0:T(8,128)(2,1)}, bf16[32,64,256]{2,1,0:T(8,128)(2,1)S(1)}, u32[]{:S(2)}) copy-start(bf16[32,64,256]{2,1,0:T(8,128)(2,1)S(1)} %collective-permute-done.12.refs_12_) | copy-start | bytes 3145732
  36.3 20.6 %copy-start.5 = (bf16[32,64,256]{2,1,0:T(8,128)(2,1)}, bf16[32,64,256]{2,1,0:T(8,128)(2,1)S(1)}, u32[]{:S(2)}) copy-start(bf16[32,64,256]{2,1,0:T(8,128)(2,1)S(1)} %collective-permute-done.11.refs_9_) | copy-start | bytes 3145732
  36.3 13.7 %collective-permute-start.14 = (bf16[16,64,256]{2,1,0:T(8,128)(2,1)S(1)}, bf16[16,64,256]{2,1,0:T(8,128)(2,1)}, u32[]{:S(2)}, u32[]{:S(2)}) collective-permute-start(bf16[16,64,256]{2,1,0:T(8,128)(2,1)S(1)} %slice.7), channel_id=1, source_target_pairs={{0,192},{64,0},{128,64},{192,128},{1,193},{65,1},{129,65},{193,129... | collective-permute-start | bytes 1572872 | tf_op jit(solution)/shard_map/ppermute | solution.py:326
  37.5 13.4 %collective-permute-start.13 = (bf16[16,64,256]{2,1,0:T(8,128)(2,1)S(1)}, bf16[16,64,256]{2,1,0:T(8,128)(2,1)}, u32[]{:S(2)}, u32[]{:S(2)}) collective-permute-start(bf16[16,64,256]{2,1,0:T(8,128)(2,1)S(1)} %slice.6), channel_id=1, source_target_pairs={{0,64},{64,128},{128,192},{192,0},{1,65},{65,129},{129,193},{193,1... | collective-permute-start | bytes 1572872 | tf_op jit(solution)/shard_map/ppermute | solution.py:326
  38.0 7.7 %collective-permute-start.9 = (bf16[528,256]{1,0:T(8,128)(2,1)}, bf16[528,256]{1,0:T(8,128)(2,1)}, u32[]{:S(2)}, u32[]{:S(2)}) collective-permute-start(bf16[528,256]{1,0:T(8,128)(2,1)} %collective-permute-done.7.refs_4_), channel_id=1, source_target_pairs={{0,8},{1,57},{8,16},{9,1},{16,24},{17,9},{24,32},{25,17},{32,40},{... | collective-permute-start | bytes 811016 | tf_op jit(solution)/shard_map/ppermute | solution.py:334
  41.9 11.3 %collective-permute-start.10 = (bf16[528,256]{1,0:T(8,128)(2,1)}, bf16[528,256]{1,0:T(8,128)(2,1)}, u32[]{:S(2)}, u32[]{:S(2)}) collective-permute-start(bf16[528,256]{1,0:T(8,128)(2,1)} %collective-permute-done.8.refs_5_), channel_id=1, source_target_pairs={{0,8},{1,57},{8,16},{9,1},{16,24},{17,9},{24,32},{25,17},{32,40},{... | collective-permute-start | bytes 811016 | tf_op jit(solution)/shard_map/ppermute | solution.py:334
  43.4 14.4 %copy-start = (s32[2]{0:T(128)S(1)}, s32[2]{0:T(128)}, u32[]{:S(2)}) copy-start(s32[2]{0:T(128)} %pad_add_fusion.me_ref) | copy-start | bytes 28
  43.4 13.5 %collective-permute-start.15 = (bf16[32,64,256]{2,1,0:T(8,128)(2,1)S(1)}, bf16[32,64,256]{2,1,0:T(8,128)(2,1)}, u32[]{:S(2)}, u32[]{:S(2)}) collective-permute-start(bf16[32,64,256]{2,1,0:T(8,128)(2,1)S(1)} %collective-permute-done.11.refs_9_), channel_id=1, source_target_pairs={{0,1},{1,0},{2,3},{3,2},{4,5},{5,4},{6,7},{7,6},{8,9},{9,8},{10,11... | collective-permute-start | bytes 3145736 | tf_op jit(solution)/shard_map/ppermute | solution.py:338
  45.7 11.3 %collective-permute-start.18 = (bf16[32,64,256]{2,1,0:T(8,128)(2,1)S(1)}, bf16[32,64,256]{2,1,0:T(8,128)(2,1)}, u32[]{:S(2)}, u32[]{:S(2)}) collective-permute-start(bf16[32,64,256]{2,1,0:T(8,128)(2,1)S(1)} %collective-permute-done.12.refs_12_), channel_id=1, source_target_pairs={{0,1},{1,0},{2,3},{3,2},{4,5},{5,4},{6,7},{7,6},{8,9},{9,8},{10,11... | collective-permute-start | bytes 3145736 | tf_op jit(solution)/shard_map/ppermute | solution.py:338
  50.0 6.9 %collective-permute-start.17 = (bf16[16,64,256]{2,1,0:T(8,128)(2,1)}, bf16[16,64,256]{2,1,0:T(8,128)(2,1)S(1)}, u32[]{:S(2)}, u32[]{:S(2)}) collective-permute-start(bf16[16,64,256]{2,1,0:T(8,128)(2,1)} %collective-permute-done.14.refs_11_), channel_id=1, source_target_pairs={{0,1},{1,0},{2,3},{3,2},{4,5},{5,4},{6,7},{7,6},{8,9},{9,8},{10,11... | collective-permute-start | bytes 1572872 | tf_op jit(solution)/shard_map/ppermute | solution.py:338
  50.8 6.1 %collective-permute-start.16 = (bf16[16,64,256]{2,1,0:T(8,128)(2,1)}, bf16[16,64,256]{2,1,0:T(8,128)(2,1)S(1)}, u32[]{:S(2)}, u32[]{:S(2)}) collective-permute-start(bf16[16,64,256]{2,1,0:T(8,128)(2,1)} %collective-permute-done.13.refs_10_), channel_id=1, source_target_pairs={{0,1},{1,0},{2,3},{3,2},{4,5},{5,4},{6,7},{7,6},{8,9},{9,8},{10,11... | collective-permute-start | bytes 1572872 | tf_op jit(solution)/shard_map/ppermute | solution.py:338
  56.9 0.8 copy-start.6
  56.9 0.9 %copy-start.7 = (bf16[16,64,256]{2,1,0:T(8,128)(2,1)}, bf16[16,64,256]{2,1,0:T(8,128)(2,1)S(1)}, u32[]{:S(2)}) copy-start(bf16[16,64,256]{2,1,0:T(8,128)(2,1)S(1)} %collective-permute-done.16.refs_14_) | copy-start | bytes 1572868
  57.9 0.7 copy-start.1
  68.0 17.2 %copy-start.3 = (f32[8,64,256]{2,1,0:T(8,128)S(1)}, f32[8,64,256]{2,1,0:T(8,128)}, u32[]{:S(2)}) copy-start(f32[8,64,256]{2,1,0:T(8,128)} %get-tuple-element.45) | copy-start | bytes 1572868
  68.0 1.6 %collective-permute-start.19 = (bf16[8,64,256]{2,1,0:T(8,128)(2,1)S(1)}, bf16[8,64,256]{2,1,0:T(8,128)(2,1)S(1)}, u32[]{:S(2)}, u32[]{:S(2)}) collective-permute-start(bf16[8,64,256]{2,1,0:T(8,128)(2,1)S(1)} %get-tuple-element.40), channel_id=1, source_target_pairs={{0,1},{1,0},{2,3},{3,2},{4,5},{5,4},{6,7},{7,6},{8,9},{9,8},{10,11... | collective-permute-start | bytes 786440 | tf_op jit(solution)/shard_map/ppermute | solution.py:338
  68.1 3.9 %collective-permute-start.21 = (bf16[8,64,256]{2,1,0:T(8,128)(2,1)S(1)}, bf16[8,64,256]{2,1,0:T(8,128)(2,1)S(1)}, u32[]{:S(2)}, u32[]{:S(2)}) collective-permute-start(bf16[8,64,256]{2,1,0:T(8,128)(2,1)S(1)} %get-tuple-element.42), channel_id=1, source_target_pairs={{0,1},{1,0},{2,3},{3,2},{4,5},{5,4},{6,7},{7,6},{8,9},{9,8},{10,11... | collective-permute-start | bytes 786440 | tf_op jit(solution)/shard_map/ppermute | solution.py:338
  68.6 4.2 %collective-permute-start.23 = (bf16[8,64,256]{2,1,0:T(8,128)(2,1)S(1)}, bf16[8,64,256]{2,1,0:T(8,128)(2,1)S(1)}, u32[]{:S(2)}, u32[]{:S(2)}) collective-permute-start(bf16[8,64,256]{2,1,0:T(8,128)(2,1)S(1)} %get-tuple-element.44), channel_id=1, source_target_pairs={{0,1},{1,0},{2,3},{3,2},{4,5},{5,4},{6,7},{7,6},{8,9},{9,8},{10,11... | collective-permute-start | bytes 786440 | tf_op jit(solution)/shard_map/ppermute | solution.py:338
  68.7 6.3 %collective-permute-start.25 = (bf16[8,64,256]{2,1,0:T(8,128)(2,1)S(1)}, bf16[8,64,256]{2,1,0:T(8,128)(2,1)S(1)}, u32[]{:S(2)}, u32[]{:S(2)}) collective-permute-start(bf16[8,64,256]{2,1,0:T(8,128)(2,1)S(1)} %get-tuple-element.46), channel_id=1, source_target_pairs={{0,1},{1,0},{2,3},{3,2},{4,5},{5,4},{6,7},{7,6},{8,9},{9,8},{10,11... | collective-permute-start | bytes 786440 | tf_op jit(solution)/shard_map/ppermute | solution.py:338
  69.7 9.4 %collective-permute-start.20 = (bf16[8,64,256]{2,1,0:T(8,128)(2,1)S(1)}, bf16[8,64,256]{2,1,0:T(8,128)(2,1)S(1)}, u32[]{:S(2)}, u32[]{:S(2)}) collective-permute-start(bf16[8,64,256]{2,1,0:T(8,128)(2,1)S(1)} %add_convert_fusion.2), channel_id=1, source_target_pairs={{0,4},{2,6},{4,0},{6,2},{1,5},{3,7},{5,1},{7,3},{8,12},{10,14},{12... | collective-permute-start | bytes 786440 | tf_op jit(solution)/shard_map/ppermute | solution.py:326
  72.1 13.0 %collective-permute-start.22 = (bf16[8,64,256]{2,1,0:T(8,128)(2,1)S(1)}, bf16[8,64,256]{2,1,0:T(8,128)(2,1)S(1)}, u32[]{:S(2)}, u32[]{:S(2)}) collective-permute-start(bf16[8,64,256]{2,1,0:T(8,128)(2,1)S(1)} %add_convert_fusion.1), channel_id=1, source_target_pairs={{0,2},{2,4},{4,6},{6,0},{1,3},{3,5},{5,7},{7,1},{8,10},{10,12},{12... | collective-permute-start | bytes 786440 | tf_op jit(solution)/shard_map/ppermute | solution.py:326
  72.9 12.3 %collective-permute-start.24 = (bf16[8,64,256]{2,1,0:T(8,128)(2,1)S(1)}, bf16[8,64,256]{2,1,0:T(8,128)(2,1)S(1)}, u32[]{:S(2)}, u32[]{:S(2)}) collective-permute-start(bf16[8,64,256]{2,1,0:T(8,128)(2,1)S(1)} %add_convert_fusion), channel_id=1, source_target_pairs={{0,6},{2,0},{4,2},{6,4},{1,7},{3,1},{5,3},{7,5},{8,14},{10,8},{12,... | collective-permute-start | bytes 786440 | tf_op jit(solution)/shard_map/ppermute | solution.py:326

commit v8 on v7

--- a/solution.py
+++ b/solution.py
@@ -44,7 +44,7 @@
     named = jnp.where(row == 0, owner_ref[...][None], jnp.where(row == 1, target_ref[...][None], 0))
     slot = lax.broadcasted_iota(I32, (slots, products), 0)
     spread = lax.broadcasted_iota(I32, (slots, products), 1) // TPS == slot
-    named = jnp.dot(named.astype(F32), spread.astype(F32), precision=lax.Precision.HIGHEST)
+    named = exact_dot(named, spread.astype(F32).astype(BF16))
     own, target = named[0:1].astype(I32), named[1:2].astype(I32)
     a, b = a_ref[...][None], b_ref[...][None]
     place = jnp.where(live_ref[...][None] > 0, own // (N_X * N_CORE), -1)

time: 86.3 us -> 87.6 us (1.015)
  starting transfers between devices: 46.6 us -> 48.3 us
    ppermute x9, starting transfers between devices: 11.1 us -> 12.3 us  [other_core(): return lax.ppermute(value, 'core', [(0, 1), (1, 0)])]
where the time goes in v8:
time: 87.6 us; the launch traced here: 87.5 us
  starting transfers between devices  48.3 us (55%)
  Pallas kernels  19.2 us (22%)
  waiting for transfers between devices  14.9 us (17%)
  local copies, waits for them, and re-layouts  3.06 us (3%)
  other arithmetic  1.74 us (2%)
    ppermute x7, starting transfers between devices, apart(): return lax.ppermute(value, (axis, 'core'), perm)  21.4 us
    ppermute x10, starting transfers between devices, shift_by(): lax.ppermute(value, axis, [(i, (i + step) % size) for i in range(size)])  14.6 us
    ppermute x9, starting transfers between devices, other_core(): return lax.ppermute(value, 'core', [(0, 1), (1, 0)])  12.3 us
    ppermute x10, waiting for transfers between devices, shift_by(): lax.ppermute(value, axis, [(i, (i + step) % size) for i in range(size)])  9.64 us
    pallas_call x1, Pallas kernels, products(): pl.pallas_call(products_kernel, out_shape=[jax.ShapeDtypeStruct(shape, ki...  9.63 us
    ppermute x7, waiting for transfers between devices, apart(): return lax.ppermute(value, (axis, 'core'), perm)  4.71 us
    pallas_call x1, Pallas kernels, sort_products(): pl.pallas_call(sort_kernel, out_shape=jax.ShapeDtypeStruct((LIST // MOST...  3.64 us
    unnamed x28, local copies, waits for them, and re-layouts  2.88 us
  transfers between devices with their start and end apart: 26, of which 6 were waited for; matrix products, arithmetic and copies ran while one was open for 1% of the time, Pallas kernels for 9%

profile of v8, /device:TPU:1, one launch (start us, length us, event | category | flops | bytes accessed | tf_op | source)
XLA Modules:
  0.0 87.5 jit_solution(5785361824457919143)
XLA Ops:
  0.0 1.8 %spread_rows.1 = (bf16[4,64,128]{2,1,0:T(8,128)(2,1)}, bf16[4,64,128]{2,1,0:T(8,128)(2,1)}, bf16[4,64,128]{2,1,0:T(8,128)(2,1)}, bf16[4,64,128]{2,1,0:T(8,128)(2,1)}) custom-call(s32[1]{0:T(128)} %bitcast.2.rep_ref, bf16[8,64,256]{2,1,0:T(8,128)(2,1)} %bitcast.6), custom_call_target="tpu_custom_call" | custom-call | tf_op jit(solution)/shard_map/spread_rows/pallas_call | solution.py:102
  1.8 2.1 %collective-permute-start = (bf16[4,64,128]{2,1,0:T(8,128)(2,1)}, bf16[4,64,128]{2,1,0:T(8,128)(2,1)S(1)}, u32[]{:S(2)}, u32[]{:S(2)}) collective-permute-start(bf16[4,64,128]{2,1,0:T(8,128)(2,1)} %get-tuple-element.33), channel_id=1, source_target_pairs={{0,64},{64,128},{128,192},{192,0},{1,65},{65,129},{129,193},{193,1... | collective-permute-start | bytes 196616 | tf_op jit(solution)/shard_map/ppermute | solution.py:326
  3.9 2.6 %collective-permute-start.1 = (bf16[4,64,128]{2,1,0:T(8,128)(2,1)}, bf16[4,64,128]{2,1,0:T(8,128)(2,1)S(1)}, u32[]{:S(2)}, u32[]{:S(2)}) collective-permute-start(bf16[4,64,128]{2,1,0:T(8,128)(2,1)} %get-tuple-element.34), channel_id=1, source_target_pairs={{0,128},{64,192},{128,0},{192,64},{1,129},{65,193},{129,1},{193,65... | collective-permute-start | bytes 196616 | tf_op jit(solution)/shard_map/ppermute | solution.py:326
  6.6 1.1 %collective-permute-start.2 = (bf16[4,64,128]{2,1,0:T(8,128)(2,1)}, bf16[4,64,128]{2,1,0:T(8,128)(2,1)S(1)}, u32[]{:S(2)}, u32[]{:S(2)}) collective-permute-start(bf16[4,64,128]{2,1,0:T(8,128)(2,1)} %get-tuple-element.35), channel_id=1, source_target_pairs={{0,192},{64,0},{128,64},{192,128},{1,193},{65,1},{129,65},{193,129... | collective-permute-start | bytes 196616 | tf_op jit(solution)/shard_map/ppermute | solution.py:326
  7.6 2.3 %product_table.1.table_ref = bf16[16,256]{1,0:T(8,128)(2,1)} custom-call(s32[1]{0:T(128)} %bitcast.4.x_ref, s32[384]{0:T(512)} %a_ref.1, s32[384]{0:T(512)} %b_ref.1, s32[384]{0:T(512)} %live_ref.1, s32[48]{0:T(128)} %bitcast.7, s32[48]{0:T(128)} %target_ref.1), custom_call_target="tpu_custom_call" | custom-call | flops 8000000000 | bytes 65536 | tf_op jit(solution)/shard_map/product_table/pallas_call | solution.py:78
  10.0 0.1 constant_dynamic-slice_fusion
  10.1 0.1 collective-permute-start.12
  10.2 1.5 %collective-permute-start.11 = (bf16[32,64,256]{2,1,0:T(8,128)(2,1)S(1)}, bf16[32,64,256]{2,1,0:T(8,128)(2,1)S(1)}, u32[]{:S(2)}, u32[]{:S(2)}) collective-permute-start(bf16[32,64,256]{2,1,0:T(8,128)(2,1)S(1)} %constant_dynamic-slice_fusion), channel_id=1, source_target_pairs={{0,64},{64,128},{128,192},{192,0},{1,65},{65,129},{129,193},{193,1... | collective-permute-start | bytes 3145736 | tf_op jit(solution)/shard_map/ppermute | solution.py:326
  11.6 0.0 collective-permute-done.refs_1_
  11.6 0.0 collective-permute-done.1.refs_2_
  11.6 0.0 collective-permute-done.2.refs_3_
  11.7 0.6 copy-done.11
  12.2 0.0 copy-done.12
  12.3 0.6 copy-done.13
  12.9 1.8 %join_k.1.refs_0_ = bf16[528,256]{1,0:T(8,128)(2,1)} custom-call(bf16[16,256]{1,0:T(8,128)(2,1)} %product_table.1.table_ref, bf16[4,64,128]{2,1,0:T(8,128)(2,1)} %get-tuple-element.32.refs_0_, bf16[4,64,128]{2,1,0:T(8,128)(2,1)} %copy-done.11, bf16[4,64,128]{2,1,0:T(8,128)(2,1)} %copy-done.12, bf16[4,64,128]{2,1,0:T(8,128)(2,1)} %copy-done.13), custom_call_target="tpu_custom_call" | custom-call | flops 20000000000 | bytes 524288 | tf_op jit(solution)/shard_map/join_k/pallas_call | solution.py:125
  14.7 2.1 %collective-permute-start.4 = (bf16[528,256]{1,0:T(8,128)(2,1)}, bf16[528,256]{1,0:T(8,128)(2,1)S(1)}, u32[]{:S(2)}, u32[]{:S(2)}) collective-permute-start(bf16[528,256]{1,0:T(8,128)(2,1)} %join_k.1.refs_0_), channel_id=1, source_target_pairs={{0,1},{1,0},{2,3},{3,2},{4,5},{5,4},{6,7},{7,6},{8,9},{9,8},{10,11... | collective-permute-start | bytes 811016 | tf_op jit(solution)/shard_map/ppermute | solution.py:338
  16.8 5.6 %collective-permute-start.3 = (bf16[528,256]{1,0:T(8,128)(2,1)}, bf16[528,256]{1,0:T(8,128)(2,1)S(1)}, u32[]{:S(2)}, u32[]{:S(2)}) collective-permute-start(bf16[528,256]{1,0:T(8,128)(2,1)} %join_k.1.refs_0_), channel_id=1, source_target_pairs={{0,8},{1,57},{8,16},{9,1},{16,24},{17,9},{24,32},{25,17},{32,40},{... | collective-permute-start | bytes 811016 | tf_op jit(solution)/shard_map/ppermute | solution.py:334
  22.3 0.0 collective-permute-done.4
  22.3 1.4 %collective-permute-start.5 = (bf16[528,256]{1,0:T(8,128)(2,1)S(1)}, bf16[528,256]{1,0:T(8,128)(2,1)S(1)}, u32[]{:S(2)}, u32[]{:S(2)}) collective-permute-start(bf16[528,256]{1,0:T(8,128)(2,1)S(1)} %collective-permute-done.4), channel_id=1, source_target_pairs={{0,8},{1,57},{8,16},{9,1},{16,24},{17,9},{24,32},{25,17},{32,40},{... | collective-permute-start | bytes 811016 | tf_op jit(solution)/shard_map/ppermute | solution.py:334
  23.7 2.3 %collective-permute-done.3.refs_1_ = bf16[528,256]{1,0:T(8,128)(2,1)S(1)} collective-permute-done((bf16[528,256]{1,0:T(8,128)(2,1)}, bf16[528,256]{1,0:T(8,128)(2,1)S(1)}, u32[]{:S(2)}, u32[]{:S(2)}) %collective-permute-start.3) | collective-permute-done | bytes 270368 | tf_op jit(solution)/shard_map/ppermute | solution.py:334
  26.1 3.3 %collective-permute-start.6 = (bf16[528,256]{1,0:T(8,128)(2,1)S(1)}, bf16[528,256]{1,0:T(8,128)(2,1)S(1)}, u32[]{:S(2)}, u32[]{:S(2)}) collective-permute-start(bf16[528,256]{1,0:T(8,128)(2,1)S(1)} %collective-permute-done.3.refs_1_), channel_id=1, source_target_pairs={{0,8},{1,57},{8,16},{9,1},{16,24},{17,9},{24,32},{25,17},{32,40},{... | collective-permute-start | bytes 811016 | tf_op jit(solution)/shard_map/ppermute | solution.py:334
  29.4 0.0 collective-permute-done.5.refs_2_
  29.4 2.9 %collective-permute-start.7 = (bf16[528,256]{1,0:T(8,128)(2,1)S(1)}, bf16[528,256]{1,0:T(8,128)(2,1)}, u32[]{:S(2)}, u32[]{:S(2)}) collective-permute-start(bf16[528,256]{1,0:T(8,128)(2,1)S(1)} %collective-permute-done.5.refs_2_), channel_id=1, source_target_pairs={{0,8},{1,57},{8,16},{9,1},{16,24},{17,9},{24,32},{25,17},{32,40},{... | collective-permute-start | bytes 811016 | tf_op jit(solution)/shard_map/ppermute | solution.py:334
  32.3 0.5 collective-permute-done.6.refs_3_
  32.8 3.4 %collective-permute-start.8 = (bf16[528,256]{1,0:T(8,128)(2,1)S(1)}, bf16[528,256]{1,0:T(8,128)(2,1)}, u32[]{:S(2)}, u32[]{:S(2)}) collective-permute-start(bf16[528,256]{1,0:T(8,128)(2,1)S(1)} %collective-permute-done.6.refs_3_), channel_id=1, source_target_pairs={{0,8},{1,57},{8,16},{9,1},{16,24},{17,9},{24,32},{25,17},{32,40},{... | collective-permute-start | bytes 811016 | tf_op jit(solution)/shard_map/ppermute | solution.py:334
  36.2 0.0 collective-permute-done.7.refs_4_
  36.2 0.0 collective-permute-done.12.refs_12_
  36.2 0.0 collective-permute-done.11.refs_9_
  36.3 1.1 %collective-permute-start.14 = (bf16[16,64,256]{2,1,0:T(8,128)(2,1)S(1)}, bf16[16,64,256]{2,1,0:T(8,128)(2,1)}, u32[]{:S(2)}, u32[]{:S(2)}) collective-permute-start(bf16[16,64,256]{2,1,0:T(8,128)(2,1)S(1)} %slice.7), channel_id=1, source_target_pairs={{0,192},{64,0},{128,64},{192,128},{1,193},{65,1},{129,65},{193,129... | collective-permute-start | bytes 1572872 | tf_op jit(solution)/shard_map/ppermute | solution.py:326
  37.4 0.5 collective-permute-start.13
  37.9 3.9 %collective-permute-start.9 = (bf16[528,256]{1,0:T(8,128)(2,1)}, bf16[528,256]{1,0:T(8,128)(2,1)}, u32[]{:S(2)}, u32[]{:S(2)}) collective-permute-start(bf16[528,256]{1,0:T(8,128)(2,1)} %collective-permute-done.7.refs_4_), channel_id=1, source_target_pairs={{0,8},{1,57},{8,16},{9,1},{16,24},{17,9},{24,32},{25,17},{32,40},{... | collective-permute-start | bytes 811016 | tf_op jit(solution)/shard_map/ppermute | solution.py:334
  41.9 0.0 collective-permute-done.8.refs_5_
  41.9 0.9 %collective-permute-start.10 = (bf16[528,256]{1,0:T(8,128)(2,1)}, bf16[528,256]{1,0:T(8,128)(2,1)}, u32[]{:S(2)}, u32[]{:S(2)}) collective-permute-start(bf16[528,256]{1,0:T(8,128)(2,1)} %collective-permute-done.8.refs_5_), channel_id=1, source_target_pairs={{0,8},{1,57},{8,16},{9,1},{16,24},{17,9},{24,32},{25,17},{32,40},{... | collective-permute-start | bytes 811016 | tf_op jit(solution)/shard_map/ppermute | solution.py:334
  42.8 0.6 pad_add_fusion.me_ref
  43.4 0.3 collective-permute-start.15
  43.8 1.9 %collective-permute-done.9.refs_6_ = bf16[528,256]{1,0:T(8,128)(2,1)} collective-permute-done((bf16[528,256]{1,0:T(8,128)(2,1)}, bf16[528,256]{1,0:T(8,128)(2,1)}, u32[]{:S(2)}, u32[]{:S(2)}) %collective-permute-start.9) | collective-permute-done | bytes 270368 | tf_op jit(solution)/shard_map/ppermute | solution.py:334
  45.6 4.3 %collective-permute-start.18 = (bf16[32,64,256]{2,1,0:T(8,128)(2,1)S(1)}, bf16[32,64,256]{2,1,0:T(8,128)(2,1)}, u32[]{:S(2)}, u32[]{:S(2)}) collective-permute-start(bf16[32,64,256]{2,1,0:T(8,128)(2,1)S(1)} %collective-permute-done.12.refs_12_), channel_id=1, source_target_pairs={{0,1},{1,0},{2,3},{3,2},{4,5},{5,4},{6,7},{7,6},{8,9},{9,8},{10,11... | collective-permute-start | bytes 3145736 | tf_op jit(solution)/shard_map/ppermute | solution.py:338
  49.9 0.0 collective-permute-done.14.refs_11_
  49.9 0.9 collective-permute-start.17
  50.8 0.0 collective-permute-done.13.refs_10_
  50.8 2.4 %collective-permute-start.16 = (bf16[16,64,256]{2,1,0:T(8,128)(2,1)}, bf16[16,64,256]{2,1,0:T(8,128)(2,1)S(1)}, u32[]{:S(2)}, u32[]{:S(2)}) collective-permute-start(bf16[16,64,256]{2,1,0:T(8,128)(2,1)} %collective-permute-done.13.refs_10_), channel_id=1, source_target_pairs={{0,1},{1,0},{2,3},{3,2},{4,5},{5,4},{6,7},{7,6},{8,9},{9,8},{10,11... | collective-permute-start | bytes 1572872 | tf_op jit(solution)/shard_map/ppermute | solution.py:338
  53.2 0.0 collective-permute-done.10.refs_7_
  53.2 3.6 %sort_products.1.listed = s32[11,128]{1,0:T(8,128)} custom-call(s32[2]{0:T(128)} %pad_add_fusion.me_ref, bf16[528,256]{1,0:T(8,128)(2,1)} %join_k.1.refs_0_, bf16[528,256]{1,0:T(8,128)(2,1)} %copy-done.8, bf16[528,256]{1,0:T(8,128)(2,1)} %copy-done.9, bf16[528,256]{1,0:T(8,128)(2,1)} %copy-done.10, bf16[528,256]{1,0:T(8,128)(2,1)} %collective-permute-done.7.refs_4_, ...), custom_call_target="tpu_custom_call" | custom-call | flops 20000000000 | bytes 65536 | tf_op jit(solution)/shard_map/sort_products/pallas_call | solution.py:211
  56.9 0.0 collective-permute-done.16.refs_14_
  56.9 0.0 copy-start.7
  56.9 0.0 collective-permute-done.18.refs_16_
  56.9 0.7 copy-done.6
  57.6 0.2 copy-done.7
  57.8 0.7 copy-done.1
  58.5 9.6 %products.1 = (bf16[8,64,256]{2,1,0:T(8,128)(2,1)S(1)}, bf16[8,64,256]{2,1,0:T(8,128)(2,1)S(1)}, bf16[8,64,256]{2,1,0:T(8,128)(2,1)S(1)}, bf16[8,64,256]{2,1,0:T...) custom-call(s32[2]{0:T(128)S(1)} %copy-done, ...), custom_call_target="tpu_custom_call" | custom-call | flops 3221225472 | bytes 10485760 | tf_op jit(solution)/shard_map/products/pallas_call | solution.py:305
  68.2 1.7 %collective-permute-start.19 = (bf16[8,64,256]{2,1,0:T(8,128)(2,1)S(1)}, bf16[8,64,256]{2,1,0:T(8,128)(2,1)S(1)}, u32[]{:S(2)}, u32[]{:S(2)}) collective-permute-start(bf16[8,64,256]{2,1,0:T(8,128)(2,1)S(1)} %get-tuple-element.40), channel_id=1, source_target_pairs={{0,1},{1,0},{2,3},{3,2},{4,5},{5,4},{6,7},{7,6},{8,9},{9,8},{10,11... | collective-permute-start | bytes 786440 | tf_op jit(solution)/shard_map/ppermute | solution.py:338
  69.9 0.1 collective-permute-start.21
  70.0 0.4 collective-permute-start.23
  70.4 0.1 collective-permute-start.25
  70.5 0.6 collective-permute-done.19
  71.0 0.1 add_convert_fusion.2
  71.1 2.8 %collective-permute-start.20 = (bf16[8,64,256]{2,1,0:T(8,128)(2,1)S(1)}, bf16[8,64,256]{2,1,0:T(8,128)(2,1)S(1)}, u32[]{:S(2)}, u32[]{:S(2)}) collective-permute-start(bf16[8,64,256]{2,1,0:T(8,128)(2,1)S(1)} %add_convert_fusion.2), channel_id=1, source_target_pairs={{0,4},{2,6},{4,0},{6,2},{1,5},{3,7},{5,1},{7,3},{8,12},{10,14},{12... | collective-permute-start | bytes 786440 | tf_op jit(solution)/shard_map/ppermute | solution.py:326
  73.9 0.1 add_convert_fusion.1
  74.0 0.1 collective-permute-start.22
  74.1 0.1 add_convert_fusion
  74.2 2.7 %collective-permute-start.24 = (bf16[8,64,256]{2,1,0:T(8,128)(2,1)S(1)}, bf16[8,64,256]{2,1,0:T(8,128)(2,1)S(1)}, u32[]{:S(2)}, u32[]{:S(2)}) collective-permute-start(bf16[8,64,256]{2,1,0:T(8,128)(2,1)S(1)} %add_convert_fusion), channel_id=1, source_target_pairs={{0,6},{2,0},{4,2},{6,4},{1,7},{3,1},{5,3},{7,5},{8,14},{10,8},{12,... | collective-permute-start | bytes 786440 | tf_op jit(solution)/shard_map/ppermute | solution.py:326
  76.9 3.3 %collective-permute-done.20 = bf16[8,64,256]{2,1,0:T(8,128)(2,1)S(1)} collective-permute-done((bf16[8,64,256]{2,1,0:T(8,128)(2,1)S(1)}, bf16[8,64,256]{2,1,0:T(8,128)(2,1)S(1)}, u32[]{:S(2)}, u32[]{:S(2)}) %collective-permute-start.20) | collective-permute-done | bytes 262176 | tf_op jit(solution)/shard_map/ppermute | solution.py:326
  80.3 6.3 %collective-permute-done.22 = bf16[8,64,256]{2,1,0:T(8,128)(2,1)S(1)} collective-permute-done((bf16[8,64,256]{2,1,0:T(8,128)(2,1)S(1)}, bf16[8,64,256]{2,1,0:T(8,128)(2,1)S(1)}, u32[]{:S(2)}, u32[]{:S(2)}) %collective-permute-start.22) | collective-permute-done | bytes 262176 | tf_op jit(solution)/shard_map/ppermute | solution.py:326
  86.6 0.9 %add_add_fusion = f32[8,64,256]{2,1,0:T(8,128)} fusion(f32[8,64,256]{2,1,0:T(8,128)S(1)} %copy-done.3, bf16[8,64,256]{2,1,0:T(8,128)(2,1)S(1)} %collective-permute-done.25, bf16[8,64,256]{2,1,0:T(8,128)(2,1)S(1)} %collective-permute-done.24, bf16[8,64,256]{2,1,0:T(8,128)(2,1)S(1)} %collective-permute-done.22, bf16[8,64,256]{2,1,0:T(8,128)(2,1)S(1)} %collective-permute-done.20), kind=kLoop, calls=%fused_computation | loop fusion | flops 1048576 | bytes 2097152 | tf_op jit(solution)/shard_map/add | solution.py:372
  (29 shorter events, 0.1 us)
Async XLA Ops:
  1.8 9.8 %collective-permute-start = (bf16[4,64,128]{2,1,0:T(8,128)(2,1)}, bf16[4,64,128]{2,1,0:T(8,128)(2,1)S(1)}, u32[]{:S(2)}, u32[]{:S(2)}) collective-permute-start(bf16[4,64,128]{2,1,0:T(8,128)(2,1)} %get-tuple-element.33), channel_id=1, source_target_pairs={{0,64},{64,128},{128,192},{192,0},{1,65},{65,129},{129,193},{193,1... | collective-permute-start | bytes 196616 | tf_op jit(solution)/shard_map/ppermute | solution.py:326
  3.9 7.7 %collective-permute-start.1 = (bf16[4,64,128]{2,1,0:T(8,128)(2,1)}, bf16[4,64,128]{2,1,0:T(8,128)(2,1)S(1)}, u32[]{:S(2)}, u32[]{:S(2)}) collective-permute-start(bf16[4,64,128]{2,1,0:T(8,128)(2,1)} %get-tuple-element.34), channel_id=1, source_target_pairs={{0,128},{64,192},{128,0},{192,64},{1,129},{65,193},{129,1},{193,65... | collective-permute-start | bytes 196616 | tf_op jit(solution)/shard_map/ppermute | solution.py:326
  6.6 5.1 %collective-permute-start.2 = (bf16[4,64,128]{2,1,0:T(8,128)(2,1)}, bf16[4,64,128]{2,1,0:T(8,128)(2,1)S(1)}, u32[]{:S(2)}, u32[]{:S(2)}) collective-permute-start(bf16[4,64,128]{2,1,0:T(8,128)(2,1)} %get-tuple-element.35), channel_id=1, source_target_pairs={{0,192},{64,0},{128,64},{192,128},{1,193},{65,1},{129,65},{193,129... | collective-permute-start | bytes 196616 | tf_op jit(solution)/shard_map/ppermute | solution.py:326
  7.6 2.3 %copy-start.2 = (bf16[64,64,256]{2,1,0:T(8,128)(2,1)S(1)}, bf16[64,64,256]{2,1,0:T(8,128)(2,1)}, u32[]{:S(2)}) copy-start(bf16[64,64,256]{2,1,0:T(8,128)(2,1)} %refs_8_.1) | copy-start | bytes 6291460
  10.1 26.1 %collective-permute-start.12 = (bf16[32,64,256]{2,1,0:T(8,128)(2,1)S(1)}, bf16[32,64,256]{2,1,0:T(8,128)(2,1)S(1)}, u32[]{:S(2)}, u32[]{:S(2)}) collective-permute-start(bf16[32,64,256]{2,1,0:T(8,128)(2,1)S(1)} %constant_dynamic-slice_fusion), channel_id=1, source_target_pairs={{0,192},{64,0},{128,64},{192,128},{1,193},{65,1},{129,65},{193,129... | collective-permute-start | bytes 3145736 | tf_op jit(solution)/shard_map/ppermute | solution.py:326
  10.2 26.0 %collective-permute-start.11 = (bf16[32,64,256]{2,1,0:T(8,128)(2,1)S(1)}, bf16[32,64,256]{2,1,0:T(8,128)(2,1)S(1)}, u32[]{:S(2)}, u32[]{:S(2)}) collective-permute-start(bf16[32,64,256]{2,1,0:T(8,128)(2,1)S(1)} %constant_dynamic-slice_fusion), channel_id=1, source_target_pairs={{0,64},{64,128},{128,192},{192,0},{1,65},{65,129},{129,193},{193,1... | collective-permute-start | bytes 3145736 | tf_op jit(solution)/shard_map/ppermute | solution.py:326
  11.6 0.6 copy-start.11
  11.6 0.6 copy-start.12
  12.3 0.6 copy-start.13
  14.7 7.7 %collective-permute-start.4 = (bf16[528,256]{1,0:T(8,128)(2,1)}, bf16[528,256]{1,0:T(8,128)(2,1)S(1)}, u32[]{:S(2)}, u32[]{:S(2)}) collective-permute-start(bf16[528,256]{1,0:T(8,128)(2,1)} %join_k.1.refs_0_), channel_id=1, source_target_pairs={{0,1},{1,0},{2,3},{3,2},{4,5},{5,4},{6,7},{7,6},{8,9},{9,8},{10,11... | collective-permute-start | bytes 811016 | tf_op jit(solution)/shard_map/ppermute | solution.py:338
  16.8 9.3 %collective-permute-start.3 = (bf16[528,256]{1,0:T(8,128)(2,1)}, bf16[528,256]{1,0:T(8,128)(2,1)S(1)}, u32[]{:S(2)}, u32[]{:S(2)}) collective-permute-start(bf16[528,256]{1,0:T(8,128)(2,1)} %join_k.1.refs_0_), channel_id=1, source_target_pairs={{0,8},{1,57},{8,16},{9,1},{16,24},{17,9},{24,32},{25,17},{32,40},{... | collective-permute-start | bytes 811016 | tf_op jit(solution)/shard_map/ppermute | solution.py:334
  22.3 7.0 %collective-permute-start.5 = (bf16[528,256]{1,0:T(8,128)(2,1)S(1)}, bf16[528,256]{1,0:T(8,128)(2,1)S(1)}, u32[]{:S(2)}, u32[]{:S(2)}) collective-permute-start(bf16[528,256]{1,0:T(8,128)(2,1)S(1)} %collective-permute-done.4), channel_id=1, source_target_pairs={{0,8},{1,57},{8,16},{9,1},{16,24},{17,9},{24,32},{25,17},{32,40},{... | collective-permute-start | bytes 811016 | tf_op jit(solution)/shard_map/ppermute | solution.py:334
  26.1 27.1 %copy-start.8 = (bf16[528,256]{1,0:T(8,128)(2,1)}, bf16[528,256]{1,0:T(8,128)(2,1)S(1)}, u32[]{:S(2)}) copy-start(bf16[528,256]{1,0:T(8,128)(2,1)S(1)} %collective-permute-done.3.refs_1_) | copy-start | bytes 811012
  26.1 6.7 %collective-permute-start.6 = (bf16[528,256]{1,0:T(8,128)(2,1)S(1)}, bf16[528,256]{1,0:T(8,128)(2,1)S(1)}, u32[]{:S(2)}, u32[]{:S(2)}) collective-permute-start(bf16[528,256]{1,0:T(8,128)(2,1)S(1)} %collective-permute-done.3.refs_1_), channel_id=1, source_target_pairs={{0,8},{1,57},{8,16},{9,1},{16,24},{17,9},{24,32},{25,17},{32,40},{... | collective-permute-start | bytes 811016 | tf_op jit(solution)/shard_map/ppermute | solution.py:334
  29.4 6.8 %copy-start.9 = (bf16[528,256]{1,0:T(8,128)(2,1)}, bf16[528,256]{1,0:T(8,128)(2,1)S(1)}, u32[]{:S(2)}) copy-start(bf16[528,256]{1,0:T(8,128)(2,1)S(1)} %collective-permute-done.5.refs_2_) | copy-start | bytes 811012
  29.4 6.8 %collective-permute-start.7 = (bf16[528,256]{1,0:T(8,128)(2,1)S(1)}, bf16[528,256]{1,0:T(8,128)(2,1)}, u32[]{:S(2)}, u32[]{:S(2)}) collective-permute-start(bf16[528,256]{1,0:T(8,128)(2,1)S(1)} %collective-permute-done.5.refs_2_), channel_id=1, source_target_pairs={{0,8},{1,57},{8,16},{9,1},{16,24},{17,9},{24,32},{25,17},{32,40},{... | collective-permute-start | bytes 811016 | tf_op jit(solution)/shard_map/ppermute | solution.py:334
  32.8 5.2 %copy-start.10 = (bf16[528,256]{1,0:T(8,128)(2,1)}, bf16[528,256]{1,0:T(8,128)(2,1)S(1)}, u32[]{:S(2)}) copy-start(bf16[528,256]{1,0:T(8,128)(2,1)S(1)} %collective-permute-done.6.refs_3_) | copy-start | bytes 811012
  32.8 9.1 %collective-permute-start.8 = (bf16[528,256]{1,0:T(8,128)(2,1)S(1)}, bf16[528,256]{1,0:T(8,128)(2,1)}, u32[]{:S(2)}, u32[]{:S(2)}) collective-permute-start(bf16[528,256]{1,0:T(8,128)(2,1)S(1)} %collective-permute-done.6.refs_3_), channel_id=1, source_target_pairs={{0,8},{1,57},{8,16},{9,1},{16,24},{17,9},{24,32},{25,17},{32,40},{... | collective-permute-start | bytes 811016 | tf_op jit(solution)/shard_map/ppermute | solution.py:334
  36.2 20.6 %copy-start.4 = (bf16[32,64,256]{2,1,0:T(8,128)(2,1)}, bf16[32,64,256]{2,1,0:T(8,128)(2,1)S(1)}, u32[]{:S(2)}) copy-start(bf16[32,64,256]{2,1,0:T(8,128)(2,1)S(1)} %collective-permute-done.12.refs_12_) | copy-start | bytes 3145732
  36.2 20.6 %copy-start.5 = (bf16[32,64,256]{2,1,0:T(8,128)(2,1)}, bf16[32,64,256]{2,1,0:T(8,128)(2,1)S(1)}, u32[]{:S(2)}) copy-start(bf16[32,64,256]{2,1,0:T(8,128)(2,1)S(1)} %collective-permute-done.11.refs_9_) | copy-start | bytes 3145732
  36.3 13.7 %collective-permute-start.14 = (bf16[16,64,256]{2,1,0:T(8,128)(2,1)S(1)}, bf16[16,64,256]{2,1,0:T(8,128)(2,1)}, u32[]{:S(2)}, u32[]{:S(2)}) collective-permute-start(bf16[16,64,256]{2,1,0:T(8,128)(2,1)S(1)} %slice.7), channel_id=1, source_target_pairs={{0,192},{64,0},{128,64},{192,128},{1,193},{65,1},{129,65},{193,129... | collective-permute-start | bytes 1572872 | tf_op jit(solution)/shard_map/ppermute | solution.py:326
  37.4 13.4 %collective-permute-start.13 = (bf16[16,64,256]{2,1,0:T(8,128)(2,1)S(1)}, bf16[16,64,256]{2,1,0:T(8,128)(2,1)}, u32[]{:S(2)}, u32[]{:S(2)}) collective-permute-start(bf16[16,64,256]{2,1,0:T(8,128)(2,1)S(1)} %slice.6), channel_id=1, source_target_pairs={{0,64},{64,128},{128,192},{192,0},{1,65},{65,129},{129,193},{193,1... | collective-permute-start | bytes 1572872 | tf_op jit(solution)/shard_map/ppermute | solution.py:326
  37.9 7.7 %collective-permute-start.9 = (bf16[528,256]{1,0:T(8,128)(2,1)}, bf16[528,256]{1,0:T(8,128)(2,1)}, u32[]{:S(2)}, u32[]{:S(2)}) collective-permute-start(bf16[528,256]{1,0:T(8,128)(2,1)} %collective-permute-done.7.refs_4_), channel_id=1, source_target_pairs={{0,8},{1,57},{8,16},{9,1},{16,24},{17,9},{24,32},{25,17},{32,40},{... | collective-permute-start | bytes 811016 | tf_op jit(solution)/shard_map/ppermute | solution.py:334
  41.9 11.3 %collective-permute-start.10 = (bf16[528,256]{1,0:T(8,128)(2,1)}, bf16[528,256]{1,0:T(8,128)(2,1)}, u32[]{:S(2)}, u32[]{:S(2)}) collective-permute-start(bf16[528,256]{1,0:T(8,128)(2,1)} %collective-permute-done.8.refs_5_), channel_id=1, source_target_pairs={{0,8},{1,57},{8,16},{9,1},{16,24},{17,9},{24,32},{25,17},{32,40},{... | collective-permute-start | bytes 811016 | tf_op jit(solution)/shard_map/ppermute | solution.py:334
  43.4 14.4 %copy-start = (s32[2]{0:T(128)S(1)}, s32[2]{0:T(128)}, u32[]{:S(2)}) copy-start(s32[2]{0:T(128)} %pad_add_fusion.me_ref) | copy-start | bytes 28
  43.4 13.5 %collective-permute-start.15 = (bf16[32,64,256]{2,1,0:T(8,128)(2,1)S(1)}, bf16[32,64,256]{2,1,0:T(8,128)(2,1)}, u32[]{:S(2)}, u32[]{:S(2)}) collective-permute-start(bf16[32,64,256]{2,1,0:T(8,128)(2,1)S(1)} %collective-permute-done.11.refs_9_), channel_id=1, source_target_pairs={{0,1},{1,0},{2,3},{3,2},{4,5},{5,4},{6,7},{7,6},{8,9},{9,8},{10,11... | collective-permute-start | bytes 3145736 | tf_op jit(solution)/shard_map/ppermute | solution.py:338
  45.6 11.3 %collective-permute-start.18 = (bf16[32,64,256]{2,1,0:T(8,128)(2,1)S(1)}, bf16[32,64,256]{2,1,0:T(8,128)(2,1)}, u32[]{:S(2)}, u32[]{:S(2)}) collective-permute-start(bf16[32,64,256]{2,1,0:T(8,128)(2,1)S(1)} %collective-permute-done.12.refs_12_), channel_id=1, source_target_pairs={{0,1},{1,0},{2,3},{3,2},{4,5},{5,4},{6,7},{7,6},{8,9},{9,8},{10,11... | collective-permute-start | bytes 3145736 | tf_op jit(solution)/shard_map/ppermute | solution.py:338
  49.9 6.9 %collective-permute-start.17 = (bf16[16,64,256]{2,1,0:T(8,128)(2,1)}, bf16[16,64,256]{2,1,0:T(8,128)(2,1)S(1)}, u32[]{:S(2)}, u32[]{:S(2)}) collective-permute-start(bf16[16,64,256]{2,1,0:T(8,128)(2,1)} %collective-permute-done.14.refs_11_), channel_id=1, source_target_pairs={{0,1},{1,0},{2,3},{3,2},{4,5},{5,4},{6,7},{7,6},{8,9},{9,8},{10,11... | collective-permute-start | bytes 1572872 | tf_op jit(solution)/shard_map/ppermute | solution.py:338
  50.8 6.1 %collective-permute-start.16 = (bf16[16,64,256]{2,1,0:T(8,128)(2,1)}, bf16[16,64,256]{2,1,0:T(8,128)(2,1)S(1)}, u32[]{:S(2)}, u32[]{:S(2)}) collective-permute-start(bf16[16,64,256]{2,1,0:T(8,128)(2,1)} %collective-permute-done.13.refs_10_), channel_id=1, source_target_pairs={{0,1},{1,0},{2,3},{3,2},{4,5},{5,4},{6,7},{7,6},{8,9},{9,8},{10,11... | collective-permute-start | bytes 1572872 | tf_op jit(solution)/shard_map/ppermute | solution.py:338
  56.8 0.8 copy-start.6
  56.9 0.9 %copy-start.7 = (bf16[16,64,256]{2,1,0:T(8,128)(2,1)}, bf16[16,64,256]{2,1,0:T(8,128)(2,1)S(1)}, u32[]{:S(2)}) copy-start(bf16[16,64,256]{2,1,0:T(8,128)(2,1)S(1)} %collective-permute-done.16.refs_14_) | copy-start | bytes 1572868
  57.8 0.7 copy-start.1
  68.2 18.4 %copy-start.3 = (f32[8,64,256]{2,1,0:T(8,128)S(1)}, f32[8,64,256]{2,1,0:T(8,128)}, u32[]{:S(2)}) copy-start(f32[8,64,256]{2,1,0:T(8,128)} %get-tuple-element.45) | copy-start | bytes 1572868
  68.2 2.9 %collective-permute-start.19 = (bf16[8,64,256]{2,1,0:T(8,128)(2,1)S(1)}, bf16[8,64,256]{2,1,0:T(8,128)(2,1)S(1)}, u32[]{:S(2)}, u32[]{:S(2)}) collective-permute-start(bf16[8,64,256]{2,1,0:T(8,128)(2,1)S(1)} %get-tuple-element.40), channel_id=1, source_target_pairs={{0,1},{1,0},{2,3},{3,2},{4,5},{5,4},{6,7},{7,6},{8,9},{9,8},{10,11... | collective-permute-start | bytes 786440 | tf_op jit(solution)/shard_map/ppermute | solution.py:338
  69.9 4.1 %collective-permute-start.21 = (bf16[8,64,256]{2,1,0:T(8,128)(2,1)S(1)}, bf16[8,64,256]{2,1,0:T(8,128)(2,1)S(1)}, u32[]{:S(2)}, u32[]{:S(2)}) collective-permute-start(bf16[8,64,256]{2,1,0:T(8,128)(2,1)S(1)} %get-tuple-element.42), channel_id=1, source_target_pairs={{0,1},{1,0},{2,3},{3,2},{4,5},{5,4},{6,7},{7,6},{8,9},{9,8},{10,11... | collective-permute-start | bytes 786440 | tf_op jit(solution)/shard_map/ppermute | solution.py:338
  70.0 4.1 %collective-permute-start.23 = (bf16[8,64,256]{2,1,0:T(8,128)(2,1)S(1)}, bf16[8,64,256]{2,1,0:T(8,128)(2,1)S(1)}, u32[]{:S(2)}, u32[]{:S(2)}) collective-permute-start(bf16[8,64,256]{2,1,0:T(8,128)(2,1)S(1)} %get-tuple-element.44), channel_id=1, source_target_pairs={{0,1},{1,0},{2,3},{3,2},{4,5},{5,4},{6,7},{7,6},{8,9},{9,8},{10,11... | collective-permute-start | bytes 786440 | tf_op jit(solution)/shard_map/ppermute | solution.py:338
  70.4 6.5 %collective-permute-start.25 = (bf16[8,64,256]{2,1,0:T(8,128)(2,1)S(1)}, bf16[8,64,256]{2,1,0:T(8,128)(2,1)S(1)}, u32[]{:S(2)}, u32[]{:S(2)}) collective-permute-start(bf16[8,64,256]{2,1,0:T(8,128)(2,1)S(1)} %get-tuple-element.46), channel_id=1, source_target_pairs={{0,1},{1,0},{2,3},{3,2},{4,5},{5,4},{6,7},{7,6},{8,9},{9,8},{10,11... | collective-permute-start | bytes 786440 | tf_op jit(solution)/shard_map/ppermute | solution.py:338
  71.1 9.2 %collective-permute-start.20 = (bf16[8,64,256]{2,1,0:T(8,128)(2,1)S(1)}, bf16[8,64,256]{2,1,0:T(8,128)(2,1)S(1)}, u32[]{:S(2)}, u32[]{:S(2)}) collective-permute-start(bf16[8,64,256]{2,1,0:T(8,128)(2,1)S(1)} %add_convert_fusion.2), channel_id=1, source_target_pairs={{0,4},{2,6},{4,0},{6,2},{1,5},{3,7},{5,1},{7,3},{8,12},{10,14},{12... | collective-permute-start | bytes 786440 | tf_op jit(solution)/shard_map/ppermute | solution.py:326
  74.0 12.5 %collective-permute-start.22 = (bf16[8,64,256]{2,1,0:T(8,128)(2,1)S(1)}, bf16[8,64,256]{2,1,0:T(8,128)(2,1)S(1)}, u32[]{:S(2)}, u32[]{:S(2)}) collective-permute-start(bf16[8,64,256]{2,1,0:T(8,128)(2,1)S(1)} %add_convert_fusion.1), channel_id=1, source_target_pairs={{0,2},{2,4},{4,6},{6,0},{1,3},{3,5},{5,7},{7,1},{8,10},{10,12},{12... | collective-permute-start | bytes 786440 | tf_op jit(solution)/shard_map/ppermute | solution.py:326
  74.2 12.4 %collective-permute-start.24 = (bf16[8,64,256]{2,1,0:T(8,128)(2,1)S(1)}, bf16[8,64,256]{2,1,0:T(8,128)(2,1)S(1)}, u32[]{:S(2)}, u32[]{:S(2)}) collective-permute-start(bf16[8,64,256]{2,1,0:T(8,128)(2,1)S(1)} %add_convert_fusion), channel_id=1, source_target_pairs={{0,6},{2,0},{4,2},{6,4},{1,7},{3,1},{5,3},{7,5},{8,14},{10,8},{12,... | collective-permute-start | bytes 786440 | tf_op jit(solution)/shard_map/ppermute | solution.py:326
